TPU v7x, 32 devices: a whole 2x2x4 slice. The times are simulated.
32 devices in a mesh: dp: 8 (over y, x, core), tensor: 4 (over z).
Axes of the slice: x: 2, y: 2, z: 4, core: 2. Of those that a mesh axis runs over, the one named last changes fastest.
Arguments:
- tokens_in: bfloat16 [16384, 1024], P(('dp', 'tensor')), may hold values from -6 to 6
- segment_ids: int32 [16, 1024], P('dp'), may hold values from 0 to 3, as said below
- qkv_weight: bfloat16 [2, 3, 1024, 1024], P(None, None, 'dp', 'tensor'), may hold values from -0.1875 to 0.1875
- qv_bias: bfloat16 [2, 2, 1024], P(None, None, ('tensor', 'dp')), may hold values from -3 to 3
- out_weight: bfloat16 [2, 1024, 1024], P(None, 'tensor', 'dp'), may hold values from -0.75 to 0.75
- up_weight: bfloat16 [2, 1024, 4096], P(None, 'dp', 'tensor'), may hold values from -0.1875 to 0.1875
- up_bias: bfloat16 [2, 4096], P(None, ('tensor', 'dp')), may hold values from -3 to 3
- down_weight: bfloat16 [2, 4096, 1024], P(None, 'tensor', 'dp'), may hold values from -0.09375 to 0.09375
- row_params: bfloat16 [2, 6, 1024], P(None, None, ('dp', 'tensor'))
- cotangent: bfloat16 [16384, 1024], P(('dp', 'tensor')), may hold values from -6 to 6
Outputs:
- output: bfloat16 [16384, 1024], P(('dp', 'tensor'))
- grad_input: float32 [16384, 1024], P(('dp', 'tensor'))
- grad_qkv_weight: float32 [2, 3, 1024, 1024], P(None, None, 'dp', 'tensor')
- grad_qv_bias: float32 [2, 2, 1024], P(None, None, ('tensor', 'dp'))
- grad_out_weight: float32 [2, 1024, 1024], P(None, 'tensor', 'dp')
- grad_up_weight: float32 [2, 1024, 4096], P(None, 'dp', 'tensor')
- grad_up_bias: float32 [2, 4096], P(None, ('tensor', 'dp'))
- grad_down_weight: float32 [2, 4096, 1024], P(None, 'tensor', 'dp')
- grad_row_params: float32 [2, 6, 1024], P(None, None, ('dp', 'tensor'))
Inputs may be any that keep to these rules, and one draw needn't show every extreme that they name: `segment_ids`: within each sequence the numbers never fall and start at 0; equal numbers mark one document.
All inputs are finite; a program needn't handle non-finite values.
Results may differ from a plain program's by a relative error of at most 0.022.
Values may be sent and summed in bfloat16 or wider, within the bound.
No kernel may reach another device: no remote copies, remote signals or barrier semaphores. Data moves between devices by JAX's collectives and lax.ppermute only.
A program may use at most 192 MiB of HBM per device.

v0:
```python
import jax
import jax.numpy as jnp
from jax import lax
from jax.sharding import PartitionSpec as P

HEADS = 16
HEAD_DIM = 64
QBLK = 512


EPSILON = 1e-05
MASKED = -1e30


def layer_norm(values, gain_row, shift_row):
    centre = jnp.mean(values, axis=-1, keepdims=True)
    centred = values - centre
    spread = jnp.mean(centred * centred, axis=-1, keepdims=True)
    return centred * lax.rsqrt(spread + EPSILON) * gain_row + shift_row


def norm_back(values, gain_row, shift_row, upstream):
    result, pullback = jax.vjp(layer_norm, values, gain_row, shift_row)
    return pullback(upstream)


def gelu_tanh(values):
    return jax.nn.gelu(values, approximate=True)


def block_scores(query_block, key_rows, first_row, segment, slope_row, score_scale):
    block_rows = query_block.shape[0]
    length = key_rows.shape[0]
    query_place = first_row + jnp.arange(block_rows, dtype=jnp.int32)
    key_place = jnp.arange(length, dtype=jnp.int32)
    query_segment = lax.dynamic_slice_in_dim(segment, first_row, block_rows)
    allowed = (query_place[:, None] >= key_place[None, :]) & (
        query_segment[:, None] == segment[None, :]
    )
    distance = (query_place[:, None] - key_place[None, :]).astype(jnp.float32)
    scores = (
        jnp.einsum("qhd,khd->hqk", query_block, key_rows, preferred_element_type=jnp.float32)
        * score_scale
    )
    scores = scores - slope_row[:, None, None] * distance[None]
    return jnp.where(allowed[None], scores, MASKED)


def attend_forward(queries, key_rows, value_rows, segment, slope_row, score_scale, block_rows):
    length = queries.shape[0]

    def one_block(block_at):
        first_row = block_at * block_rows
        query_block = lax.dynamic_slice_in_dim(queries, first_row, block_rows)
        scores = block_scores(query_block, key_rows, first_row, segment, slope_row, score_scale)
        row_max = jnp.max(scores, axis=-1, keepdims=True)
        lifted = jnp.exp(scores - row_max)
        row_total = jnp.sum(lifted, axis=-1, keepdims=True)
        weights = (lifted / row_total).astype(jnp.bfloat16)
        mixed = jnp.einsum("hqk,khd->qhd", weights, value_rows, preferred_element_type=jnp.float32)
        return (mixed.astype(jnp.bfloat16), (row_max + jnp.log(row_total))[..., 0])

    mixed, log_total = lax.map(one_block, jnp.arange(length // block_rows, dtype=jnp.int32))
    return (mixed.reshape(queries.shape), log_total)


def attend_backward(
    queries, key_rows, value_rows, segment, log_total, upstream, slope_row, score_scale, block_rows
):
    length = queries.shape[0]

    def one_block(running, block_at):
        key_grad, value_grad = running
        first_row = block_at * block_rows
        query_block = lax.dynamic_slice_in_dim(queries, first_row, block_rows)
        upstream_block = lax.dynamic_slice_in_dim(upstream, first_row, block_rows)
        scores = block_scores(query_block, key_rows, first_row, segment, slope_row, score_scale)
        chances = jnp.exp(scores - log_total[block_at][..., None])
        weights = chances.astype(jnp.bfloat16)
        value_grad = value_grad + jnp.einsum(
            "hqk,qhd->khd", weights, upstream_block, preferred_element_type=jnp.float32
        )
        chance_grad = jnp.einsum(
            "qhd,khd->hqk", upstream_block, value_rows, preferred_element_type=jnp.float32
        )
        row_inner = jnp.sum(chance_grad * chances, axis=-1, keepdims=True)
        score_grad = (chances * (chance_grad - row_inner)).astype(jnp.bfloat16)
        query_grad = (
            jnp.einsum("hqk,khd->qhd", score_grad, key_rows, preferred_element_type=jnp.float32)
            * score_scale
        )
        key_grad = (
            key_grad
            + jnp.einsum(
                "hqk,qhd->khd", score_grad, query_block, preferred_element_type=jnp.float32
            )
            * score_scale
        )
        return ((key_grad, value_grad), query_grad)

    zero_grad = jnp.zeros(key_rows.shape, jnp.float32)
    (key_grad, value_grad), query_grad = lax.scan(
        one_block, (zero_grad, zero_grad), jnp.arange(length // block_rows, dtype=jnp.int32)
    )
    return (query_grad.reshape(queries.shape), key_grad, value_grad)


def split_heads(matrix, sequences, heads_here):
    return matrix.reshape(sequences, -1, heads_here, matrix.shape[1] // heads_here)


def attention_forward(
    queries, key_rows, value_rows, segment_ids, slope_row, score_scale, block_rows
):
    sequences = segment_ids.shape[0]
    heads_here = slope_row.shape[0]

    def one_sequence(inputs):
        return attend_forward(
            inputs[0], inputs[1], inputs[2], inputs[3], slope_row, score_scale, block_rows
        )

    mixed, log_total = lax.map(
        one_sequence,
        (
            split_heads(queries, sequences, heads_here),
            split_heads(key_rows, sequences, heads_here),
            split_heads(value_rows, sequences, heads_here),
            segment_ids,
        ),
    )
    return (mixed.reshape(queries.shape), log_total)


def attention_backward(
    queries,
    key_rows,
    value_rows,
    segment_ids,
    log_total,
    upstream,
    slope_row,
    score_scale,
    block_rows,
):
    sequences = segment_ids.shape[0]
    heads_here = slope_row.shape[0]

    def one_sequence(inputs):
        return attend_backward(
            inputs[0],
            inputs[1],
            inputs[2],
            inputs[3],
            inputs[4],
            inputs[5],
            slope_row,
            score_scale,
            block_rows,
        )

    query_grad, key_grad, value_grad = lax.map(
        one_sequence,
        (
            split_heads(queries, sequences, heads_here),
            split_heads(key_rows, sequences, heads_here),
            split_heads(value_rows, sequences, heads_here),
            segment_ids,
            log_total,
            split_heads(upstream, sequences, heads_here),
        ),
    )
    return (
        query_grad.reshape(queries.shape),
        key_grad.reshape(queries.shape),
        value_grad.reshape(queries.shape),
    )


def fetch_layer(number, qkv_weight, out_weight, up_weight, down_weight, qv_bias, up_bias):
    return (
        lax.all_gather(qkv_weight[number], "dp", axis=1, tiled=True),
        lax.all_gather(out_weight[number], "dp", axis=1, tiled=True),
        lax.all_gather(up_weight[number], "dp", axis=0, tiled=True),
        lax.all_gather(down_weight[number], "dp", axis=1, tiled=True),
        lax.all_gather(qv_bias[number], "dp", axis=1, tiled=True),
        lax.all_gather(up_bias[number], "dp", axis=0, tiled=True),
    )


def fetch_again(number, qkv_weight, out_weight, up_weight, down_weight, qv_bias, up_bias):
    return (
        lax.all_gather(qkv_weight[number], "dp", axis=1, tiled=True),
        lax.all_gather(out_weight[number], "dp", axis=1, tiled=True),
        lax.all_gather(up_weight[number], "dp", axis=0, tiled=True),
        lax.all_gather(down_weight[number], "dp", axis=1, tiled=True),
        lax.all_gather(qv_bias[number], "dp", axis=1, tiled=True),
        lax.all_gather(up_bias[number], "dp", axis=0, tiled=True),
    )


def spread_rows(values):
    return lax.all_gather(values, "tensor", axis=0, tiled=True)


def spread_grads(values):
    return lax.all_gather(values, "tensor", axis=0, tiled=True)


def reduce_forward(row_term, shard_rows):
    return lax.psum_scatter(
        row_term(jnp.int32(0), shard_rows * lax.axis_size("tensor")).astype(jnp.bfloat16),
        "tensor",
        scatter_dimension=0,
        tiled=True,
    ).astype(jnp.float32)


def reduce_backward(row_term, shard_rows):
    return lax.psum_scatter(
        row_term(jnp.int32(0), shard_rows * lax.axis_size("tensor")).astype(jnp.bfloat16),
        "tensor",
        scatter_dimension=0,
        tiled=True,
    ).astype(jnp.float32)


def rows_product(left_rows, right_matrix, pattern):

    def row_term(first_row, row_count):
        return jnp.einsum(pattern, left_rows, right_matrix, preferred_element_type=jnp.float32)

    return row_term


def body(
    tokens_in,
    segment_ids,
    qkv_weight,
    qv_bias,
    out_weight,
    up_weight,
    up_bias,
    down_weight,
    row_params,
    cotangent,
):
    layers = qkv_weight.shape[0]
    shard_rows = tokens_in.shape[0]
    heads_here = HEADS // lax.axis_size("tensor")
    head_number = lax.axis_index("tensor") * heads_here + jnp.arange(heads_here, dtype=jnp.int32)
    slope_row = 2.0 ** (-8.0 * (head_number.astype(jnp.float32) + 1.0) / HEADS)
    score_scale = HEAD_DIM ** (-0.5)
    everything = lax.all_gather(row_params, ("dp", "tensor"), axis=2, tiled=True).astype(
        jnp.float32
    )
    stream = tokens_in.astype(jnp.float32)
    stash = []
    fetched = []
    for number in range(layers):
        weights = fetch_layer(
            number, qkv_weight, out_weight, up_weight, down_weight, qv_bias, up_bias
        )
        fetched.append(weights)
        qkv_full, out_full, up_full, down_full, qv_full, up_bias_full = weights
        normed = layer_norm(stream, everything[number, 0], everything[number, 1]).astype(
            jnp.bfloat16
        )
        normed_all = spread_rows(normed)
        projected = jnp.einsum(
            "gd,cde->gce", normed_all, qkv_full, preferred_element_type=jnp.float32
        )
        qv_float = qv_full.astype(jnp.float32)
        queries = (projected[:, 0] + qv_float[0]).astype(jnp.bfloat16)
        key_rows = projected[:, 1].astype(jnp.bfloat16)
        value_rows = (projected[:, 2] + qv_float[1]).astype(jnp.bfloat16)
        attended, log_total = attention_forward(
            queries, key_rows, value_rows, segment_ids, slope_row, score_scale, QBLK
        )
        middle = stream + (
            reduce_forward(rows_product(attended, out_full, "ge,ed->gd"), shard_rows)
            + everything[number, 2]
        )
        normed_two = layer_norm(middle, everything[number, 3], everything[number, 4]).astype(
            jnp.bfloat16
        )
        ffn_inputs = spread_rows(normed_two)
        pre_gelu = jnp.dot(
            ffn_inputs, up_full, preferred_element_type=jnp.float32
        ) + up_bias_full.astype(jnp.float32)
        hidden = gelu_tanh(pre_gelu).astype(jnp.bfloat16)
        ffn_out = reduce_forward(rows_product(hidden, down_full, "gf,fd->gd"), shard_rows)
        ffn_mats = (up_full, down_full)
        stash.append(
            (
                stream,
                normed_all,
                queries,
                key_rows,
                value_rows,
                attended,
                log_total,
                middle,
                ffn_inputs,
                pre_gelu,
                hidden,
                ffn_mats,
            )
        )
        stream = middle + (ffn_out + everything[number, 5])
    output = stream.astype(jnp.bfloat16)
    upstream = cotangent.astype(jnp.float32)
    row_grads = [None] * layers
    layer_grads = [None] * layers
    for number in reversed(range(layers)):
        (
            stream_in,
            normed_all,
            queries,
            key_rows,
            value_rows,
            attended,
            log_total,
            middle,
            ffn_inputs,
            pre_gelu,
            hidden,
            ffn_mats,
        ) = stash[number]
        weights = fetch_again(
            number, qkv_weight, out_weight, up_weight, down_weight, qv_bias, up_bias
        )
        qkv_full, out_full, up_full, down_full, qv_full, up_bias_full = weights
        down_bias_grad = jnp.sum(upstream, axis=0)
        down_in = spread_grads(upstream.astype(jnp.bfloat16))
        down_grad = jnp.einsum("gf,gd->fd", hidden, down_in, preferred_element_type=jnp.float32)
        hidden_grad = jnp.einsum(
            "gd,fd->gf", down_in, down_full, preferred_element_type=jnp.float32
        )
        pre_grad = jax.vjp(gelu_tanh, pre_gelu)[1](hidden_grad)[0]
        up_bias_grad = jnp.sum(pre_grad, axis=0)
        pre_low = pre_grad.astype(jnp.bfloat16)
        up_grad = jnp.einsum("gd,gf->df", ffn_inputs, pre_low, preferred_element_type=jnp.float32)
        normed_two_grad = reduce_backward(rows_product(pre_low, up_full, "gf,df->gd"), shard_rows)
        middle_grad, gain_two_grad, shift_two_grad = norm_back(
            middle, everything[number, 3], everything[number, 4], normed_two_grad
        )
        middle_grad = middle_grad + upstream
        out_bias_grad = jnp.sum(middle_grad, axis=0)
        out_in = spread_grads(middle_grad.astype(jnp.bfloat16))
        out_grad = jnp.einsum("ge,gd->ed", attended, out_in, preferred_element_type=jnp.float32)
        attended_grad = jnp.einsum(
            "gd,ed->ge", out_in, out_full, preferred_element_type=jnp.float32
        ).astype(jnp.bfloat16)
        query_grad, key_grad, value_grad = attention_backward(
            queries,
            key_rows,
            value_rows,
            segment_ids,
            log_total,
            attended_grad,
            slope_row,
            score_scale,
            QBLK,
        )
        qv_grad = jnp.stack([jnp.sum(query_grad, axis=0), jnp.sum(value_grad, axis=0)])
        qkv_low = jnp.stack([query_grad, key_grad, value_grad], axis=1).astype(jnp.bfloat16)
        qkv_grad = jnp.einsum(
            "gd,gce->cde", normed_all, qkv_low, preferred_element_type=jnp.float32
        )
        normed_grad = reduce_backward(rows_product(qkv_low, qkv_full, "gce,cde->gd"), shard_rows)
        stream_grad, gain_one_grad, shift_one_grad = norm_back(
            stream_in, everything[number, 0], everything[number, 1], normed_grad
        )
        upstream = middle_grad + stream_grad
        row_grads[number] = jnp.stack(
            [
                gain_one_grad,
                shift_one_grad,
                out_bias_grad,
                gain_two_grad,
                shift_two_grad,
                down_bias_grad,
            ]
        )
        layer_grads[number] = (
            lax.psum_scatter(
                qkv_grad.astype(jnp.bfloat16), "dp", scatter_dimension=1, tiled=True
            ).astype(jnp.float32),
            lax.psum_scatter(
                out_grad.astype(jnp.bfloat16), "dp", scatter_dimension=1, tiled=True
            ).astype(jnp.float32),
            lax.psum_scatter(
                up_grad.astype(jnp.bfloat16), "dp", scatter_dimension=0, tiled=True
            ).astype(jnp.float32),
            lax.psum_scatter(
                down_grad.astype(jnp.bfloat16), "dp", scatter_dimension=1, tiled=True
            ).astype(jnp.float32),
            lax.psum_scatter(
                qv_grad.astype(jnp.bfloat16), "dp", scatter_dimension=1, tiled=True
            ).astype(jnp.float32),
            lax.psum_scatter(
                up_bias_grad.astype(jnp.bfloat16), "dp", scatter_dimension=0, tiled=True
            ).astype(jnp.float32),
        )
    joined = [
        jnp.stack([layer_grads[number][member] for number in range(layers)]) for member in range(6)
    ]
    row_summed = lax.psum_scatter(
        jnp.stack(row_grads), ("dp", "tensor"), scatter_dimension=2, tiled=True
    )
    return (
        output,
        upstream,
        joined[0],
        joined[4],
        joined[1],
        joined[2],
        joined[5],
        joined[3],
        row_summed,
    )


def solution(mesh):
    placed = (
        P(("dp", "tensor"), None),
        P("dp", None),
        P(None, None, "dp", "tensor"),
        P(None, None, ("tensor", "dp")),
        P(None, "tensor", "dp"),
        P(None, "dp", "tensor"),
        P(None, ("tensor", "dp")),
        P(None, "tensor", "dp"),
        P(None, None, ("dp", "tensor")),
        P(("dp", "tensor"), None),
    )
    return jax.shard_map(
        body,
        mesh=mesh,
        in_specs=placed,
        out_specs=(
            P(("dp", "tensor"), None),
            P(("dp", "tensor"), None),
            P(None, None, "dp", "tensor"),
            P(None, None, ("tensor", "dp")),
            P(None, "tensor", "dp"),
            P(None, "dp", "tensor"),
            P(None, ("tensor", "dp")),
            P(None, "tensor", "dp"),
            P(None, None, ("dp", "tensor")),
        ),
        check_vma=False,
    )
```

profile of v0, /device:TPU:9, one launch (start us, length us, event | category | flops | bytes accessed | tf_op | source)
XLA Modules:
  0.0 2488.4 jit_solution(6884526169489728170)
XLA Ops:
  10.0 62.6 %all_gather.71 = bf16[2,6,1024]{1,0,2:T(2,128)(2,1)S(1)} all-gather(bf16[2,6,32]{1,0,2:T(2,128)(2,1)S(1)} %copy.147), channel_id=1, replica_groups=mesh['dp'=8,'tensor'=4] {'dp','tensor'}, dimensions={2}, use_global_device_ids=true | all-gather | bytes 25344 | tf_op jit(solution)/shard_map/all_gather | solution.py:254
  74.2 44.6 %slice_reduce_fusion = (f32[1024]{0:T(1024)}, f32[1024]{0:T(1024)}, f32[1024]{0:T(1024)}, f32[1024]{0:T(1024)}, f32[1024]{0:T(1024)}, /*index=5*/f32[1024]{0:T(1...) fusion(f32[2,6,1024]{1,0,2:T(2,128)S(1)} %convert_element_type.252), kind=kLoop, calls=%fused_computation.263 | loop fusion | bytes 98304 | tf_op jit(solution)/shard_map/slice | solution.py:310
  121.5 15.8 all-gather.1
  152.2 53.3 %all-gather.27.cloned.1.call-done = bf16[2048,1024]{1,0:T(8,128)(2,1)} async-done(((bf16[512,1024]{1,0:T(8,128)(2,1)}), bf16[2048,1024]{1,0:T(8,128)(2,1)}) %all-gather.27.cloned.1.call-update) | async-done | bytes 4194320 | tf_op jit(solution)/shard_map/all_gather | solution.py:203
  232.9 54.3 %while.115 = (s32[]{:T(128)}, bf16[2,1024,4,64]{3,2,1,0:T(4,128)(2,1)}, f32[2,2,4,512]{3,2,1,0:T(4,128)S(1)}, bf16[2,1024,4,64]{1,3,2,0:T(8,128)(2,1)}, s32[2,10...) while((s32[]{:T(128)}, ...), condition=%wide.region_7.8_spmd.clone, body=%wide.region_2.7_spmd.clone.sunk | while | flops 577370624 | bytes 43116048 | solution.py:123
  235.8 22.4 while.122
  262.8 22.4 while.122
  297.0 76.1 %reduce-scatter.38.cloned.1.call-done = bf16[512,1024]{1,0:T(8,128)(2,1)} async-done(((bf16[2048,1024]{1,0:T(8,128)(2,1)}), bf16[512,1024]{1,0:T(8,128)(2,1)}) %reduce-scatter.38.cloned.1.call-update) | async-done | bytes 1048592 | tf_op jit(solution)/shard_map/reduce_scatter | solution.py:211
  389.2 15.2 all-gather.45.cloned.1.call-done
  404.4 79.9 %all-gather.29.cloned.1.call-done = bf16[2048,1024]{1,0:T(8,128)(2,1)} async-done(((bf16[512,1024]{1,0:T(8,128)(2,1)}), bf16[2048,1024]{1,0:T(8,128)(2,1)}) %all-gather.29.cloned.1.call-update) | async-done | bytes 4194320 | tf_op jit(solution)/shard_map/all_gather | solution.py:203
  495.0 21.5 all-gather.47.cloned.1.call-done
  516.5 11.8 convolution_convert_fusion.5
  529.1 75.8 %reduce-scatter.40.cloned.1.call-done = bf16[512,1024]{1,0:T(8,128)(2,1)} async-done(((bf16[2048,1024]{1,0:T(8,128)(2,1)}), bf16[512,1024]{1,0:T(8,128)(2,1)}) %reduce-scatter.40.cloned.1.call-update) | async-done | bytes 1048592 | tf_op jit(solution)/shard_map/reduce_scatter | solution.py:211
  623.4 12.2 all-gather.8
  635.6 79.7 %all-gather.31.cloned.1.call-done = bf16[2048,1024]{1,0:T(8,128)(2,1)} async-done(((bf16[512,1024]{1,0:T(8,128)(2,1)}), bf16[2048,1024]{1,0:T(8,128)(2,1)}) %all-gather.31.cloned.1.call-update) | async-done | bytes 4194320 | tf_op jit(solution)/shard_map/all_gather | solution.py:203
  742.9 54.4 %while.117 = (s32[]{:T(128)}, bf16[2,1024,4,64]{3,2,1,0:T(4,128)(2,1)}, f32[2,2,4,512]{3,2,1,0:T(4,128)S(1)}, bf16[2,1024,4,64]{1,3,2,0:T(8,128)(2,1)}, s32[2,10...) while((s32[]{:T(128)}, ...), condition=%wide.region_19.20_spmd.clone, body=%wide.region_14.19_spmd.clone.sunk | while | flops 577370624 | bytes 43116048 | solution.py:123
  745.8 22.4 while.123
  772.7 22.4 while.123
  805.9 77.2 %reduce-scatter.42.cloned.1.call-done = bf16[512,1024]{1,0:T(8,128)(2,1)} async-done(((bf16[2048,1024]{1,0:T(8,128)(2,1)}), bf16[512,1024]{1,0:T(8,128)(2,1)}) %reduce-scatter.42.cloned.1.call-update) | async-done | bytes 1048592 | tf_op jit(solution)/shard_map/reduce_scatter | solution.py:211
  898.2 16.4 all-gather.51.cloned.1.call-done
  914.6 79.9 %all-gather.33.cloned.1.call-done = bf16[2048,1024]{1,0:T(8,128)(2,1)} async-done(((bf16[512,1024]{1,0:T(8,128)(2,1)}), bf16[2048,1024]{1,0:T(8,128)(2,1)}) %all-gather.33.cloned.1.call-update) | async-done | bytes 4194320 | tf_op jit(solution)/shard_map/all_gather | solution.py:203
  1005.1 21.1 all-gather.53.cloned.1.call-done
  1026.2 79.4 %all-gather.35.cloned.1.call-done = bf16[2048,1024]{1,0:T(8,128)(2,1)} async-done(((bf16[512,1024]{1,0:T(8,128)(2,1)}), bf16[2048,1024]{1,0:T(8,128)(2,1)}) %all-gather.35.cloned.1.call-update) | async-done | bytes 4194320 | tf_op jit(solution)/shard_map/all_gather | solution.py:207
  1105.6 14.3 fusion.196
  1129.8 11.2 convolution_convert_fusion.4
  1141.1 65.2 %reduce-scatter.46.cloned.1.call-done = bf16[512,1024]{1,0:T(8,128)(2,1)} async-done(((bf16[2048,1024]{1,0:T(8,128)(2,1)}), bf16[512,1024]{1,0:T(8,128)(2,1)}) %reduce-scatter.46.cloned.1.call-update) | async-done | bytes 1048592 | tf_op jit(solution)/shard_map/reduce_scatter | solution.py:220
  1209.0 76.7 %reduce-scatter.44.cloned.1.call-done = bf16[512,1024]{1,0:T(8,128)(2,1)} async-done(((bf16[2048,1024]{1,0:T(8,128)(2,1)}), bf16[512,1024]{1,0:T(8,128)(2,1)}) %reduce-scatter.44.cloned.1.call-update) | async-done | bytes 1048592 | tf_op jit(solution)/shard_map/reduce_scatter | solution.py:211
  1293.7 76.7 %all-gather.37.cloned.1.call-done = bf16[2048,1024]{1,0:T(8,128)(2,1)} async-done(((bf16[512,1024]{1,0:T(8,128)(2,1)}), bf16[2048,1024]{1,0:T(8,128)(2,1)}) %all-gather.37.cloned.1.call-update) | async-done | bytes 4194320 | tf_op jit(solution)/shard_map/all_gather | solution.py:207
  1381.7 89.3 %while.119 = (s32[]{:T(128)}, f32[2,1024,4,64]{3,2,1,0:T(4,128)}, bf16[2,1024,4,64]{1,3,2,0:T(8,128)(2,1)}, f32[2,1024,4,64]{1,3,2,0:T(8,128)}, bf16[2,1024,4,64...) while((s32[]{:T(128)}, f32[2,1024,4,64]{3,2,1,0:T(4,128)}, ...), condition=%wide.region_31.32_spmd.clone, body=%wide.region_27.31_spmd.clone.sunk | while | flops 1369307648 | bytes 128025488 | solution.py:162
  1387.6 30.7 %while.124 = (s32[]{:T(128)}, f32[1024,4,64]{0,2,1:T(8,128)S(1)}, f32[1024,4,64]{0,2,1:T(8,128)S(1)}, f32[2,512,4,64]{1,3,2,0:T(8,128)}, s32[2]{0:T(128)S(1)}, /...) while((s32[]{:T(128)}, f32[1024,4,64]{0,2,1:T(8,128)S(1)}, ...), condition=%wide.region_30.30_spmd.clone, body=%wide.region_28.29_spmd.clone.sunk | while | flops 1369307648 | bytes 88138152 | solution.py:102
  1432.3 30.7 %while.124 = (s32[]{:T(128)}, f32[1024,4,64]{0,2,1:T(8,128)S(1)}, f32[1024,4,64]{0,2,1:T(8,128)S(1)}, f32[2,512,4,64]{1,3,2,0:T(8,128)}, s32[2]{0:T(128)S(1)}, /...) while((s32[]{:T(128)}, f32[1024,4,64]{0,2,1:T(8,128)S(1)}, ...), condition=%wide.region_30.30_spmd.clone, body=%wide.region_28.29_spmd.clone.sunk | while | flops 1369307648 | bytes 88138152 | solution.py:102
  1500.7 78.0 %reduce-scatter.48.cloned.1.call-done = bf16[512,1024]{1,0:T(8,128)(2,1)} async-done(((bf16[2048,1024]{1,0:T(8,128)(2,1)}), bf16[512,1024]{1,0:T(8,128)(2,1)}) %reduce-scatter.48.cloned.1.call-update) | async-done | bytes 1048592 | tf_op jit(solution)/shard_map/reduce_scatter | solution.py:220
  1587.5 78.8 %all-gather.39.cloned.1.call-done = bf16[2048,1024]{1,0:T(8,128)(2,1)} async-done(((bf16[512,1024]{1,0:T(8,128)(2,1)}), bf16[2048,1024]{1,0:T(8,128)(2,1)}) %all-gather.39.cloned.1.call-update) | async-done | bytes 4194320 | tf_op jit(solution)/shard_map/all_gather | solution.py:207
  1666.3 14.4 fusion.197
  1689.1 78.0 %reduce-scatter.50.cloned.1.call-done = bf16[512,1024]{1,0:T(8,128)(2,1)} async-done(((bf16[2048,1024]{1,0:T(8,128)(2,1)}), bf16[512,1024]{1,0:T(8,128)(2,1)}) %reduce-scatter.50.cloned.1.call-update) | async-done | bytes 1048592 | tf_op jit(solution)/shard_map/reduce_scatter | solution.py:220
  1840.6 14.3 all-gather.41.cloned.1.call-done
  1865.7 89.4 %while.121 = (s32[]{:T(128)}, f32[2,1024,4,64]{3,2,1,0:T(4,128)}, bf16[2,1024,4,64]{1,3,2,0:T(8,128)(2,1)}, f32[2,1024,4,64]{1,3,2,0:T(8,128)}, bf16[2,1024,4,64...) while((s32[]{:T(128)}, f32[2,1024,4,64]{3,2,1,0:T(4,128)}, ...), condition=%wide.region_42.43_spmd.clone, body=%wide.region_38.42_spmd.clone.sunk | while | flops 1369307648 | bytes 128025488 | solution.py:162
  1871.8 30.4 %while.125 = (s32[]{:T(128)}, f32[1024,4,64]{0,2,1:T(8,128)S(1)}, f32[1024,4,64]{0,2,1:T(8,128)S(1)}, f32[2,512,4,64]{1,3,2,0:T(8,128)}, s32[2]{0:T(128)S(1)}, /...) while((s32[]{:T(128)}, f32[1024,4,64]{0,2,1:T(8,128)S(1)}, ...), condition=%wide.region_41.41_spmd.clone, body=%wide.region_39.40_spmd.clone.sunk | while | flops 1369307648 | bytes 88138152 | solution.py:102
  1916.2 30.4 %while.125 = (s32[]{:T(128)}, f32[1024,4,64]{0,2,1:T(8,128)S(1)}, f32[1024,4,64]{0,2,1:T(8,128)S(1)}, f32[2,512,4,64]{1,3,2,0:T(8,128)}, s32[2]{0:T(128)S(1)}, /...) while((s32[]{:T(128)}, f32[1024,4,64]{0,2,1:T(8,128)S(1)}, ...), condition=%wide.region_41.41_spmd.clone, body=%wide.region_39.40_spmd.clone.sunk | while | flops 1369307648 | bytes 88138152 | solution.py:102
  2018.7 11.9 all-reduce.2
  2031.3 30.5 %reduce-scatter.70.cloned.1.call-done = bf16[128,1024]{1,0:T(8,128)(2,1)} async-done(((bf16[1024,1024]{1,0:T(8,128)(2,1)}), bf16[128,1024]{1,0:T(8,128)(2,1)}) %reduce-scatter.70.cloned.1.call-update) | async-done | bytes 262160
  2062.9 43.6 %reduce-scatter.56.cloned.1.call-done = bf16[128,1024]{1,0:T(8,128)(2,1)} async-done(((bf16[1024,1024]{1,0:T(8,128)(2,1)}), bf16[128,1024]{1,0:T(8,128)(2,1)}) %reduce-scatter.56.cloned.1.call-update) | async-done | bytes 262160 | tf_op jit(solution)/shard_map/reduce_scatter | solution.py:393
  2106.5 44.5 %reduce-scatter.54.cloned.1.call-done = bf16[128,1024]{1,0:T(8,128)(2,1)} async-done(((bf16[1024,1024]{1,0:T(8,128)(2,1)}), bf16[128,1024]{1,0:T(8,128)(2,1)}) %reduce-scatter.54.cloned.1.call-update) | async-done | bytes 262160 | tf_op jit(solution)/shard_map/reduce_scatter | solution.py:393
  2154.1 32.9 %reduce-scatter.62.cloned.1.call-done = bf16[32,2]{1,0:T(8,128)(2,1)} async-done(((bf16[256,2]{1,0:T(8,128)(2,1)}), bf16[32,2]{1,0:T(8,128)(2,1)}) %reduce-scatter.62.cloned.1.call-update) | async-done | bytes 144
  2188.4 35.7 %reduce-scatter.66.cloned.1.call-done = bf16[128,256]{1,0:T(8,128)(2,1)} async-done(((bf16[1024,256]{1,0:T(8,128)(2,1)}), bf16[128,256]{1,0:T(8,128)(2,1)}) %reduce-scatter.66.cloned.1.call-update) | async-done | bytes 65552
  2225.8 40.9 %reduce-scatter.58.cloned.1.call-done = bf16[128,768]{1,0:T(8,128)(2,1)} async-done(((bf16[1024,768]{1,0:T(8,128)(2,1)}), bf16[128,768]{1,0:T(8,128)(2,1)}) %reduce-scatter.58.cloned.1.call-update) | async-done | bytes 196624
  2269.3 76.8 %reduce-scatter.52.cloned.1.call-done = bf16[512,1024]{1,0:T(8,128)(2,1)} async-done(((bf16[2048,1024]{1,0:T(8,128)(2,1)}), bf16[512,1024]{1,0:T(8,128)(2,1)}) %reduce-scatter.52.cloned.1.call-update) | async-done | bytes 1048592 | tf_op jit(solution)/shard_map/reduce_scatter | solution.py:220
  2357.9 122.0 %reduce-scatter.74.cloned.1.call-done = f32[32,12]{1,0:T(8,128)} async-done(((f32[1024,12]{1,0:T(8,128)}), f32[32,12]{1,0:T(8,128)}) %reduce-scatter.74.cloned.1.call-update) | async-done | bytes 1552
  (832 shorter events, 674.9 us)
Async XLA Ops:
  7.2 145.0 %all-gather.43.cloned.1.call-start = ((), (), s32[]{:S(2)}) async-start(), calls=%async_computation.37 | async-start | bytes 1769472 | tf_op jit(solution)/shard_map/all_gather | solution.py:182
  9.1 196.4 %all-gather.27.cloned.1.call-start = ((), (), s32[]{:S(2)}) async-start(), calls=%async_computation.19 | async-start | bytes 5242880 | tf_op jit(solution)/shard_map/all_gather | solution.py:203
  120.8 252.3 %reduce-scatter.38.cloned.1.call-start = ((), (), s32[]{:S(2)}) async-start(), calls=%async_computation.20 | async-start | bytes 5242880 | tf_op jit(solution)/shard_map/reduce_scatter | solution.py:211
  295.1 109.3 %all-gather.45.cloned.1.call-start = ((), (), s32[]{:S(2)}) async-start(), calls=%async_computation.38 | async-start | bytes 2359296 | tf_op jit(solution)/shard_map/all_gather | solution.py:184
  297.0 187.4 %all-gather.29.cloned.1.call-start = ((), (), s32[]{:S(2)}) async-start(), calls=%async_computation.21 | async-start | bytes 5242880 | tf_op jit(solution)/shard_map/all_gather | solution.py:203
  376.7 118.3 %copy-start.83 = (f32[512]{0:T(512)}, f32[512]{0:T(512)S(1)}, u32[]{:S(2)}) copy-start(f32[512]{0:T(512)S(1)} %multiply_reduce_fusion.4) | copy-start | bytes 6148
  376.8 118.3 %copy-start.75 = (f32[512]{0:T(512)}, f32[512]{0:T(512)S(1)}, u32[]{:S(2)}) copy-start(f32[512]{0:T(512)S(1)} %fusion.171) | copy-start | bytes 6148
  378.4 138.1 %all-gather.47.cloned.1.call-start = ((), (), s32[]{:S(2)}) async-start(), calls=%async_computation.39 | async-start | bytes 2359296 | tf_op jit(solution)/shard_map/all_gather | solution.py:185
  379.3 225.6 %reduce-scatter.40.cloned.1.call-start = ((), (), s32[]{:S(2)}) async-start(), calls=%async_computation.22 | async-start | bytes 5242880 | tf_op jit(solution)/shard_map/reduce_scatter | solution.py:211
  389.2 127.3 %copy-start.105 = (f32[1,1024]{1,0:T(1,128)}, f32[1,1024]{1,0:T(1,128)S(1)}, u32[]{:S(2)}) copy-start(f32[1,1024]{1,0:T(1,128)S(1)} %convert_element_type.308) | copy-start | bytes 12292
  528.3 107.3 %all-gather.49.cloned.1.call-start = ((), (), s32[]{:S(2)}) async-start(), calls=%async_computation.40 | async-start | bytes 1769472 | tf_op jit(solution)/shard_map/all_gather | solution.py:182
  529.1 186.3 %all-gather.31.cloned.1.call-start = ((), (), s32[]{:S(2)}) async-start(), calls=%async_computation.23 | async-start | bytes 5242880 | tf_op jit(solution)/shard_map/all_gather | solution.py:203
  607.1 108.2 %copy-start.85 = (f32[512]{0:T(512)}, f32[512]{0:T(512)S(1)}, u32[]{:S(2)}) copy-start(f32[512]{0:T(512)S(1)} %multiply_reduce_fusion.3) | copy-start | bytes 6148
  607.1 108.2 %copy-start.79 = (f32[512]{0:T(512)}, f32[512]{0:T(512)S(1)}, u32[]{:S(2)}) copy-start(f32[512]{0:T(512)S(1)} %fusion.172) | copy-start | bytes 6148
  609.5 273.6 %reduce-scatter.42.cloned.1.call-start = ((), (), s32[]{:S(2)}) async-start(), calls=%async_computation.24 | async-start | bytes 5242880 | tf_op jit(solution)/shard_map/reduce_scatter | solution.py:211
  805.1 109.5 %all-gather.51.cloned.1.call-start = ((), (), s32[]{:S(2)}) async-start(), calls=%async_computation.41 | async-start | bytes 2359296 | tf_op jit(solution)/shard_map/all_gather | solution.py:184
  805.8 188.6 %all-gather.33.cloned.1.call-start = ((), (), s32[]{:S(2)}) async-start(), calls=%async_computation.25 | async-start | bytes 5242880 | tf_op jit(solution)/shard_map/all_gather | solution.py:203
  887.4 138.8 %all-gather.53.cloned.1.call-start = ((), (), s32[]{:S(2)}) async-start(), calls=%async_computation.42 | async-start | bytes 2359296 | tf_op jit(solution)/shard_map/all_gather | solution.py:185
  888.2 217.4 %all-gather.35.cloned.1.call-start = ((), (), s32[]{:S(2)}) async-start(), calls=%async_computation.27 | async-start | bytes 5242880 | tf_op jit(solution)/shard_map/all_gather | solution.py:207
  888.8 317.5 %reduce-scatter.46.cloned.1.call-start = ((), (), s32[]{:S(2)}) async-start(), calls=%async_computation.28 | async-start | bytes 5242880 | tf_op jit(solution)/shard_map/reduce_scatter | solution.py:220
  898.2 230.4 %copy-start.107 = (f32[1,1024]{1,0:T(1,128)}, f32[1,1024]{1,0:T(1,128)S(1)}, u32[]{:S(2)}) copy-start(f32[1,1024]{1,0:T(1,128)S(1)} %convert_element_type.310) | copy-start | bytes 12292
  1128.3 157.5 %reduce-scatter.44.cloned.1.call-start = ((), (), s32[]{:S(2)}) async-start(), calls=%async_computation.26 | async-start | bytes 5242880 | tf_op jit(solution)/shard_map/reduce_scatter | solution.py:211
  1141.0 144.8 %copy-start.89 = (f32[1024]{0:T(1024)S(1)}, f32[1024]{0:T(1024)}, u32[]{:S(2)}) copy-start(f32[1024]{0:T(1024)} %get-tuple-element.852) | copy-start | bytes 12292
  1141.0 229.4 %all-gather.37.cloned.1.call-start = ((), (), s32[]{:S(2)}) async-start(), calls=%async_computation.29 | async-start | bytes 5242880 | tf_op jit(solution)/shard_map/all_gather | solution.py:207
  1291.6 287.1 %reduce-scatter.48.cloned.1.call-start = ((), (), s32[]{:S(2)}) async-start(), calls=%async_computation.30 | async-start | bytes 5242880 | tf_op jit(solution)/shard_map/reduce_scatter | solution.py:220
  1500.7 165.6 %all-gather.39.cloned.1.call-start = ((), (), s32[]{:S(2)}) async-start(), calls=%async_computation.31 | async-start | bytes 5242880 | tf_op jit(solution)/shard_map/all_gather | solution.py:207
  1587.4 95.3 %copy-start.115 = (bf16[1,1024,1024]{2,1,0:T(8,128)(2,1)S(1)}, bf16[1,1024,1024]{2,1,0:T(8,128)(2,1)}, u32[]{:S(2)}) copy-start(bf16[1,1024,1024]{2,1,0:T(8,128)(2,1)} %all-gather.45.cloned.1.call-done) | copy-start | bytes 6291460
  1587.4 179.6 %reduce-scatter.50.cloned.1.call-start = ((), (), s32[]{:S(2)}) async-start(), calls=%async_computation.32 | async-start | bytes 5242880 | tf_op jit(solution)/shard_map/reduce_scatter | solution.py:220
  1689.1 165.7 %all-gather.41.cloned.1.call-start = ((), (), s32[]{:S(2)}) async-start(), calls=%async_computation.33 | async-start | bytes 5242880 | tf_op jit(solution)/shard_map/all_gather | solution.py:207
  1776.0 231.6 %reduce-scatter.72.cloned.1.call-start = ((), (), s32[]{:S(2)}) async-start(), calls=%async_computation.50 | async-start | bytes 2359296
  1789.7 219.1 %reduce-scatter.64.cloned.1.call-start = ((), (), s32[]{:S(2)}) async-start(), calls=%async_computation.46 | async-start | bytes 73728
  1790.7 218.8 %reduce-scatter.68.cloned.1.call-start = ((), (), s32[]{:S(2)}) async-start(), calls=%async_computation.48 | async-start | bytes 589824
  1795.3 222.1 %reduce-scatter.60.cloned.1.call-start = ((), (), s32[]{:S(2)}) async-start(), calls=%async_computation.44 | async-start | bytes 1769472
  1807.7 254.1 %reduce-scatter.70.cloned.1.call-start = ((), (), s32[]{:S(2)}) async-start(), calls=%async_computation.49 | async-start | bytes 2359296
  1821.2 285.4 %reduce-scatter.56.cloned.1.call-start = ((), (), s32[]{:S(2)}) async-start(), calls=%async_computation.36 | async-start | bytes 2359296 | tf_op jit(solution)/shard_map/reduce_scatter | solution.py:393
  1830.7 320.4 %reduce-scatter.54.cloned.1.call-start = ((), (), s32[]{:S(2)}) async-start(), calls=%async_computation.35 | async-start | bytes 2359296 | tf_op jit(solution)/shard_map/reduce_scatter | solution.py:393
  1840.3 346.8 %reduce-scatter.62.cloned.1.call-start = ((), (), s32[]{:S(2)}) async-start(), calls=%async_computation.45 | async-start | bytes 73728
  1967.3 256.8 %reduce-scatter.66.cloned.1.call-start = ((), (), s32[]{:S(2)}) async-start(), calls=%async_computation.47 | async-start | bytes 589824
  1981.7 285.0 %reduce-scatter.58.cloned.1.call-start = ((), (), s32[]{:S(2)}) async-start(), calls=%async_computation.43 | async-start | bytes 1769472
  1997.7 348.4 %reduce-scatter.52.cloned.1.call-start = ((), (), s32[]{:S(2)}) async-start(), calls=%async_computation.34 | async-start | bytes 5242880 | tf_op jit(solution)/shard_map/reduce_scatter | solution.py:220
  2005.8 474.1 %reduce-scatter.74.cloned.1.call-start = ((), (), s32[]{:S(2)}) async-start(), calls=%async_computation.51 | async-start | bytes 540672
  2153.1 192.9 %copy-start.5 = (bf16[512,1024]{1,0:T(8,128)(2,1)S(1)}, bf16[512,1024]{1,0:T(8,128)(2,1)}, u32[]{:S(2)}) copy-start(bf16[512,1024]{1,0:T(8,128)(2,1)} %param.26) | copy-start | bytes 3145732
  2153.1 192.9 %copy-start.67 = (f32[1024]{0:T(1024)S(1)}, f32[1024]{0:T(1024)}, u32[]{:S(2)}) copy-start(f32[1024]{0:T(1024)} %copy-done.66) | copy-start | bytes 12292
  2153.1 192.9 %copy-start.71 = (f32[512]{0:T(512)S(1)}, f32[512]{0:T(512)}, u32[]{:S(2)}) copy-start(f32[512]{0:T(512)} %copy-done.70) | copy-start | bytes 6148
  2224.1 123.8 %copy-start.82 = (f32[512]{0:T(512)S(1)}, f32[512]{0:T(512)}, u32[]{:S(2)}) copy-start(f32[512]{0:T(512)} %copy-done.81) | copy-start | bytes 6148
  2224.1 123.8 %copy-start.78 = (f32[512]{0:T(512)S(1)}, f32[512]{0:T(512)}, u32[]{:S(2)}) copy-start(f32[512]{0:T(512)} %copy-done.77) | copy-start | bytes 6148
  2268.1 82.5 %copy-start.96 = (f32[1024]{0:T(1024)S(1)}, f32[1024]{0:T(1024)}, u32[]{:S(2)}) copy-start(f32[1024]{0:T(1024)} %get-tuple-element.1064) | copy-start | bytes 12292
  2268.1 82.5 %copy-start.97 = (f32[1024]{0:T(1024)S(1)}, f32[1024]{0:T(1024)}, u32[]{:S(2)}) copy-start(f32[1024]{0:T(1024)} %get-tuple-element.843) | copy-start | bytes 12292
  (139 other events, 2704.6 us)
Sparse Core Ops, SparseCore 0:
  10.5 27.2 all-gather.42
  120.9 84.5 all-gather.26
  295.2 77.8 reduce-scatter.37
  375.6 28.7 all-gather.44
  406.5 77.7 all-gather.28
  486.8 29.6 all-gather.46
  528.4 76.3 reduce-scatter.39
  606.8 28.1 all-gather.48
  637.1 78.1 all-gather.30
  805.2 77.8 reduce-scatter.41
  885.7 28.7 all-gather.50
  916.6 77.7 all-gather.32
  996.5 29.6 all-gather.52
  1027.7 77.8 all-gather.34
  1128.4 77.8 reduce-scatter.45
  1208.4 77.2 reduce-scatter.43
  1291.7 78.6 all-gather.36
  1500.8 77.8 reduce-scatter.47
  1587.6 78.6 all-gather.38
  1689.2 77.8 reduce-scatter.49
  1776.1 78.6 all-gather.40
  1858.5 42.3 reduce-scatter.71
  1904.4 32.7 reduce-scatter.63
  1941.0 34.1 reduce-scatter.67
  1978.4 38.8 reduce-scatter.59
  2020.5 41.2 reduce-scatter.69
  2065.3 41.2 reduce-scatter.55
  2109.8 41.1 reduce-scatter.53
  2154.3 32.7 reduce-scatter.61
  2190.0 34.1 reduce-scatter.65
  2227.8 38.9 reduce-scatter.57
  2269.2 76.8 reduce-scatter.51
  2354.7 125.1 reduce-scatter.73
where the time goes:
time: 2510 us; the launch traced here: 2490 us
  waiting for transfers between devices  1580 us (63%)
  matrix products  306 us (12%)
  local copies, waits for them, and re-layouts  300 us (12%)
  blocking collectives  141 us (6%)
  other arithmetic  114 us (5%)
  loops' own time  28 us (1%)
    reduce_scatter x4, waiting for transfers between devices, reduce_forward(): lax.psum_scatter(row_term(jnp.int32(0), shard_rows * lax.axis_size('tenso...  306 us
    reduce_scatter x4, waiting for transfers between devices, reduce_backward(): lax.psum_scatter(row_term(jnp.int32(0), shard_rows * lax.axis_size('tenso...  298 us
    all_gather x4, waiting for transfers between devices, spread_rows(): return lax.all_gather(values, 'tensor', axis=0, tiled=True)  293 us
    unnamed x42, waiting for transfers between devices  272 us
    all_gather x4, waiting for transfers between devices, spread_grads(): return lax.all_gather(values, 'tensor', axis=0, tiled=True)  249 us
    reduce_scatter x2, waiting for transfers between devices, body(): lax.psum_scatter(up_grad.astype(jnp.bfloat16), 'dp', scatter_dimension=0,...  88.1 us
    unnamed x254, local copies, waits for them, and re-layouts  74.2 us
    all_gather x1, blocking collectives, body(): lax.all_gather(row_params, ('dp', 'tensor'), axis=2, tiled=True)  62.6 us
  transfers between devices with their start and end apart: 33, of which 28 were waited for; matrix products, arithmetic and copies ran while one was open for 13% of the time, Pallas kernels for 0%

commit v1 on v0

v1 whole, which is shorter than its diff:
```python
import functools

import jax
import jax.numpy as jnp
from jax import lax
from jax.experimental import pallas as pl
from jax.experimental.pallas import tpu as pltpu
from jax.sharding import PartitionSpec as P

HEADS = 16
HEAD_DIM = 64
LANES = 128
QBLK = 256

EPSILON = 1e-05
MASKED = -1e30
BOTH = ("dp", "tensor")
F32 = jnp.float32
BF16 = jnp.bfloat16


def dot_nt(left, right):
    return lax.dot_general(left, right, (((1,), (1,)), ((), ())), preferred_element_type=F32)


def dot_nn(left, right):
    return lax.dot_general(left, right, (((1,), (0,)), ((), ())), preferred_element_type=F32)


def dot_tn(left, right):
    return lax.dot_general(left, right, (((0,), (0,)), ((), ())), preferred_element_type=F32)


def fill_places(seg_col, seg_row, places, length):
    for first in range(0, length, QBLK):
        count = first + QBLK
        key_at = lax.broadcasted_iota(jnp.int32, (count, QBLK), 0)
        query_at = first + lax.broadcasted_iota(jnp.int32, (count, QBLK), 1)
        allowed = (key_at <= query_at) & (
            seg_col[0:count, :] == seg_row[:, first : first + QBLK]
        )
        places[0:count, first : first + QBLK] = jnp.where(
            allowed, key_at.astype(F32), MASKED
        )


def head_lanes(values, member):
    lane = lax.broadcasted_iota(jnp.int32, values.shape, 1)
    return jnp.where(lane // HEAD_DIM == member, values, jnp.zeros_like(values))


def forward_kernel(slopes, packed, seg_col, seg_row, mixed, places):
    group = pl.program_id(0)
    length = packed.shape[0]

    @pl.when(group == 0)
    def _():
        fill_places(seg_col, seg_row, places, length)

    scale = HEAD_DIM**-0.5
    values_t = packed[:, 2 * LANES : 3 * LANES].astype(F32).T.astype(BF16)
    keys = [
        head_lanes(packed[:, LANES : 2 * LANES].astype(F32), member).astype(BF16)
        for member in range(2)
    ]
    for first in range(0, length, QBLK):
        count = first + QBLK
        queries = (packed[first:count, 0:LANES].astype(F32) * scale).astype(BF16)
        parts = []
        for member in range(2):
            slope = slopes[group, member]
            scores = dot_nt(keys[member][0:count, :], queries)
            scores = scores + slope * places[0:count, first:count]
            top = jnp.max(scores, axis=0, keepdims=True)
            lifted = jnp.exp(scores - top)
            total = jnp.sum(lifted, axis=0, keepdims=True)
            rows = values_t[member * HEAD_DIM : (member + 1) * HEAD_DIM, 0:count]
            parts.append(dot_nn(rows, lifted.astype(BF16)) / total)
        mixed[first:count, :] = jnp.concatenate(parts, axis=0).T.astype(BF16)


def backward_kernel(
    slopes, packed, upstream, seg_col, seg_row, packed_grad, sums, places, key_grad, value_grad
):
    group = pl.program_id(0)
    length = packed.shape[0]

    @pl.when(group == 0)
    def _():
        fill_places(seg_col, seg_row, places, length)

    scale = HEAD_DIM**-0.5
    keys_f32 = packed[:, LANES : 2 * LANES].astype(F32)
    values_f32 = packed[:, 2 * LANES : 3 * LANES].astype(F32)
    keys = [head_lanes(keys_f32, member).astype(BF16) for member in range(2)]
    value_rows = [head_lanes(values_f32, member).astype(BF16) for member in range(2)]
    keys_t = (keys_f32 * scale).T.astype(BF16)
    query_sum = jnp.zeros((1, LANES), F32)
    for first in reversed(range(0, length, QBLK)):
        count = first + QBLK
        queries_f32 = packed[first:count, 0:LANES].astype(F32) * scale
        queries = queries_f32.astype(BF16)
        above_f32 = upstream[first:count, :].astype(F32)
        above = above_f32.astype(BF16)
        parts = []
        key_part = None
        value_part = None
        for member in range(2):
            slope = slopes[group, member]
            scores = dot_nt(keys[member][0:count, :], queries)
            scores = scores + slope * places[0:count, first:count]
            top = jnp.max(scores, axis=0, keepdims=True)
            lifted = jnp.exp(scores - top)
            total = jnp.sum(lifted, axis=0, keepdims=True)
            chances = lifted * (1.0 / total)
            chance_grad = dot_nt(value_rows[member][0:count, :], above)
            inner = jnp.sum(chance_grad * chances, axis=0, keepdims=True)
            score_grad = (chances * (chance_grad - inner)).astype(BF16)
            rows = keys_t[member * HEAD_DIM : (member + 1) * HEAD_DIM, 0:count]
            parts.append(dot_nn(rows, score_grad))
            key_term = dot_nn(score_grad, head_lanes(queries_f32, member).astype(BF16))
            value_term = dot_nn(chances.astype(BF16), head_lanes(above_f32, member).astype(BF16))
            key_part = key_term if member == 0 else key_part + key_term
            value_part = value_term if member == 0 else value_part + value_term
        query_grad = jnp.concatenate(parts, axis=0).T
        query_sum = query_sum + jnp.sum(query_grad, axis=0, keepdims=True)
        packed_grad[first:count, 0:LANES] = query_grad.astype(BF16)
        if count == length:
            key_grad[...] = key_part
            value_grad[...] = value_part
        else:
            key_grad[0:count, :] += key_part
            value_grad[0:count, :] += value_part
    packed_grad[:, LANES : 2 * LANES] = key_grad[...].astype(BF16)
    packed_grad[:, 2 * LANES : 3 * LANES] = value_grad[...].astype(BF16)
    sums[0:1, :] = query_sum
    sums[1:2, :] = jnp.sum(value_grad[...], axis=0, keepdims=True)


def attention_forward(packed, seg_col, seg_row, slopes):
    length, width = packed.shape
    groups = width // (3 * LANES)
    return pl.pallas_call(
        forward_kernel,
        grid=(groups,),
        in_specs=[
            pl.BlockSpec(memory_space=pltpu.SMEM),
            pl.BlockSpec((length, 3 * LANES), lambda g: (0, g)),
            pl.BlockSpec((length, 1), lambda g: (0, 0)),
            pl.BlockSpec((1, length), lambda g: (0, 0)),
        ],
        out_specs=pl.BlockSpec((length, LANES), lambda g: (0, g)),
        out_shape=jax.ShapeDtypeStruct((length, groups * LANES), BF16),
        scratch_shapes=[pltpu.VMEM((length, length), F32)],
        compiler_params=pltpu.CompilerParams(vmem_limit_bytes=40 * 2**20),
        cost_estimate=pl.CostEstimate(
            flops=groups * 2 * length * length * 256 * 3,
            bytes_accessed=groups * length * LANES * 8,
            transcendentals=groups * length * length * 2,
        ),
    )(slopes, packed, seg_col, seg_row)


def attention_backward(packed, upstream, seg_col, seg_row, slopes):
    length, width = packed.shape
    groups = width // (3 * LANES)
    return pl.pallas_call(
        backward_kernel,
        grid=(groups,),
        in_specs=[
            pl.BlockSpec(memory_space=pltpu.SMEM),
            pl.BlockSpec((length, 3 * LANES), lambda g: (0, g)),
            pl.BlockSpec((length, LANES), lambda g: (0, g)),
            pl.BlockSpec((length, 1), lambda g: (0, 0)),
            pl.BlockSpec((1, length), lambda g: (0, 0)),
        ],
        out_specs=[
            pl.BlockSpec((length, 3 * LANES), lambda g: (0, g)),
            pl.BlockSpec((None, 2, LANES), lambda g: (g, 0, 0)),
        ],
        out_shape=[
            jax.ShapeDtypeStruct((length, width), BF16),
            jax.ShapeDtypeStruct((groups, 2, LANES), F32),
        ],
        scratch_shapes=[
            pltpu.VMEM((length, length), F32),
            pltpu.VMEM((length, LANES), F32),
            pltpu.VMEM((length, LANES), F32),
        ],
        compiler_params=pltpu.CompilerParams(vmem_limit_bytes=48 * 2**20),
        cost_estimate=pl.CostEstimate(
            flops=groups * 2 * length * length * 256 * 8,
            bytes_accessed=groups * length * LANES * 14,
            transcendentals=groups * length * length * 2,
        ),
    )(slopes, packed, upstream, seg_col, seg_row)


def normalise(values):
    centred = values - jnp.mean(values, axis=-1, keepdims=True)
    spread = jnp.mean(centred * centred, axis=-1, keepdims=True)
    inverse = lax.rsqrt(spread + EPSILON)
    return centred * inverse, inverse


def layer_norm(values, gain_row, shift_row):
    return normalise(values)[0] * gain_row + shift_row


def norm_back(values, gain_row, upstream):
    unit, inverse = normalise(values)
    gain_grad = jnp.sum(upstream * unit, axis=0)
    shift_grad = jnp.sum(upstream, axis=0)
    inner = upstream * gain_row
    result = inverse * (
        inner
        - jnp.mean(inner, axis=-1, keepdims=True)
        - unit * jnp.mean(inner * unit, axis=-1, keepdims=True)
    )
    return result, gain_grad, shift_grad


def gelu_tanh(values):
    return jax.nn.gelu(values, approximate=True)


def bits_of(count):
    return [1 << place for place in range(count.bit_length() - 1)]


def body(
    dp_size,
    tensor_size,
    tokens_in,
    segment_ids,
    qkv_weight,
    qv_bias,
    out_weight,
    up_weight,
    up_bias,
    down_weight,
    row_params,
    cotangent,
):
    layers = qkv_weight.shape[0]
    shard_rows, features = tokens_in.shape
    spans = 2 * segment_ids.shape[0]
    inner_size = tensor_size // spans
    pairs = dp_size // 2
    devices = dp_size * tensor_size
    heads_half = HEADS // tensor_size // 2
    half_width = heads_half * HEAD_DIM
    wide = features // dp_size

    dp_at = lax.axis_index("dp")
    tensor_at = lax.axis_index("tensor")
    core = dp_at % 2
    pair = dp_at // 2
    span = tensor_at // inner_size
    inner = tensor_at % inner_size
    core_one = core == 1

    core_mask = tensor_size
    inner_masks = bits_of(inner_size)
    span_bits = bits_of(spans)
    pair_bits = bits_of(pairs)
    span_masks = {bit: bit * inner_size for bit in span_bits}
    pair_masks = {bit: bit * 2 * tensor_size for bit in pair_bits}

    def swap(values, mask):
        return lax.ppermute(values, BOTH, [(at, at ^ mask) for at in range(devices)])

    def crossed(at):
        at_core = (at // tensor_size) % 2
        at_span = (at % tensor_size) // inner_size
        return at if at_core == at_span % 2 else at ^ (core_mask | inner_size)

    def cross(values):
        return lax.ppermute(values, BOTH, [(at, crossed(at)) for at in range(devices)])

    def ordered(values, mask, is_high, axis):
        other = swap(values, mask)
        return jnp.concatenate(
            [jnp.where(is_high, other, values), jnp.where(is_high, values, other)], axis=axis
        )

    def group_rows(values):
        for mask in inner_masks:
            values = ordered(values, mask, (inner & mask) != 0, 0)
        return ordered(values, core_mask, core_one, 0)

    def group_sum(values):
        for mask in inner_masks + [core_mask]:
            low = values.astype(BF16)
            values = low.astype(F32) + swap(low, mask).astype(F32)
        return values

    high_spans = list(reversed(span_bits))
    orders = []
    for chosen in (pair_bits, list(reversed(pair_bits))):
        orders.append(
            [("span", bit) for bit in high_spans[:-1]]
            + [("pair", bit) for bit in chosen[:-1]]
            + [("span", bit) for bit in high_spans[-1:]]
            + [("pair", bit) for bit in chosen[-1:]]
        )

    def offsets(kind, order):
        found = [0]
        for step_kind, bit in order:
            if step_kind == kind:
                found = found + [place ^ bit for place in found]
        return found

    span_offsets = offsets("span", orders[0])
    pair_offsets = [offsets("pair", order) for order in orders]

    def mask_of(kind, bit):
        return span_masks[bit] if kind == "span" else pair_masks[bit]

    def to_local(values):
        axis = values.ndim - 1
        blocks = []
        for half in range(2):
            for offset in pair_offsets[half]:
                at = ((pair ^ offset) * 2 + half) * wide
                blocks.append(lax.dynamic_slice_in_dim(values, at, wide, axis))
        return jnp.concatenate(blocks, axis=axis)

    def from_local(values):
        axis = values.ndim - 1
        blocks = []
        for true_pair in range(pairs):
            for half in range(2):
                table = [0] * pairs
                for position, offset in enumerate(pair_offsets[half]):
                    table[offset] = position
                position = jnp.asarray(table, jnp.int32)[pair ^ true_pair]
                at = (half * pairs + position) * wide
                blocks.append(lax.dynamic_slice_in_dim(values, at, wide, axis))
        return jnp.concatenate(blocks, axis=axis)

    def fetch(halves, feature_axis):
        done = []
        for half, order in zip(halves, orders):
            for kind, bit in order:
                axis = feature_axis if kind == "pair" else 1 - feature_axis
                half = jnp.concatenate([half, swap(half, mask_of(kind, bit))], axis=axis)
            done.append(half)
        return jnp.concatenate(done, axis=feature_axis)

    def split_cores(low, high):
        mine = jnp.where(core_one, high, low)
        other = swap(jnp.where(core_one, low, high), core_mask)
        return jnp.where(core_one, other, mine), jnp.where(core_one, mine, other)

    def fetch_qkv(number):
        local = qkv_weight[number].transpose(1, 0, 2)
        rows = local.shape[0]
        low = local[:, :, :half_width].reshape(rows, 3 * half_width)
        high = local[:, :, half_width:].reshape(rows, 3 * half_width)
        return fetch(split_cores(low, high), 0)

    def fetch_columns(local):
        middle_at = local.shape[1] // 2
        return fetch(split_cores(local[:, :middle_at], local[:, middle_at:]), 0)

    def fetch_rows(local):
        middle_at = local.shape[0] // 2
        return fetch(split_cores(local[:middle_at], local[middle_at:]), 1)

    def reduce_grad(term, feature_axis):
        done = []
        part = features // 2
        for half, order in enumerate(orders):
            keep = term(half * part, part // 2).astype(BF16)
            send = term(half * part + part // 2, part // 2).astype(BF16)
            steps = list(reversed(order))
            for at, (kind, bit) in enumerate(steps):
                other = swap(send, mask_of(kind, bit))
                if at + 1 == len(steps):
                    done.append(keep.astype(F32) + other.astype(F32))
                    break
                next_kind = steps[at + 1][0]
                axis = feature_axis if next_kind == "pair" else 1 - feature_axis
                size = keep.shape[axis] // 2
                pieces = []
                for first in (0, size):
                    ours = lax.slice_in_dim(keep, first, first + size, axis=axis)
                    theirs = lax.slice_in_dim(other, first, first + size, axis=axis)
                    pieces.append((ours.astype(F32) + theirs.astype(F32)).astype(BF16))
                keep, send = pieces
        return done

    def join_cores(halves):
        first, second = halves
        mine = jnp.where(core_one, second, first)
        other = swap(jnp.where(core_one, first, second).astype(BF16), core_mask).astype(F32)
        return jnp.where(core_one, other, mine), jnp.where(core_one, mine, other)

    small_local = jnp.concatenate(
        [row_params.reshape(-1), qv_bias.reshape(-1), up_bias.reshape(-1)]
    )[None]
    small = small_local
    for mask in bits_of(devices):
        small = ordered(small, mask, (dp_at * tensor_size + tensor_at) & mask != 0, 0)
    row_size, qv_size = row_params.size, qv_bias.size
    rows_every = to_local(
        small[:, :row_size]
        .reshape(devices, layers, 6, -1)
        .transpose(1, 2, 0, 3)
        .reshape(layers, 6, features)
        .astype(F32)
    )

    def local_units(values, kinds):
        values = values.reshape(dp_size, spans, inner_size, layers, kinds, -1)
        values = lax.dynamic_slice_in_dim(values, core * pairs, pairs, 0)
        values = lax.dynamic_slice_in_dim(values, inner, 1, 2)[:, :, 0]
        blocks = [
            lax.dynamic_slice_in_dim(values, span ^ offset, 1, 1)[:, 0] for offset in span_offsets
        ]
        values = jnp.stack(blocks)
        return values.transpose(2, 3, 0, 1, 4).reshape(layers, kinds, -1).astype(F32)

    qv_local = local_units(small[:, row_size : row_size + qv_size], 2)
    up_bias_local = local_units(small[:, row_size + qv_size :], 1)[:, 0]

    span_at = jnp.stack([span ^ offset for offset in span_offsets])
    heads_at = (span_at * inner_size + inner)[:, None] * (2 * heads_half) + core * heads_half
    heads_at = heads_at + jnp.arange(heads_half, dtype=jnp.int32)[None]
    slopes = (2.0 ** (-8.0 * (heads_at.astype(F32) + 1.0) / HEADS)).reshape(-1, 2)
    joined_spans = max(1, LANES // half_width)

    def to_lanes(packed):
        if joined_spans == 1:
            return packed
        length = packed.shape[0]
        packed = packed.reshape(length, -1, joined_spans, 3, half_width)
        return packed.transpose(0, 1, 3, 2, 4).reshape(length, -1)

    def from_lanes(packed):
        if joined_spans == 1:
            return packed
        length = packed.shape[0]
        packed = packed.reshape(length, -1, 3, joined_spans, half_width)
        return packed.transpose(0, 1, 3, 2, 4).reshape(length, -1)

    own_segment = lax.dynamic_slice_in_dim(segment_ids, span // 2, 1, 0)
    seg_row = jnp.where(core == span % 2, own_segment, swap(own_segment, core_mask))
    seg_col = seg_row.reshape(-1, 1)

    stream = to_local(group_rows(cross(tokens_in))).astype(F32)
    upstream_low = to_local(group_rows(cross(cotangent)))

    stash = []
    for number in range(layers):
        rows = rows_every[number]
        qkv_full = fetch_qkv(number)
        out_full = fetch_rows(out_weight[number])
        up_full = fetch_columns(up_weight[number])
        down_full = fetch_rows(down_weight[number])
        normed = layer_norm(stream, rows[0], rows[1]).astype(BF16)
        qkv_bias = jnp.stack(
            [qv_local[number, 0], jnp.zeros_like(qv_local[number, 0]), qv_local[number, 1]]
        )
        qkv_bias = qkv_bias.reshape(3, spans, half_width).transpose(1, 0, 2).reshape(-1)
        packed = (jnp.dot(normed, qkv_full, preferred_element_type=F32) + qkv_bias).astype(BF16)
        packed = to_lanes(packed)
        attended = attention_forward(packed, seg_col, seg_row, slopes)
        middle = stream + (
            group_sum(jnp.dot(attended, out_full, preferred_element_type=F32)) + rows[2]
        )
        normed_two = layer_norm(middle, rows[3], rows[4]).astype(BF16)
        pre_gelu = (
            jnp.dot(normed_two, up_full, preferred_element_type=F32) + up_bias_local[number]
        )
        hidden = gelu_tanh(pre_gelu).astype(BF16)
        stash.append(
            (
                stream,
                normed,
                packed,
                attended,
                middle,
                normed_two,
                pre_gelu,
                hidden,
                qkv_full,
                out_full,
                up_full,
                down_full,
            )
        )
        stream = middle + (
            group_sum(jnp.dot(hidden, down_full, preferred_element_type=F32)) + rows[5]
        )

    def give_back(values):
        at = (core * inner_size + inner) * shard_rows
        return cross(lax.dynamic_slice_in_dim(from_local(values), at, shard_rows, 0))

    output = give_back(stream.astype(BF16))

    def total_sum(values):
        for bit in span_bits:
            values = values + swap(values, span_masks[bit])
        for bit in pair_bits:
            values = values + swap(values, pair_masks[bit])
        return values

    upstream = upstream_low.astype(F32)
    weight_grads = [None] * layers
    small_grads = [None] * layers
    for number in reversed(range(layers)):
        (
            stream_in,
            normed,
            packed,
            attended,
            middle,
            normed_two,
            pre_gelu,
            hidden,
            qkv_full,
            out_full,
            up_full,
            down_full,
        ) = stash[number]
        rows = rows_every[number]

        def columns_of(left, right):
            def term(first, count):
                return dot_tn(left, right[:, first : first + count])

            return term

        def rows_of(left, right):
            def term(first, count):
                return dot_tn(left[:, first : first + count], right)

            return term

        down_bias_grad = jnp.sum(upstream, axis=0)
        down_in = upstream.astype(BF16)
        hidden_grad = dot_nt(down_in, down_full)
        pre_grad = jax.vjp(gelu_tanh, pre_gelu)[1](hidden_grad)[0]
        up_bias_grad = jnp.sum(pre_grad, axis=0)
        pre_low = pre_grad.astype(BF16)
        normed_two_grad = group_sum(dot_nt(pre_low, up_full))
        down_grad = reduce_grad(columns_of(hidden, down_in), 1)
        up_grad = reduce_grad(rows_of(normed_two, pre_low), 0)
        middle_grad, gain_two_grad, shift_two_grad = norm_back(middle, rows[3], normed_two_grad)
        middle_grad = middle_grad + upstream
        out_bias_grad = jnp.sum(middle_grad, axis=0)
        out_in = middle_grad.astype(BF16)
        attended_grad = dot_nt(out_in, out_full).astype(BF16)
        out_grad = reduce_grad(columns_of(attended, out_in), 1)
        packed_grad, qv_sums = attention_backward(packed, attended_grad, seg_col, seg_row, slopes)
        packed_grad = from_lanes(packed_grad)
        normed_grad = group_sum(dot_nt(packed_grad, qkv_full))
        qkv_grad = reduce_grad(rows_of(normed, packed_grad), 0)
        stream_grad, gain_one_grad, shift_one_grad = norm_back(stream_in, rows[0], normed_grad)
        upstream = middle_grad + stream_grad

        row_grads = from_local(
            jnp.stack(
                [
                    gain_one_grad,
                    shift_one_grad,
                    out_bias_grad,
                    gain_two_grad,
                    shift_two_grad,
                    down_bias_grad,
                ]
            )
        )
        qv_units = qv_sums.transpose(1, 0, 2).reshape(2, spans, half_width)
        units = jnp.concatenate(
            [qv_units.transpose(1, 0, 2).reshape(spans, -1), up_bias_grad.reshape(spans, -1)],
            axis=1,
        )
        table = [0] * spans
        for position, offset in enumerate(span_offsets):
            table[offset] = position
        order_at = jnp.stack(
            [jnp.asarray(table, jnp.int32)[span ^ true_span] for true_span in range(spans)]
        )
        units = jnp.take(units, order_at, axis=0)
        small_grads[number] = total_sum(jnp.concatenate([row_grads.reshape(-1), units.reshape(-1)]))

        low, high = join_cores(qkv_grad)
        row_count = low.shape[0]
        qkv_own = jnp.concatenate(
            [low.reshape(row_count, 3, half_width), high.reshape(row_count, 3, half_width)], axis=2
        ).transpose(1, 0, 2)
        weight_grads[number] = (
            qkv_own,
            jnp.concatenate(join_cores(out_grad), axis=0),
            jnp.concatenate(join_cores(up_grad), axis=1),
            jnp.concatenate(join_cores(down_grad), axis=0),
        )

    summed = jnp.stack(small_grads)
    row_total = 6 * features
    own = features // devices
    row_summed = lax.dynamic_slice_in_dim(
        summed[:, :row_total].reshape(layers, 6, features),
        (dp_at * tensor_size + tensor_at) * own,
        own,
        2,
    )
    units = summed[:, row_total:].reshape(layers, spans, -1)
    units = lax.dynamic_slice_in_dim(units, span, 1, 1)[:, 0]
    other_units = swap(units, core_mask)
    units = jnp.where(core_one == (dp_at >= pairs), units, other_units)
    place = dp_at % pairs
    qv_part = units[:, : 2 * half_width].reshape(layers, 2, pairs, -1)
    up_part = units[:, 2 * half_width :].reshape(layers, pairs, -1)
    qv_own = lax.dynamic_slice_in_dim(qv_part, place, 1, 2)[:, :, 0]
    up_own = lax.dynamic_slice_in_dim(up_part, place, 1, 1)[:, 0]

    joined = [
        jnp.stack([weight_grads[number][member] for number in range(layers)]) for member in range(4)
    ]
    return (
        output,
        give_back(upstream.astype(BF16)).astype(F32),
        joined[0],
        qv_own,
        joined[1],
        joined[2],
        up_own,
        joined[3],
        row_summed,
    )


def solution(mesh):
    placed = (
        P(("dp", "tensor"), None),
        P("dp", None),
        P(None, None, "dp", "tensor"),
        P(None, None, ("tensor", "dp")),
        P(None, "tensor", "dp"),
        P(None, "dp", "tensor"),
        P(None, ("tensor", "dp")),
        P(None, "tensor", "dp"),
        P(None, None, ("dp", "tensor")),
        P(("dp", "tensor"), None),
    )
    return jax.shard_map(
        functools.partial(body, mesh.shape["dp"], mesh.shape["tensor"]),
        mesh=mesh,
        in_specs=placed,
        out_specs=(
            P(("dp", "tensor"), None),
            P(("dp", "tensor"), None),
            P(None, None, "dp", "tensor"),
            P(None, None, ("tensor", "dp")),
            P(None, "tensor", "dp"),
            P(None, "dp", "tensor"),
            P(None, ("tensor", "dp")),
            P(None, "tensor", "dp"),
            P(None, None, ("dp", "tensor")),
        ),
        check_vma=False,
    )
```

time: 2510 us -> 1130 us (0.45)
  waiting for transfers between devices: 1580 us -> 388 us
  local copies, waits for them, and re-layouts: 300 us -> 40.1 us
  starting transfers between devices: 2.53 us -> 236 us
  blocking collectives: 141 us -> 0 us
  Pallas kernels: 0 us -> 90.9 us
  matrix products: 306 us -> 242 us
  loops' own time: 28 us -> 0 us
    reduce_scatter x10 -> x0, waiting for transfers between devices: 692 us -> none  [the longest x4 306 us: reduce_forward(): lax.psum_scatter(row_term(jnp.int32(0), shard_rows * lax.axis_size('tenso...]
    all_gather x14 -> x0, waiting for transfers between devices: 616 us -> none  [the longest x4 293 us: spread_rows(): return lax.all_gather(values, 'tensor', axis=0, tiled=True)]
    ppermute x0 -> x173, waiting for transfers between devices: none -> 388 us  [the longest x169 388 us: swap(): lax.ppermute(values, BOTH, [(at, at ^ mask) for at in range(devices)])]
    unnamed x42 -> x0, waiting for transfers between devices: 272 us -> none
    ppermute x0 -> x173, starting transfers between devices: none -> 236 us  [the longest x169 207 us: swap(): lax.ppermute(values, BOTH, [(at, at ^ mask) for at in range(devices)])]
    all_gather x7 -> x0, blocking collectives: 129 us -> none  [the longest x1 62.6 us: body(): lax.all_gather(row_params, ('dp', 'tensor'), axis=2, tiled=True)]
    pallas_call x0 -> x4, Pallas kernels: none -> 90.9 us  [the longest x2 54.8 us: attention_backward(): pl.pallas_call(backward_kernel, grid=(groups,), in_specs=[pl.BlockSpec(me...]
    slice x17 -> x4, local copies, waits for them, and re-layouts: 70 us -> 1.3 us  [the longest x1 0.65 us: body(): rows[5]]
  transfers between devices with their start and end apart: 33 -> 173, of which waited for: 28 -> 81; matrix products, arithmetic and copies ran while one was open for 13% -> 23% of each run, Pallas kernels for 0% -> 8%
where the time goes in v1:
time: 1130 us; the launch traced here: 1110 us
  waiting for transfers between devices  388 us (34%)
  matrix products  242 us (21%)
  starting transfers between devices  236 us (21%)
  other arithmetic  107 us (9%)
  Pallas kernels  90.9 us (8%)
  local copies, waits for them, and re-layouts  40.1 us (4%)
    ppermute x169, waiting for transfers between devices, swap(): lax.ppermute(values, BOTH, [(at, at ^ mask) for at in range(devices)])  388 us
    ppermute x169, starting transfers between devices, swap(): lax.ppermute(values, BOTH, [(at, at ^ mask) for at in range(devices)])  207 us
    dot_general x8, matrix products, dot_nt(): lax.dot_general(left, right, (((1,), (1,)), ((), ())), preferred_element_...  101 us
    dot_general x32, matrix products, dot_tn(): lax.dot_general(left, right, (((0,), (0,)), ((), ())), preferred_element_...  62.7 us
    pallas_call x2, Pallas kernels, attention_backward(): pl.pallas_call(backward_kernel, grid=(groups,), in_specs=[pl.BlockSpec(me...  54.8 us
    pallas_call x2, Pallas kernels, attention_forward(): pl.pallas_call(forward_kernel, grid=(groups,), in_specs=[pl.BlockSpec(mem...  36.1 us
    ppermute x4, starting transfers between devices, cross(): lax.ppermute(values, BOTH, [(at, crossed(at)) for at in range(devices)])  29.3 us
    dot_general x2, matrix products, body(): jnp.dot(normed_two, up_full, preferred_element_type=F32)  28.6 us
  transfers between devices with their start and end apart: 173, of which 81 were waited for; matrix products, arithmetic and copies ran while one was open for 23% of the time, Pallas kernels for 8%

profile of v1, /device:TPU:9, one launch (start us, length us, event | category | flops | bytes accessed | tf_op | source)
XLA Modules:
  0.0 1112.6 jit_solution(11307475484749729183)
XLA Ops:
  3.1 9.6 collective-permute-start.85
  15.0 9.4 collective-permute-start
  95.6 9.2 collective-permute-done.20
  107.5 5.7 collective-permute-done.10
  119.9 12.1 %collective-permute-done.15 = bf16[256,1536]{1,0:T(8,128)(2,1)S(1)} collective-permute-done((bf16[256,1536]{1,0:T(8,128)(2,1)S(1)}, bf16[256,1536]{1,0:T(8,128)(2,1)S(1)}, u32[]{:S(2)}, u32[]{:S(2)}) %collective-permute-start.15) | collective-permute-done | bytes 786464 | tf_op jit(solution)/shard_map/ppermute | solution.py:271
  133.5 8.7 add_convert_fusion.1.packed
  142.3 18.0 %shard_map.529 = bf16[1024,512]{1,0:T(8,128)(2,1)S(1)} custom-call(f32[4,2]{1,0:T(4,128)S(1)} %multiply_power_fusion.slopes, bf16[1024,1536]{1,0:T(8,128)(2,1)S(1)} %add_convert_fusion.1.packed, s32[1024,1]{1,0:T(8,128)S(1)} %copy.87.seg_col, s32[1,1024]{1,0:T(1,128)S(1)} %broadcast_select_fusion.28.seg_row), custom_call_target="tpu_custom_call" | custom-call | flops 6442450944 | bytes 4194304 | tf_op jit(solution)/shard_map/pallas_call | solution.py:143
  192.9 11.0 collective-permute-done.30
  207.1 8.1 collective-permute-done.43
  220.4 8.1 collective-permute-done.39
  235.9 14.9 %collective-permute-done.35 = bf16[256,2048]{1,0:T(8,128)(2,1)S(1)} collective-permute-done((bf16[256,2048]{1,0:T(8,128)(2,1)S(1)}, bf16[256,2048]{1,0:T(8,128)(2,1)S(1)}, u32[]{:S(2)}, u32[]{:S(2)}) %collective-permute-start.35) | collective-permute-done | bytes 1048608 | tf_op jit(solution)/shard_map/ppermute | solution.py:271
  255.4 14.3 %multiply_convert_fusion.1 = (bf16[1024,2048]{1,0:T(8,128)(2,1)}, f32[1024,2048]{1,0:T(8,128)}) fusion(f32[2048]{0:T(1024)S(1)} %bitcast.258, bf16[1024,1024]{0,1:T(8,128)(2,1)S(1)} %add_convert_fusion.5, bf16[256,2048]{1,0:T(8,128)(2,1)} %copy-done.235, bf16[256,1024]{1,0:T(8,128)(2,1)S(1)} %copy-done.110, ...), kind=kOutput, calls=%fused_computation.19 | convolution fusion | flops 4357881856 | bytes 18882560 | tf_op jit(solution)/shard_map/dot_general | solution.py:476
  278.5 13.8 %convolution_convert_fusion.30 = bf16[1024,1024]{0,1:T(8,128)(2,1)S(1)} fusion(bf16[1024,2048]{1,0:T(8,128)(2,1)} %get-tuple-element.252, bf16[2048,256]{1,0:T(8,128)(2,1)} %copy-done.239, bf16[1024,256]{1,0:T(8,128)(2,1)S(1)} %copy-done.116, bf16[1024,128]{1,0:T(8,128)(2,1)S(1)} %collective-permute-done.42, ...), kind=kOutput, calls=%fused_computation.146 | convolution fusion | flops 4337958912 | bytes 10485760 | tf_op jit(solution)/shard_map/dot_general | solution.py:496
  302.2 11.4 %collective-permute-done.70 = bf16[128,512]{1,0:T(8,128)(2,1)S(1)} collective-permute-done((bf16[128,512]{1,0:T(8,128)(2,1)S(1)}, bf16[128,512]{1,0:T(8,128)(2,1)S(1)}, u32[]{:S(2)}, u32[]{:S(2)}) %collective-permute-start.70) | collective-permute-done | bytes 131104 | tf_op jit(solution)/shard_map/ppermute | solution.py:271
  336.0 8.1 collective-permute-done.49
  347.7 13.8 %collective-permute-done.54 = bf16[256,1536]{1,0:T(8,128)(2,1)S(1)} collective-permute-done((bf16[256,1536]{1,0:T(8,128)(2,1)S(1)}, bf16[256,1536]{1,0:T(8,128)(2,1)S(1)}, u32[]{:S(2)}, u32[]{:S(2)}) %collective-permute-start.54) | collective-permute-done | bytes 786464 | tf_op jit(solution)/shard_map/ppermute | solution.py:271
  363.2 8.7 add_convert_fusion.packed
  372.0 18.0 %shard_map.530 = bf16[1024,512]{1,0:T(8,128)(2,1)S(1)} custom-call(f32[4,2]{1,0:T(4,128)S(1)} %multiply_power_fusion.slopes, bf16[1024,1536]{1,0:T(8,128)(2,1)S(1)} %add_convert_fusion.packed, s32[1024,1]{1,0:T(8,128)S(1)} %copy.87.seg_col, s32[1,1024]{1,0:T(1,128)S(1)} %broadcast_select_fusion.28.seg_row), custom_call_target="tpu_custom_call" | custom-call | flops 6442450944 | bytes 4194304 | tf_op jit(solution)/shard_map/pallas_call | solution.py:143
  402.0 10.1 collective-permute-done.77
  424.9 14.3 %multiply_convert_fusion = (bf16[1024,2048]{1,0:T(8,128)(2,1)}, f32[1024,2048]{1,0:T(8,128)}) fusion(f32[2048]{0:T(1024)S(1)} %bitcast.260, bf16[1024,1024]{0,1:T(8,128)(2,1)S(1)} %add_convert_fusion.3, bf16[256,2048]{1,0:T(8,128)(2,1)} %copy-done.243, bf16[256,1024]{1,0:T(8,128)(2,1)S(1)} %copy-done.128, bf16[128,1024]{1,0:T(8,128)(2,1)S(1)} %copy-done.74, ...), kind=kOutput, calls=%fused_computation.18 | convolution fusion | flops 4357881856 | bytes 18882560 | tf_op jit(solution)/shard_map/dot_general | solution.py:476
  439.2 6.6 collective-permute-done.82
  446.4 22.6 %fusion.144 = (f32[2048]{0:T(1024)}, bf16[1024,2048]{1,0:T(8,128)(2,1)S(1)}) fusion(f32[1024,2048]{1,0:T(8,128)} %get-tuple-element.256, f32[2048]{0:T(1024)S(1)} %bitcast.261, bf16[1024,1024]{0,1:T(8,128)(2,1)S(1)} %get-tuple-element.60, bf16[2048,256]{1,0:T(8,128)(2,1)} %collective-permute-done.82, bf16[1024,256]{1,0:T(8,128)(2,1)S(1)} %copy-done.122, ...), kind=kOutput, calls=%fused_computation.646 | convolution fusion | flops 4383045632 | bytes 18890752 | tf_op jit(solution)/shard_map/dot_general | solution.py:23
  478.1 17.6 %convolution_convert_fusion.27 = bf16[1024,1024]{0,1:T(8,128)(2,1)S(1)} fusion(bf16[1024,2048]{1,0:T(8,128)(2,1)S(1)} %get-tuple-element.85, bf16[256,2048]{1,0:T(8,128)(2,1)S(1)} %copy-done.244, bf16[256,1024]{1,0:T(8,128)(2,1)S(1)} %copy-done.128, bf16[128,1024]{1,0:T(8,128)(2,1)S(1)} %copy-done.74, bf16[128,512]{1,0:T(8,128)(2,1)S(1)} %collective-permute-done.70, ...), kind=kOutput, calls=%fused_computation.143 | convolution fusion | flops 4337958912 | bytes 10485760 | tf_op jit(solution)/shard_map/dot_general | solution.py:23
  508.1 11.6 %convolution_convert_fusion.28 = bf16[1024,1024]{0,1:T(8,128)(2,1)S(1)} fusion(bf16[1024,2048]{1,0:T(8,128)(2,1)S(1)} %copy-done.262, bf16[2048,256]{1,0:T(8,128)(2,1)} %collective-permute-done.82, bf16[1024,256]{1,0:T(8,128)(2,1)S(1)} %copy-done.123, bf16[1024,128]{1,0:T(8,128)(2,1)S(1)} %collective-permute-done.80, ...), kind=kOutput, calls=%fused_computation.144 | convolution fusion | flops 4337958912 | bytes 10485760 | tf_op jit(solution)/shard_map/dot_general | solution.py:496
  526.4 19.6 %collective-permute-done.164 = bf16[2048,256]{1,0:T(8,128)(2,1)S(1)} collective-permute-done((bf16[2048,256]{1,0:T(8,128)(2,1)S(1)}, bf16[2048,256]{1,0:T(8,128)(2,1)S(1)}, u32[]{:S(2)}, u32[]{:S(2)}) %collective-permute-start.164) | collective-permute-done | bytes 1048608 | tf_op jit(solution)/shard_map/ppermute | solution.py:271
  549.2 9.5 collective-permute-done.151
  559.5 10.4 collective-permute-done.165
  570.2 10.9 collective-permute-done.169
  591.4 7.8 collective-permute-done.153
  612.3 5.8 fusion.131
  622.4 27.6 %shard_map.531 = (bf16[1024,1536]{1,0:T(8,128)(2,1)S(1)}, f32[4,2,128]{2,1,0:T(2,128)S(1)}) custom-call(f32[4,2]{1,0:T(4,128)S(1)} %multiply_power_fusion.slopes, bf16[1024,1536]{1,0:T(8,128)(2,1)} %copy-done.7, bf16[1024,512]{1,0:T(8,128)(2,1)S(1)} %convolution_convert_fusion.33.upstream, s32[1024,1]{1,0:T(8,128)S(1)} %copy.87.seg_col, ...), custom_call_target="tpu_custom_call" | custom-call | flops 17179869184 | bytes 7340032 | tf_op jit(solution)/shard_map/pallas_call | solution.py:167
  663.8 9.6 collective-permute-start.84
  673.5 12.6 %convolution_convert_fusion.26 = bf16[1024,1024]{0,1:T(8,128)(2,1)S(1)} fusion(bf16[1024,1536]{1,0:T(8,128)(2,1)S(1)} %get-tuple-element.14, bf16[256,1536]{1,0:T(8,128)(2,1)S(1)} %copy-done.250, bf16[256,768]{1,0:T(8,128)(2,1)S(1)} %copy-done.149, bf16[128,768]{1,0:T(8,128)(2,1)S(1)} %copy-done.87, bf16[128,384]{1,0:T(8,128)(2,1)S(1)} %copy-done.80, ...), kind=kOutput, calls=%fused_computation.142 | convolution fusion | flops 3253731328 | bytes 8388608 | tf_op jit(solution)/shard_map/dot_general | solution.py:23
  693.6 17.2 %collective-permute-done.128 = bf16[512,256]{1,0:T(8,128)(2,1)} collective-permute-done((bf16[512,256]{1,0:T(8,128)(2,1)}, bf16[512,256]{1,0:T(8,128)(2,1)}, u32[]{:S(2)}, u32[]{:S(2)}) %collective-permute-start.128) | collective-permute-done | bytes 262176 | tf_op jit(solution)/shard_map/ppermute | solution.py:271
  723.5 6.7 collective-permute-done.130
  748.5 7.6 collective-permute-done.106
  766.2 5.3 collective-permute-start.109
  790.5 19.4 %fusion.143 = (f32[2048]{0:T(1024)S(1)}, bf16[1024,2048]{1,0:T(8,128)(2,1)S(1)}) fusion(f32[1024,2048]{1,0:T(8,128)S(1)} %bitcast.265, f32[2048]{0:T(1024)S(1)} %bitcast.259, bf16[1024,1024]{0,1:T(8,128)(2,1)S(1)} %convert_element_type.1318, bf16[2048,256]{1,0:T(8,128)(2,1)S(1)} %copy-done.240, bf16[1024,256]{1,0:T(8,128)(2,1)S(1)} %copy-done.117, ...), kind=kOutput, calls=%fused_computation.645 | convolution fusion | flops 4383045632 | bytes 18890752 | tf_op jit(solution)/shard_map/dot_general | solution.py:23
  826.4 17.6 %convolution_convert_fusion.25 = bf16[1024,1024]{0,1:T(8,128)(2,1)S(1)} fusion(bf16[1024,2048]{1,0:T(8,128)(2,1)S(1)} %get-tuple-element.83, bf16[256,2048]{1,0:T(8,128)(2,1)S(1)} %copy-done.236, bf16[256,1024]{1,0:T(8,128)(2,1)S(1)} %copy-done.111, bf16[128,1024]{1,0:T(8,128)(2,1)S(1)} %copy-done.66, bf16[128,512]{1,0:T(8,128)(2,1)S(1)} %copy-done.54, ...), kind=kOutput, calls=%fused_computation.141 | convolution fusion | flops 4337958912 | bytes 10485760 | tf_op jit(solution)/shard_map/dot_general | solution.py:23
  852.4 16.4 %collective-permute-done.137 = bf16[256,2048]{1,0:T(8,128)(2,1)} collective-permute-done((bf16[256,2048]{1,0:T(8,128)(2,1)}, bf16[256,2048]{1,0:T(8,128)(2,1)}, u32[]{:S(2)}, u32[]{:S(2)}) %collective-permute-start.137) | collective-permute-done | bytes 1048608 | tf_op jit(solution)/shard_map/ppermute | solution.py:271
  875.1 16.3 %collective-permute-done.155 = bf16[2048,256]{1,0:T(8,128)(2,1)} collective-permute-done((bf16[2048,256]{1,0:T(8,128)(2,1)}, bf16[2048,256]{1,0:T(8,128)(2,1)}, u32[]{:S(2)}, u32[]{:S(2)}) %collective-permute-start.155) | collective-permute-done | bytes 1048608 | tf_op jit(solution)/shard_map/ppermute | solution.py:271
  899.2 7.6 collective-permute-done.156
  907.7 10.4 collective-permute-done.160
  925.6 9.0 collective-permute-done.140
  957.3 27.3 %shard_map.532 = (bf16[1024,1536]{1,0:T(8,128)(2,1)S(1)}, f32[4,2,128]{2,1,0:T(2,128)S(1)}) custom-call(f32[4,2]{1,0:T(4,128)S(1)} %multiply_power_fusion.slopes, bf16[1024,1536]{1,0:T(8,128)(2,1)} %copy-done.6, bf16[1024,512]{1,0:T(8,128)(2,1)S(1)} %convolution_convert_fusion.32.upstream, s32[1024,1]{1,0:T(8,128)S(1)} %copy.87.seg_col, ...), custom_call_target="tpu_custom_call" | custom-call | flops 17179869184 | bytes 7340032 | tf_op jit(solution)/shard_map/pallas_call | solution.py:167
  999.1 8.1 convolution_convert_fusion.24
  1048.5 7.9 collective-permute-done.93
  1057.2 7.6 collective-permute-done.97
  (1213 shorter events, 520.3 us)
Async XLA Ops:
  3.1 86.6 %collective-permute-start.85 = (bf16[512,1024]{0,1:T(8,128)(2,1)}, bf16[512,1024]{0,1:T(8,128)(2,1)}, u32[]{:S(2)}, u32[]{:S(2)}) collective-permute-start(bf16[512,1024]{0,1:T(8,128)(2,1)} %copy.95), channel_id=1, source_target_pairs={{0,0},{1,4},{2,2},{3,6},{4,1},{5,5},{6,3},{7,7},{8,8},{9,12},{10,1... | collective-permute-start | bytes 3145736 | tf_op jit(solution)/shard_map/ppermute | solution.py:279
  15.0 76.6 %collective-permute-start = (bf16[512,1024]{0,1:T(8,128)(2,1)}, bf16[512,1024]{0,1:T(8,128)(2,1)}, u32[]{:S(2)}, u32[]{:S(2)}) collective-permute-start(bf16[512,1024]{0,1:T(8,128)(2,1)} %copy.74), channel_id=1, source_target_pairs={{0,0},{1,4},{2,2},{3,6},{4,1},{5,5},{6,3},{7,7},{8,8},{9,12},{10,1... | collective-permute-start | bytes 3145736 | tf_op jit(solution)/shard_map/ppermute | solution.py:279
  25.1 45.2 %collective-permute-start.7 = (bf16[128,384]{1,0:T(8,128)(2,1)S(1)}, bf16[128,384]{1,0:T(8,128)(2,1)}, u32[]{:S(2)}, u32[]{:S(2)}) collective-permute-start(bf16[128,384]{1,0:T(8,128)(2,1)S(1)} %copy.78), channel_id=1, source_target_pairs={{0,4},{1,5},{2,6},{3,7},{4,0},{5,1},{6,2},{7,3},{8,12},{9,13},{10,... | collective-permute-start | bytes 294920 | tf_op jit(solution)/shard_map/ppermute | solution.py:271
  44.4 30.3 %collective-permute-start.27 = (bf16[128,512]{1,0:T(8,128)(2,1)S(1)}, bf16[128,512]{1,0:T(8,128)(2,1)S(1)}, u32[]{:S(2)}, u32[]{:S(2)}) collective-permute-start(bf16[128,512]{1,0:T(8,128)(2,1)S(1)} %broadcast_select_fusion.13), channel_id=1, source_target_pairs={{0,4},{1,5},{2,6},{3,7},{4,0},{5,1},{6,2},{7,3},{8,12},{9,13},{10,... | collective-permute-start | bytes 393224 | tf_op jit(solution)/shard_map/ppermute | solution.py:271
  104.8 65.4 %collective-permute-start.61 = (bf16[256,128]{1,0:T(8,128)(2,1)S(1)}, bf16[256,128]{1,0:T(8,128)(2,1)S(1)}, u32[]{:S(2)}, u32[]{:S(2)}) collective-permute-start(bf16[256,128]{1,0:T(8,128)(2,1)S(1)} %pad_maximum_fusion.59), channel_id=1, source_target_pairs={{0,16},{1,17},{2,18},{3,19},{4,20},{5,21},{6,22},{7,23},{8,24},{9,... | collective-permute-start | bytes 196616 | tf_op jit(solution)/shard_map/ppermute | solution.py:271
  106.2 75.1 %collective-permute-start.57 = (bf16[256,128]{1,0:T(8,128)(2,1)S(1)}, bf16[256,128]{1,0:T(8,128)(2,1)S(1)}, u32[]{:S(2)}, u32[]{:S(2)}) collective-permute-start(bf16[256,128]{1,0:T(8,128)(2,1)S(1)} %pad_maximum_fusion.58), channel_id=1, source_target_pairs={{0,8},{1,9},{2,10},{3,11},{4,12},{5,13},{6,14},{7,15},{8,0},{9,1},... | collective-permute-start | bytes 196616 | tf_op jit(solution)/shard_map/ppermute | solution.py:271
  113.2 53.4 %collective-permute-start.32 = (bf16[128,512]{1,0:T(8,128)(2,1)S(1)}, bf16[128,512]{1,0:T(8,128)(2,1)S(1)}, u32[]{:S(2)}, u32[]{:S(2)}) collective-permute-start(bf16[128,512]{1,0:T(8,128)(2,1)S(1)} %get-tuple-element.175), channel_id=1, source_target_pairs={{0,2},{1,3},{2,0},{3,1},{4,6},{5,7},{6,4},{7,5},{8,10},{9,11},{10,... | collective-permute-start | bytes 393224 | tf_op jit(solution)/shard_map/ppermute | solution.py:271
  132.0 28.4 %collective-permute-start.25 = (bf16[512,256]{1,0:T(8,128)(2,1)S(1)}, bf16[512,256]{1,0:T(8,128)(2,1)S(1)}, u32[]{:S(2)}, u32[]{:S(2)}) collective-permute-start(bf16[512,256]{1,0:T(8,128)(2,1)S(1)} %pad_maximum_fusion.36), channel_id=1, source_target_pairs={{0,8},{1,9},{2,10},{3,11},{4,12},{5,13},{6,14},{7,15},{8,0},{9,1},... | collective-permute-start | bytes 786440 | tf_op jit(solution)/shard_map/ppermute | solution.py:271
  132.1 30.7 %collective-permute-start.21 = (bf16[512,256]{1,0:T(8,128)(2,1)S(1)}, bf16[512,256]{1,0:T(8,128)(2,1)S(1)}, u32[]{:S(2)}, u32[]{:S(2)}) collective-permute-start(bf16[512,256]{1,0:T(8,128)(2,1)S(1)} %pad_maximum_fusion.35), channel_id=1, source_target_pairs={{0,16},{1,17},{2,18},{3,19},{4,20},{5,21},{6,22},{7,23},{8,24},{9,... | collective-permute-start | bytes 786440 | tf_op jit(solution)/shard_map/ppermute | solution.py:271
  166.6 63.1 %collective-permute-start.26 = (bf16[1024,1024]{0,1:T(8,128)(2,1)S(1)}, bf16[1024,1024]{0,1:T(8,128)(2,1)S(1)}, u32[]{:S(2)}, u32[]{:S(2)}) collective-permute-start(bf16[1024,1024]{0,1:T(8,128)(2,1)S(1)} %convolution_convert_fusion.31), channel_id=1, source_target_pairs={{0,4},{1,5},{2,6},{3,7},{4,0},{5,1},{6,2},{7,3},{8,12},{9,13},{10,... | collective-permute-start | bytes 6291464 | tf_op jit(solution)/shard_map/ppermute | solution.py:271
  185.3 107.0 %collective-permute-start.65 = (bf16[128,512]{1,0:T(8,128)(2,1)}, bf16[128,512]{1,0:T(8,128)(2,1)}, u32[]{:S(2)}, u32[]{:S(2)}) collective-permute-start(bf16[128,512]{1,0:T(8,128)(2,1)} %broadcast_select_fusion.9), channel_id=1, source_target_pairs={{0,4},{1,5},{2,6},{3,7},{4,0},{5,1},{6,2},{7,3},{8,12},{9,13},{10,... | collective-permute-start | bytes 393224 | tf_op jit(solution)/shard_map/ppermute | solution.py:271
  187.1 28.1 %collective-permute-start.43 = (bf16[1024,256]{1,0:T(8,128)(2,1)S(1)}, bf16[1024,256]{1,0:T(8,128)(2,1)S(1)}, u32[]{:S(2)}, u32[]{:S(2)}) collective-permute-start(bf16[1024,256]{1,0:T(8,128)(2,1)S(1)} %pad_maximum_fusion.26), channel_id=1, source_target_pairs={{0,1},{1,0},{2,3},{3,2},{4,5},{5,4},{6,7},{7,6},{8,9},{9,8},{10,11... | collective-permute-start | bytes 1572872 | tf_op jit(solution)/shard_map/ppermute | solution.py:271
  192.6 35.9 %collective-permute-start.39 = (bf16[1024,256]{1,0:T(8,128)(2,1)S(1)}, bf16[1024,256]{1,0:T(8,128)(2,1)S(1)}, u32[]{:S(2)}, u32[]{:S(2)}) collective-permute-start(bf16[1024,256]{1,0:T(8,128)(2,1)S(1)} %pad_maximum_fusion.25), channel_id=1, source_target_pairs={{0,1},{1,0},{2,3},{3,2},{4,5},{5,4},{6,7},{7,6},{8,9},{9,8},{10,11... | collective-permute-start | bytes 1572872 | tf_op jit(solution)/shard_map/ppermute | solution.py:271
  203.9 93.1 %collective-permute-start.51 = (bf16[128,384]{1,0:T(8,128)(2,1)S(1)}, bf16[128,384]{1,0:T(8,128)(2,1)S(1)}, u32[]{:S(2)}, u32[]{:S(2)}) collective-permute-start(bf16[128,384]{1,0:T(8,128)(2,1)S(1)} %get-tuple-element.189), channel_id=1, source_target_pairs={{0,2},{1,3},{2,0},{3,1},{4,6},{5,7},{6,4},{7,5},{8,10},{9,11},{10,... | collective-permute-start | bytes 294920 | tf_op jit(solution)/shard_map/ppermute | solution.py:271
  215.2 84.3 %collective-permute-start.47 = (bf16[128,384]{1,0:T(8,128)(2,1)S(1)}, bf16[128,384]{1,0:T(8,128)(2,1)S(1)}, u32[]{:S(2)}, u32[]{:S(2)}) collective-permute-start(bf16[128,384]{1,0:T(8,128)(2,1)S(1)} %get-tuple-element.188), channel_id=1, source_target_pairs={{0,2},{1,3},{2,0},{3,1},{4,6},{5,7},{6,4},{7,5},{8,10},{9,11},{10,... | collective-permute-start | bytes 294920 | tf_op jit(solution)/shard_map/ppermute | solution.py:271
  272.4 27.2 %collective-permute-start.62 = (bf16[256,256]{1,0:T(8,128)(2,1)S(1)}, bf16[256,256]{1,0:T(8,128)(2,1)S(1)}, u32[]{:S(2)}, u32[]{:S(2)}) collective-permute-start(bf16[256,256]{1,0:T(8,128)(2,1)S(1)} %copy-done.177), channel_id=1, source_target_pairs={{0,1},{1,0},{2,3},{3,2},{4,5},{5,4},{6,7},{7,6},{8,9},{9,8},{10,11... | collective-permute-start | bytes 393224 | tf_op jit(solution)/shard_map/ppermute | solution.py:271
  276.2 25.8 %collective-permute-start.58 = (bf16[256,256]{1,0:T(8,128)(2,1)S(1)}, bf16[256,256]{1,0:T(8,128)(2,1)S(1)}, u32[]{:S(2)}, u32[]{:S(2)}) collective-permute-start(bf16[256,256]{1,0:T(8,128)(2,1)S(1)} %copy-done.178), channel_id=1, source_target_pairs={{0,1},{1,0},{2,3},{3,2},{4,5},{5,4},{6,7},{7,6},{8,9},{9,8},{10,11... | collective-permute-start | bytes 393224 | tf_op jit(solution)/shard_map/ppermute | solution.py:271
  292.3 52.2 %collective-permute-start.45 = (bf16[1024,1024]{0,1:T(8,128)(2,1)S(1)}, bf16[1024,1024]{0,1:T(8,128)(2,1)S(1)}, u32[]{:S(2)}, u32[]{:S(2)}) collective-permute-start(bf16[1024,1024]{0,1:T(8,128)(2,1)S(1)} %convolution_convert_fusion.30), channel_id=1, source_target_pairs={{0,4},{1,5},{2,6},{3,7},{4,0},{5,1},{6,2},{7,3},{8,12},{9,13},{10,... | collective-permute-start | bytes 6291464 | tf_op jit(solution)/shard_map/ppermute | solution.py:271
  327.3 62.7 %collective-permute-start.63 = (bf16[512,256]{1,0:T(8,128)(2,1)S(1)}, bf16[512,256]{1,0:T(8,128)(2,1)S(1)}, u32[]{:S(2)}, u32[]{:S(2)}) collective-permute-start(bf16[512,256]{1,0:T(8,128)(2,1)S(1)} %pad_maximum_fusion.42), channel_id=1, source_target_pairs={{0,8},{1,9},{2,10},{3,11},{4,12},{5,13},{6,14},{7,15},{8,0},{9,1},... | collective-permute-start | bytes 786440 | tf_op jit(solution)/shard_map/ppermute | solution.py:271
  332.1 58.7 %collective-permute-start.59 = (bf16[512,256]{1,0:T(8,128)(2,1)S(1)}, bf16[512,256]{1,0:T(8,128)(2,1)}, u32[]{:S(2)}, u32[]{:S(2)}) collective-permute-start(bf16[512,256]{1,0:T(8,128)(2,1)S(1)} %pad_maximum_fusion.41), channel_id=1, source_target_pairs={{0,16},{1,17},{2,18},{3,19},{4,20},{5,21},{6,22},{7,23},{8,24},{9,... | collective-permute-start | bytes 786440 | tf_op jit(solution)/shard_map/ppermute | solution.py:271
  335.5 61.4 %collective-permute-start.76 = (bf16[1024,128]{1,0:T(8,128)(2,1)}, bf16[1024,128]{1,0:T(8,128)(2,1)}, u32[]{:S(2)}, u32[]{:S(2)}) collective-permute-start(bf16[1024,128]{1,0:T(8,128)(2,1)} %pad_maximum_fusion.45), channel_id=1, source_target_pairs={{0,8},{1,9},{2,10},{3,11},{4,12},{5,13},{6,14},{7,15},{8,0},{9,1},... | collective-permute-start | bytes 786440 | tf_op jit(solution)/shard_map/ppermute | solution.py:271
  361.5 37.1 %collective-permute-start.72 = (bf16[256,1024]{1,0:T(8,128)(2,1)}, bf16[256,1024]{1,0:T(8,128)(2,1)S(1)}, u32[]{:S(2)}, u32[]{:S(2)}) collective-permute-start(bf16[256,1024]{1,0:T(8,128)(2,1)} %pad_maximum_fusion.28), channel_id=1, source_target_pairs={{0,1},{1,0},{2,3},{3,2},{4,5},{5,4},{6,7},{7,6},{8,9},{9,8},{10,11... | collective-permute-start | bytes 1572872 | tf_op jit(solution)/shard_map/ppermute | solution.py:271
  362.3 37.2 %collective-permute-start.68 = (bf16[256,1024]{1,0:T(8,128)(2,1)}, bf16[256,1024]{1,0:T(8,128)(2,1)S(1)}, u32[]{:S(2)}, u32[]{:S(2)}) collective-permute-start(bf16[256,1024]{1,0:T(8,128)(2,1)} %pad_maximum_fusion.27), channel_id=1, source_target_pairs={{0,1},{1,0},{2,3},{3,2},{4,5},{5,4},{6,7},{7,6},{8,9},{9,8},{10,11... | collective-permute-start | bytes 1572872 | tf_op jit(solution)/shard_map/ppermute | solution.py:271
  393.2 27.2 %collective-permute-start.64 = (bf16[1024,1024]{0,1:T(8,128)(2,1)S(1)}, bf16[1024,1024]{0,1:T(8,128)(2,1)S(1)}, u32[]{:S(2)}, u32[]{:S(2)}) collective-permute-start(bf16[1024,1024]{0,1:T(8,128)(2,1)S(1)} %convolution_convert_fusion.29), channel_id=1, source_target_pairs={{0,4},{1,5},{2,6},{3,7},{4,0},{5,1},{6,2},{7,3},{8,12},{9,13},{10,... | collective-permute-start | bytes 6291464 | tf_op jit(solution)/shard_map/ppermute | solution.py:271
  401.7 44.0 %collective-permute-start.82 = (bf16[2048,256]{1,0:T(8,128)(2,1)}, bf16[2048,256]{1,0:T(8,128)(2,1)}, u32[]{:S(2)}, u32[]{:S(2)}) collective-permute-start(bf16[2048,256]{1,0:T(8,128)(2,1)} %pad_maximum_fusion.15), channel_id=1, source_target_pairs={{0,8},{1,9},{2,10},{3,11},{4,12},{5,13},{6,14},{7,15},{8,0},{9,1},... | collective-permute-start | bytes 3145736 | tf_op jit(solution)/shard_map/ppermute | solution.py:271
  414.2 32.2 %collective-permute-start.78 = (bf16[2048,256]{1,0:T(8,128)(2,1)}, bf16[2048,256]{1,0:T(8,128)(2,1)}, u32[]{:S(2)}, u32[]{:S(2)}) collective-permute-start(bf16[2048,256]{1,0:T(8,128)(2,1)} %pad_maximum_fusion.14), channel_id=1, source_target_pairs={{0,16},{1,17},{2,18},{3,19},{4,20},{5,21},{6,22},{7,23},{8,24},{9,... | collective-permute-start | bytes 3145736 | tf_op jit(solution)/shard_map/ppermute | solution.py:271
  495.8 112.2 %collective-permute-start.87 = (bf16[1024,1024]{0,1:T(8,128)(2,1)S(1)}, bf16[1024,1024]{0,1:T(8,128)(2,1)}, u32[]{:S(2)}, u32[]{:S(2)}) collective-permute-start(bf16[1024,1024]{0,1:T(8,128)(2,1)S(1)} %convolution_convert_fusion.27), channel_id=1, source_target_pairs={{0,4},{1,5},{2,6},{3,7},{4,0},{5,1},{6,2},{7,3},{8,12},{9,13},{10,... | collective-permute-start | bytes 6291464 | tf_op jit(solution)/shard_map/ppermute | solution.py:271
  498.7 26.4 %collective-permute-start.150 = (bf16[256,2048]{1,0:T(8,128)(2,1)}, bf16[256,2048]{1,0:T(8,128)(2,1)S(1)}, u32[]{:S(2)}, u32[]{:S(2)}) collective-permute-start(bf16[256,2048]{1,0:T(8,128)(2,1)} %convolution_convert_fusion.8), channel_id=1, source_target_pairs={{0,8},{1,9},{2,10},{3,11},{4,12},{5,13},{6,14},{7,15},{8,0},{9,1},... | collective-permute-start | bytes 3145736 | tf_op jit(solution)/shard_map/ppermute | solution.py:271
  503.4 42.6 %collective-permute-start.164 = (bf16[2048,256]{1,0:T(8,128)(2,1)S(1)}, bf16[2048,256]{1,0:T(8,128)(2,1)S(1)}, u32[]{:S(2)}, u32[]{:S(2)}) collective-permute-start(bf16[2048,256]{1,0:T(8,128)(2,1)S(1)} %convolution_convert_fusion.2), channel_id=1, source_target_pairs={{0,16},{1,17},{2,18},{3,19},{4,20},{5,21},{6,22},{7,23},{8,24},{9,... | collective-permute-start | bytes 3145736 | tf_op jit(solution)/shard_map/ppermute | solution.py:271
  505.8 41.3 %collective-permute-start.168 = (bf16[2048,256]{1,0:T(8,128)(2,1)S(1)}, bf16[2048,256]{1,0:T(8,128)(2,1)S(1)}, u32[]{:S(2)}, u32[]{:S(2)}) collective-permute-start(bf16[2048,256]{1,0:T(8,128)(2,1)S(1)} %convolution_convert_fusion), channel_id=1, source_target_pairs={{0,8},{1,9},{2,10},{3,11},{4,12},{5,13},{6,14},{7,15},{8,0},{9,1},... | collective-permute-start | bytes 3145736 | tf_op jit(solution)/shard_map/ppermute | solution.py:271
  523.6 88.8 %collective-permute-start.83 = (bf16[1024,1024]{0,1:T(8,128)(2,1)S(1)}, bf16[1024,1024]{0,1:T(8,128)(2,1)S(1)}, u32[]{:S(2)}, u32[]{:S(2)}) collective-permute-start(bf16[1024,1024]{0,1:T(8,128)(2,1)S(1)} %convolution_convert_fusion.28), channel_id=1, source_target_pairs={{0,4},{1,5},{2,6},{3,7},{4,0},{5,1},{6,2},{7,3},{8,12},{9,13},{10,... | collective-permute-start | bytes 6291464 | tf_op jit(solution)/shard_map/ppermute | solution.py:271
  548.2 33.0 %collective-permute-start.169 = (bf16[1024,256]{1,0:T(8,128)(2,1)S(1)}, bf16[1024,256]{1,0:T(8,128)(2,1)S(1)}, u32[]{:S(2)}, u32[]{:S(2)}) collective-permute-start(bf16[1024,256]{1,0:T(8,128)(2,1)S(1)} %get-tuple-element.92), channel_id=1, source_target_pairs={{0,1},{1,0},{2,3},{3,2},{4,5},{5,4},{6,7},{7,6},{8,9},{9,8},{10,11... | collective-permute-start | bytes 1572872 | tf_op jit(solution)/shard_map/ppermute | solution.py:271
  599.9 87.6 %collective-permute-start.154 = (bf16[128,512]{1,0:T(8,128)(2,1)}, bf16[128,512]{1,0:T(8,128)(2,1)}, u32[]{:S(2)}, u32[]{:S(2)}) collective-permute-start(bf16[128,512]{1,0:T(8,128)(2,1)} %select_convert_fusion.2), channel_id=1, source_target_pairs={{0,4},{1,5},{2,6},{3,7},{4,0},{5,1},{6,2},{7,3},{8,12},{9,13},{10,... | collective-permute-start | bytes 393224 | tf_op jit(solution)/shard_map/ppermute | solution.py:271
  606.9 82.6 %collective-permute-start.172 = (bf16[512,128]{1,0:T(8,128)(2,1)}, bf16[512,128]{1,0:T(8,128)(2,1)}, u32[]{:S(2)}, u32[]{:S(2)}) collective-permute-start(bf16[512,128]{1,0:T(8,128)(2,1)} %select_convert_fusion), channel_id=1, source_target_pairs={{0,4},{1,5},{2,6},{3,7},{4,0},{5,1},{6,2},{7,3},{8,12},{9,13},{10,... | collective-permute-start | bytes 393224 | tf_op jit(solution)/shard_map/ppermute | solution.py:271
  663.8 108.4 %collective-permute-start.84 = (bf16[512,1024]{0,1:T(8,128)(2,1)}, bf16[512,1024]{0,1:T(8,128)(2,1)}, u32[]{:S(2)}, u32[]{:S(2)}) collective-permute-start(bf16[512,1024]{0,1:T(8,128)(2,1)} %constant_dynamic-slice_fusion.21), channel_id=1, source_target_pairs={{0,0},{1,4},{2,2},{3,6},{4,1},{5,5},{6,3},{7,7},{8,8},{9,12},{10,1... | collective-permute-start | bytes 3145736 | tf_op jit(solution)/shard_map/ppermute | solution.py:279
  686.1 90.6 %collective-permute-start.88 = (bf16[1024,1024]{0,1:T(8,128)(2,1)S(1)}, bf16[1024,1024]{0,1:T(8,128)(2,1)}, u32[]{:S(2)}, u32[]{:S(2)}) collective-permute-start(bf16[1024,1024]{0,1:T(8,128)(2,1)S(1)} %convolution_convert_fusion.26), channel_id=1, source_target_pairs={{0,4},{1,5},{2,6},{3,7},{4,0},{5,1},{6,2},{7,3},{8,12},{9,13},{10,... | collective-permute-start | bytes 6291464 | tf_op jit(solution)/shard_map/ppermute | solution.py:271
  686.1 50.3 %collective-permute-start.101 = (bf16[256,1536]{1,0:T(8,128)(2,1)}, bf16[256,1536]{1,0:T(8,128)(2,1)}, u32[]{:S(2)}, u32[]{:S(2)}) collective-permute-start(bf16[256,1536]{1,0:T(8,128)(2,1)} %convolution_convert_fusion.18), channel_id=1, source_target_pairs={{0,16},{1,17},{2,18},{3,19},{4,20},{5,21},{6,22},{7,23},{8,24},{9,... | collective-permute-start | bytes 2359304 | tf_op jit(solution)/shard_map/ppermute | solution.py:271
  710.8 27.2 %collective-permute-start.105 = (bf16[256,1536]{1,0:T(8,128)(2,1)}, bf16[256,1536]{1,0:T(8,128)(2,1)S(1)}, u32[]{:S(2)}, u32[]{:S(2)}) collective-permute-start(bf16[256,1536]{1,0:T(8,128)(2,1)} %convolution_convert_fusion.16), channel_id=1, source_target_pairs={{0,8},{1,9},{2,10},{3,11},{4,12},{5,13},{6,14},{7,15},{8,0},{9,1},... | collective-permute-start | bytes 2359304 | tf_op jit(solution)/shard_map/ppermute | solution.py:271
  844.0 101.2 %collective-permute-start.89 = (bf16[1024,1024]{0,1:T(8,128)(2,1)S(1)}, bf16[1024,1024]{0,1:T(8,128)(2,1)}, u32[]{:S(2)}, u32[]{:S(2)}) collective-permute-start(bf16[1024,1024]{0,1:T(8,128)(2,1)S(1)} %convolution_convert_fusion.25), channel_id=1, source_target_pairs={{0,4},{1,5},{2,6},{3,7},{4,0},{5,1},{6,2},{7,3},{8,12},{9,13},{10,... | collective-permute-start | bytes 6291464 | tf_op jit(solution)/shard_map/ppermute | solution.py:271
  845.6 27.4 %collective-permute-start.141 = (bf16[256,2048]{1,0:T(8,128)(2,1)}, bf16[256,2048]{1,0:T(8,128)(2,1)}, u32[]{:S(2)}, u32[]{:S(2)}) collective-permute-start(bf16[256,2048]{1,0:T(8,128)(2,1)} %convolution_convert_fusion.12), channel_id=1, source_target_pairs={{0,8},{1,9},{2,10},{3,11},{4,12},{5,13},{6,14},{7,15},{8,0},{9,1},... | collective-permute-start | bytes 3145736 | tf_op jit(solution)/shard_map/ppermute | solution.py:271
  846.2 45.1 %collective-permute-start.155 = (bf16[2048,256]{1,0:T(8,128)(2,1)}, bf16[2048,256]{1,0:T(8,128)(2,1)}, u32[]{:S(2)}, u32[]{:S(2)}) collective-permute-start(bf16[2048,256]{1,0:T(8,128)(2,1)} %convolution_convert_fusion.6), channel_id=1, source_target_pairs={{0,16},{1,17},{2,18},{3,19},{4,20},{5,21},{6,22},{7,23},{8,24},{9,... | collective-permute-start | bytes 3145736 | tf_op jit(solution)/shard_map/ppermute | solution.py:271
  846.4 48.7 %collective-permute-start.159 = (bf16[2048,256]{1,0:T(8,128)(2,1)}, bf16[2048,256]{1,0:T(8,128)(2,1)}, u32[]{:S(2)}, u32[]{:S(2)}) collective-permute-start(bf16[2048,256]{1,0:T(8,128)(2,1)} %convolution_convert_fusion.4), channel_id=1, source_target_pairs={{0,8},{1,9},{2,10},{3,11},{4,12},{5,13},{6,14},{7,15},{8,0},{9,1},... | collective-permute-start | bytes 3145736 | tf_op jit(solution)/shard_map/ppermute | solution.py:271
  870.8 25.9 %collective-permute-start.138 = (bf16[256,1024]{1,0:T(8,128)(2,1)S(1)}, bf16[256,1024]{1,0:T(8,128)(2,1)S(1)}, u32[]{:S(2)}, u32[]{:S(2)}) collective-permute-start(bf16[256,1024]{1,0:T(8,128)(2,1)S(1)} %get-tuple-element.98), channel_id=1, source_target_pairs={{0,1},{1,0},{2,3},{3,2},{4,5},{5,4},{6,7},{7,6},{8,9},{9,8},{10,11... | collective-permute-start | bytes 1572872 | tf_op jit(solution)/shard_map/ppermute | solution.py:271
  938.2 72.5 %collective-permute-start.145 = (bf16[128,512]{1,0:T(8,128)(2,1)}, bf16[128,512]{1,0:T(8,128)(2,1)}, u32[]{:S(2)}, u32[]{:S(2)}) collective-permute-start(bf16[128,512]{1,0:T(8,128)(2,1)} %select_convert_fusion.3), channel_id=1, source_target_pairs={{0,4},{1,5},{2,6},{3,7},{4,0},{5,1},{6,2},{7,3},{8,12},{9,13},{10,... | collective-permute-start | bytes 393224 | tf_op jit(solution)/shard_map/ppermute | solution.py:271
  943.9 69.5 %collective-permute-start.163 = (bf16[512,128]{1,0:T(8,128)(2,1)}, bf16[512,128]{1,0:T(8,128)(2,1)}, u32[]{:S(2)}, u32[]{:S(2)}) collective-permute-start(bf16[512,128]{1,0:T(8,128)(2,1)} %select_convert_fusion.1), channel_id=1, source_target_pairs={{0,4},{1,5},{2,6},{3,7},{4,0},{5,1},{6,2},{7,3},{8,12},{9,13},{10,... | collective-permute-start | bytes 393224 | tf_op jit(solution)/shard_map/ppermute | solution.py:271
  997.0 47.2 %collective-permute-start.92 = (bf16[256,1536]{1,0:T(8,128)(2,1)}, bf16[256,1536]{1,0:T(8,128)(2,1)}, u32[]{:S(2)}, u32[]{:S(2)}) collective-permute-start(bf16[256,1536]{1,0:T(8,128)(2,1)} %convolution_convert_fusion.22), channel_id=1, source_target_pairs={{0,16},{1,17},{2,18},{3,19},{4,20},{5,21},{6,22},{7,23},{8,24},{9,... | collective-permute-start | bytes 2359304 | tf_op jit(solution)/shard_map/ppermute | solution.py:271
  997.1 50.0 %collective-permute-start.96 = (bf16[256,1536]{1,0:T(8,128)(2,1)}, bf16[256,1536]{1,0:T(8,128)(2,1)}, u32[]{:S(2)}, u32[]{:S(2)}) collective-permute-start(bf16[256,1536]{1,0:T(8,128)(2,1)} %convolution_convert_fusion.20), channel_id=1, source_target_pairs={{0,8},{1,9},{2,10},{3,11},{4,12},{5,13},{6,14},{7,15},{8,0},{9,1},... | collective-permute-start | bytes 2359304 | tf_op jit(solution)/shard_map/ppermute | solution.py:271
  1037.9 43.0 %collective-permute-start.90 = (bf16[1024,1024]{0,1:T(8,128)(2,1)}, bf16[1024,1024]{0,1:T(8,128)(2,1)}, u32[]{:S(2)}, u32[]{:S(2)}) collective-permute-start(bf16[1024,1024]{0,1:T(8,128)(2,1)} %convolution_convert_fusion.24), channel_id=1, source_target_pairs={{0,4},{1,5},{2,6},{3,7},{4,0},{5,1},{6,2},{7,3},{8,12},{9,13},{10,... | collective-permute-start | bytes 6291464 | tf_op jit(solution)/shard_map/ppermute | solution.py:271
  (390 other events, 8318.0 us)

commit v2 on v1

v2 whole, which is shorter than its diff:
```python
import functools

import jax
import jax.numpy as jnp
from jax import lax
from jax.experimental import pallas as pl
from jax.experimental.pallas import tpu as pltpu
from jax.sharding import PartitionSpec as P

HEADS = 16
HEAD_DIM = 64
LANES = 128
QBLK = 256

EPSILON = 1e-05
MASKED = -1e30
BOTH = ("dp", "tensor")
F32 = jnp.float32
BF16 = jnp.bfloat16


def dot_nt(left, right):
    return lax.dot_general(left, right, (((1,), (1,)), ((), ())), preferred_element_type=F32)


def dot_nn(left, right):
    return lax.dot_general(left, right, (((1,), (0,)), ((), ())), preferred_element_type=F32)


def dot_tn(left, right):
    return lax.dot_general(left, right, (((0,), (0,)), ((), ())), preferred_element_type=F32)


def fill_places(seg_col, seg_row, places, length):
    for first in range(0, length, QBLK):
        count = first + QBLK
        key_at = lax.broadcasted_iota(jnp.int32, (count, QBLK), 0)
        query_at = first + lax.broadcasted_iota(jnp.int32, (count, QBLK), 1)
        allowed = (key_at <= query_at) & (
            seg_col[0:count, :] == seg_row[:, first : first + QBLK]
        )
        places[0:count, first : first + QBLK] = jnp.where(
            allowed, key_at.astype(F32), MASKED
        )


def head_lanes(values, member):
    lane = lax.broadcasted_iota(jnp.int32, values.shape, 1)
    return jnp.where(lane // HEAD_DIM == member, values, jnp.zeros_like(values))


def forward_kernel(slopes, query_in, key_in, value_in, seg_col, seg_row, mixed, places):
    group = pl.program_id(0)
    length = query_in.shape[0]

    @pl.when(group == 0)
    def _():
        fill_places(seg_col, seg_row, places, length)

    scale = HEAD_DIM**-0.5
    values_t = value_in[...].astype(F32).T.astype(BF16)
    keys = [
        head_lanes(key_in[...].astype(F32), member).astype(BF16)
        for member in range(2)
    ]
    for first in range(0, length, QBLK):
        count = first + QBLK
        queries = (query_in[first:count, :].astype(F32) * scale).astype(BF16)
        parts = []
        for member in range(2):
            slope = slopes[group, member]
            scores = dot_nt(keys[member][0:count, :], queries)
            scores = scores + slope * places[0:count, first:count]
            top = jnp.max(scores, axis=0, keepdims=True)
            lifted = jnp.exp(scores - top)
            total = jnp.sum(lifted, axis=0, keepdims=True)
            rows = values_t[member * HEAD_DIM : (member + 1) * HEAD_DIM, 0:count]
            parts.append(dot_nn(rows, lifted.astype(BF16)) / total)
        mixed[first:count, :] = jnp.concatenate(parts, axis=0).T.astype(BF16)


def backward_kernel(
    slopes,
    query_in,
    key_in,
    value_in,
    upstream,
    seg_col,
    seg_row,
    packed_grad,
    sums,
    places,
    key_grad,
    value_grad,
):
    group = pl.program_id(0)
    length = query_in.shape[0]

    @pl.when(group == 0)
    def _():
        fill_places(seg_col, seg_row, places, length)

    scale = HEAD_DIM**-0.5
    keys_f32 = key_in[...].astype(F32)
    values_f32 = value_in[...].astype(F32)
    keys = [head_lanes(keys_f32, member).astype(BF16) for member in range(2)]
    value_rows = [head_lanes(values_f32, member).astype(BF16) for member in range(2)]
    keys_t = (keys_f32 * scale).T.astype(BF16)
    query_sum = jnp.zeros((1, LANES), F32)
    for first in reversed(range(0, length, QBLK)):
        count = first + QBLK
        queries_f32 = query_in[first:count, :].astype(F32) * scale
        queries = queries_f32.astype(BF16)
        above_f32 = upstream[first:count, :].astype(F32)
        above = above_f32.astype(BF16)
        parts = []
        key_part = None
        value_part = None
        for member in range(2):
            slope = slopes[group, member]
            scores = dot_nt(keys[member][0:count, :], queries)
            scores = scores + slope * places[0:count, first:count]
            top = jnp.max(scores, axis=0, keepdims=True)
            lifted = jnp.exp(scores - top)
            total = jnp.sum(lifted, axis=0, keepdims=True)
            chances = lifted * (1.0 / total)
            chance_grad = dot_nt(value_rows[member][0:count, :], above)
            inner = jnp.sum(chance_grad * chances, axis=0, keepdims=True)
            score_grad = (chances * (chance_grad - inner)).astype(BF16)
            rows = keys_t[member * HEAD_DIM : (member + 1) * HEAD_DIM, 0:count]
            parts.append(dot_nn(rows, score_grad))
            key_term = dot_nn(score_grad, head_lanes(queries_f32, member).astype(BF16))
            value_term = dot_nn(chances.astype(BF16), head_lanes(above_f32, member).astype(BF16))
            key_part = key_term if member == 0 else key_part + key_term
            value_part = value_term if member == 0 else value_part + value_term
        query_grad = jnp.concatenate(parts, axis=0).T
        query_sum = query_sum + jnp.sum(query_grad, axis=0, keepdims=True)
        packed_grad[0, first:count, :] = query_grad.astype(BF16)
        if count == length:
            key_grad[...] = key_part
            value_grad[...] = value_part
        else:
            key_grad[0:count, :] += key_part
            value_grad[0:count, :] += value_part
    packed_grad[1] = key_grad[...].astype(BF16)
    packed_grad[2] = value_grad[...].astype(BF16)
    sums[0:1, :] = query_sum
    sums[1:2, :] = jnp.sum(value_grad[...], axis=0, keepdims=True)


def column_blocks(packed, length, groups):
    if len(packed) == 1:
        packed = packed * 3
        starts = (0, groups, 2 * groups)
    else:
        starts = (0, 0, 0)
    specs = [
        pl.BlockSpec((length, LANES), functools.partial(lambda start, g: (0, start + g), start))
        for start in starts
    ]
    return packed, specs


def attention_forward(packed, seg_col, seg_row, slopes):
    length = packed[0].shape[0]
    width = sum(array.shape[1] for array in packed) // 3
    groups = width // LANES
    packed, specs = column_blocks(packed, length, groups)
    block = pl.BlockSpec((length, LANES), lambda g: (0, g))
    return pl.pallas_call(
        forward_kernel,
        grid=(groups,),
        in_specs=[
            pl.BlockSpec(memory_space=pltpu.SMEM),
            *specs,
            pl.BlockSpec((length, 1), lambda g: (0, 0)),
            pl.BlockSpec((1, length), lambda g: (0, 0)),
        ],
        out_specs=block,
        out_shape=jax.ShapeDtypeStruct((length, width), BF16),
        scratch_shapes=[pltpu.VMEM((length, length), F32)],
        compiler_params=pltpu.CompilerParams(vmem_limit_bytes=40 * 2**20),
        cost_estimate=pl.CostEstimate(
            flops=groups * 2 * length * length * 256 * 5,
            bytes_accessed=groups * length * LANES * 8,
            transcendentals=groups * length * length * 2,
        ),
    )(slopes, *packed, seg_col, seg_row)


def attention_backward(packed, upstream, seg_col, seg_row, slopes):
    length, width = upstream.shape
    groups = width // LANES
    packed, specs = column_blocks(packed, length, groups)
    block = pl.BlockSpec((length, LANES), lambda g: (0, g))
    return pl.pallas_call(
        backward_kernel,
        grid=(groups,),
        in_specs=[
            pl.BlockSpec(memory_space=pltpu.SMEM),
            *specs,
            block,
            pl.BlockSpec((length, 1), lambda g: (0, 0)),
            pl.BlockSpec((1, length), lambda g: (0, 0)),
        ],
        out_specs=[
            pl.BlockSpec((3, length, LANES), lambda g: (0, 0, g)),
            pl.BlockSpec((None, 2, LANES), lambda g: (g, 0, 0)),
        ],
        out_shape=[
            jax.ShapeDtypeStruct((3, length, width), BF16),
            jax.ShapeDtypeStruct((groups, 2, LANES), F32),
        ],
        scratch_shapes=[
            pltpu.VMEM((length, length), F32),
            pltpu.VMEM((length, LANES), F32),
            pltpu.VMEM((length, LANES), F32),
        ],
        compiler_params=pltpu.CompilerParams(vmem_limit_bytes=48 * 2**20),
        cost_estimate=pl.CostEstimate(
            flops=groups * 2 * length * length * 256 * 8,
            bytes_accessed=groups * length * LANES * 14,
            transcendentals=groups * length * length * 2,
        ),
    )(slopes, *packed, upstream, seg_col, seg_row)


def merge_kernel(size, count, axis, first, second, joined, done):
    copies = []
    for at in range(count):
        for which, source in enumerate((first, second)):
            near = [slice(None), slice(None)]
            far = [slice(None), slice(None)]
            near[axis] = pl.ds(at * size, size)
            far[axis] = pl.ds((2 * at + which) * size, size)
            copies.append(
                pltpu.make_async_copy(
                    source.at[tuple(near)], joined.at[tuple(far)], done.at[2 * at + which]
                )
            )
    for copy in copies:
        copy.start()
    for copy in copies:
        copy.wait()


def merge(first, second, size, count, axis):
    shape = list(first.shape)
    shape[axis] *= 2
    grain = LANES if axis == 1 else 16
    if first.size < 2**20 or size % grain or shape[1] % LANES or shape[0] % 16:
        parts = []
        for at in range(count):
            for values in (first, second):
                parts.append(lax.slice_in_dim(values, at * size, (at + 1) * size, axis=axis))
        return jnp.concatenate(parts, axis=axis)
    anywhere = pl.BlockSpec(memory_space=pl.ANY)
    return pl.pallas_call(
        functools.partial(merge_kernel, size, count, axis),
        in_specs=[anywhere, anywhere],
        out_specs=anywhere,
        out_shape=jax.ShapeDtypeStruct(tuple(shape), first.dtype),
        scratch_shapes=[pltpu.SemaphoreType.DMA((2 * count,))],
        cost_estimate=pl.CostEstimate(
            flops=0, bytes_accessed=8 * first.size, transcendentals=0
        ),
    )(first, second)


def normalise(values):
    centred = values - jnp.mean(values, axis=-1, keepdims=True)
    spread = jnp.mean(centred * centred, axis=-1, keepdims=True)
    inverse = lax.rsqrt(spread + EPSILON)
    return centred * inverse, inverse


def layer_norm(values, gain_row, shift_row):
    return normalise(values)[0] * gain_row + shift_row


def norm_back(values, gain_row, upstream):
    unit, inverse = normalise(values)
    gain_grad = jnp.sum(upstream * unit, axis=0)
    shift_grad = jnp.sum(upstream, axis=0)
    inner = upstream * gain_row
    result = inverse * (
        inner
        - jnp.mean(inner, axis=-1, keepdims=True)
        - unit * jnp.mean(inner * unit, axis=-1, keepdims=True)
    )
    return result, gain_grad, shift_grad


def gelu_tanh(values):
    return jax.nn.gelu(values, approximate=True)


def bits_of(count):
    return [1 << place for place in range(count.bit_length() - 1)]


def body(
    dp_size,
    tensor_size,
    tokens_in,
    segment_ids,
    qkv_weight,
    qv_bias,
    out_weight,
    up_weight,
    up_bias,
    down_weight,
    row_params,
    cotangent,
):
    layers = qkv_weight.shape[0]
    shard_rows, features = tokens_in.shape
    spans = 2 * segment_ids.shape[0]
    inner_size = tensor_size // spans
    pairs = dp_size // 2
    devices = dp_size * tensor_size
    heads_half = HEADS // tensor_size // 2
    half_width = heads_half * HEAD_DIM

    dp_at = lax.axis_index("dp")
    tensor_at = lax.axis_index("tensor")
    core = dp_at % 2
    pair = dp_at // 2
    span = tensor_at // inner_size
    inner = tensor_at % inner_size
    core_one = core == 1

    core_mask = tensor_size
    inner_masks = bits_of(inner_size)
    span_bits = bits_of(spans)
    pair_bits = bits_of(pairs)
    span_masks = {bit: bit * inner_size for bit in span_bits}
    pair_masks = {bit: bit * 2 * tensor_size for bit in pair_bits}

    def swap(values, mask):
        return lax.ppermute(values, BOTH, [(at, at ^ mask) for at in range(devices)])

    def crossed(at):
        at_core = (at // tensor_size) % 2
        at_span = (at % tensor_size) // inner_size
        return at if at_core == at_span % 2 else at ^ (core_mask | inner_size)

    def cross(values):
        return lax.ppermute(values, BOTH, [(at, crossed(at)) for at in range(devices)])

    def ordered(values, mask, is_high, axis):
        other = swap(values, mask)
        return jnp.concatenate(
            [jnp.where(is_high, other, values), jnp.where(is_high, values, other)], axis=axis
        )

    def group_rows(values):
        for mask in inner_masks:
            values = ordered(values, mask, (inner & mask) != 0, 0)
        return ordered(values, core_mask, core_one, 0)

    def group_sum(values):
        for mask in inner_masks + [core_mask]:
            low = values.astype(BF16)
            values = low.astype(F32) + swap(low, mask).astype(F32)
        return values

    high_spans = [("span", bit) for bit in reversed(span_bits[1:])]
    turning = [("pair", bit) for bit in pair_bits]
    turning = turning[:1] + [("span", bit) for bit in span_bits[:1]] + turning[1:]
    orders = [high_spans + turning[by:] + turning[:by] for by in range(3)]

    def mask_of(kind, bit):
        return span_masks[bit] if kind == "span" else pair_masks[bit]

    def interleave(kind, bit, present, width, outer=1):
        lower = sum(1 for at_kind, at in present if at_kind == kind and at < bit)
        upper = sum(1 for at_kind, at in present if at_kind == kind and at > bit)
        return width << lower, (outer if kind == "span" else 1) << upper

    def halves_of(values, kind, bit, present, width, axis, outer):
        size, count = interleave(kind, bit, present, width, outer)
        halves = []
        for which in range(2):
            parts = [
                lax.slice_in_dim(
                    values, (2 * at + which) * size, (2 * at + which + 1) * size, axis=axis
                )
                for at in range(count)
            ]
            halves.append(parts[0] if count == 1 else jnp.concatenate(parts, axis=axis))
        return halves

    class Fetch:
        def __init__(self, block, feature_axis, order, outer=1):
            self.block = block
            self.outer = outer
            self.feature_axis = feature_axis
            self.order = orders[order]
            self.widths = {
                "pair": block.shape[feature_axis],
                "span": block.shape[1 - feature_axis] // outer,
            }
            self.place = 0

        def send(self):
            self.other = swap(self.block, mask_of(*self.order[self.place]))

        def take(self):
            kind, bit = self.order[self.place]
            axis = self.feature_axis if kind == "pair" else 1 - self.feature_axis
            present = self.order[: self.place]
            size, count = interleave(kind, bit, present, self.widths[kind], self.outer)
            self.block = merge(self.block, self.other, size, count, axis)
            self.place += 1
            if self.place < len(self.order):
                self.send()

    class Reduce:
        def __init__(self, feature_side, unit_side, feature_axis, order, outer=1):
            self.feature_axis = feature_axis
            self.outer = outer
            self.order = list(reversed(orders[order]))
            self.widths = {
                "pair": feature_side.shape[1] // pairs,
                "span": unit_side.shape[1] // spans // outer,
            }
            kind, bit = self.order[0]
            sides = {"pair": feature_side, "span": unit_side}
            found = []
            for part in halves_of(
                sides[kind], kind, bit, self.order[1:], self.widths[kind], 1, outer
            ):
                sides[kind] = part
                pair_of = [sides["pair"], sides["span"]]
                if feature_axis == 1:
                    pair_of.reverse()
                found.append(dot_tn(*pair_of).astype(BF16))
            self.keep, send = found
            self.other = swap(send, mask_of(kind, bit))
            self.place = 1

        def take(self):
            ours = self.keep
            theirs = self.other
            if self.place == len(self.order):
                self.result = ours.astype(F32) + theirs.astype(F32)
                self.place += 1
                return
            kind, bit = self.order[self.place]
            axis = self.feature_axis if kind == "pair" else 1 - self.feature_axis
            rest = self.order[self.place + 1 :]
            width = self.widths[kind]
            sums = [
                (first.astype(F32) + second.astype(F32)).astype(BF16)
                for first, second in zip(
                    halves_of(ours, kind, bit, rest, width, axis, self.outer),
                    halves_of(theirs, kind, bit, rest, width, axis, self.outer),
                )
            ]
            self.keep = sums[0]
            self.other = swap(sums[1], mask_of(kind, bit))
            self.place += 1

    def advance(values, chains):
        return tick(values, [chain for chain in chains if chain.place <= steps])

    def tick(values, chains):
        if not chains:
            return values
        values, others = lax.optimization_barrier((values, [chain.other for chain in chains]))
        for chain, other in zip(chains, others):
            chain.other = other
            chain.take()
        return values

    def to_local(values):
        axis = values.ndim - 1
        wide = features // pairs
        return jnp.concatenate(
            [
                lax.dynamic_slice_in_dim(values, (pair ^ offset) * wide, wide, axis)
                for offset in range(pairs)
            ],
            axis=axis,
        )

    from_local = to_local

    def split_cores(low, high, axis):
        mine = jnp.where(core_one, high, low)
        other = swap(jnp.where(core_one, low, high), core_mask)
        return jnp.concatenate(
            [jnp.where(core_one, other, mine), jnp.where(core_one, mine, other)], axis=axis
        )

    def blocks_of(number, which):
        if which == 0:
            local = qkv_weight[number].transpose(1, 0, 2)
            rows = local.shape[0]
            low = local[:, :, :half_width].reshape(rows, 3 * half_width)
            high = local[:, :, half_width:].reshape(rows, 3 * half_width)
            qkv = split_cores(low, high, 0)
            if number:
                found = [(qkv, 0, 2, 3)]
            else:
                found = [
                    (qkv[:, at * half_width : (at + 1) * half_width], 0, at, 1) for at in range(3)
                ]
            half = out_weight.shape[1] // 2
            out = split_cores(out_weight[number, :half], out_weight[number, half:], 1)
            return found + [(out, 1, 2, 1)]
        half = up_weight.shape[2] // 2
        up = split_cores(up_weight[number, :, :half], up_weight[number, :, half:], 0)
        half = down_weight.shape[1] // 2
        down = split_cores(down_weight[number, :half], down_weight[number, half:], 1)
        return [(up, 0, 0, 1), (down, 1, 1, 1)]

    def join_cores(values, feature_axis):
        size = values.shape[feature_axis] // 2
        first = lax.slice_in_dim(values, 0, size, axis=feature_axis)
        second = lax.slice_in_dim(values, size, 2 * size, axis=feature_axis)
        mine = jnp.where(core_one, second, first)
        other = swap(jnp.where(core_one, first, second).astype(BF16), core_mask).astype(F32)
        return jnp.where(core_one, other, mine), jnp.where(core_one, mine, other)

    first_blocks, first_rests = zip(*[(found[0], found[1:]) for found in blocks_of(0, 0)])
    (
        first_blocks,
        tokens_in,
        segment_ids,
        qkv_weight,
        qv_bias,
        out_weight,
        up_weight,
        up_bias,
        down_weight,
        row_params,
    ) = lax.optimization_barrier(
        (
            first_blocks,
            tokens_in,
            segment_ids,
            qkv_weight,
            qv_bias,
            out_weight,
            up_weight,
            up_bias,
            down_weight,
            row_params,
        )
    )

    small_local = jnp.concatenate(
        [row_params.reshape(-1), qv_bias.reshape(-1), up_bias.reshape(-1)]
    )[None]
    small = small_local
    for mask in bits_of(devices):
        small = ordered(small, mask, (dp_at * tensor_size + tensor_at) & mask != 0, 0)
    row_size, qv_size = row_params.size, qv_bias.size
    rows_every = to_local(
        small[:, :row_size]
        .reshape(devices, layers, 6, -1)
        .transpose(1, 2, 0, 3)
        .reshape(layers, 6, features)
        .astype(F32)
    )

    def local_units(values, kinds):
        values = values.reshape(dp_size, spans, inner_size, layers, kinds, -1)
        values = lax.dynamic_slice_in_dim(values, core * pairs, pairs, 0)
        values = lax.dynamic_slice_in_dim(values, inner, 1, 2)[:, :, 0]
        blocks = [
            lax.dynamic_slice_in_dim(values, span ^ offset, 1, 1)[:, 0] for offset in range(spans)
        ]
        values = jnp.stack(blocks)
        return values.transpose(2, 3, 0, 1, 4).reshape(layers, kinds, -1).astype(F32)

    qv_local = local_units(small[:, row_size : row_size + qv_size], 2)
    up_bias_local = local_units(small[:, row_size + qv_size :], 1)[:, 0]

    span_at = jnp.stack([span ^ offset for offset in range(spans)])
    heads_at = (span_at * inner_size + inner)[:, None] * (2 * heads_half) + core * heads_half
    heads_at = heads_at + jnp.arange(heads_half, dtype=jnp.int32)[None]
    slopes = (2.0 ** (-8.0 * (heads_at.astype(F32) + 1.0) / HEADS)).reshape(-1, 2)

    own_segment = lax.dynamic_slice_in_dim(segment_ids, span // 2, 1, 0)
    seg_row = jnp.where(core == span % 2, own_segment, swap(own_segment, core_mask))
    seg_col = seg_row.reshape(-1, 1)

    steps = len(orders[0])

    def fetches_of(blocks):
        return [Fetch(block, axis, order, outer) for block, axis, order, outer in blocks]

    stages = [fetches_of([(block, *rest) for block, rest in zip(first_blocks, first_rests)])]
    for chain in stages[0]:
        chain.send()
    fetches = [stages[0]]
    for number in range(layers):
        late = fetches_of(blocks_of(number, 1))
        fetches[number] = fetches[number] + late
        if number + 1 < layers:
            fetches.append(fetches_of(blocks_of(number + 1, 0)))
            late = late + fetches[number + 1]
        stages.append(late)
    for chain in stages[0]:
        chain.take()
    for before, after in zip(stages[:-1], stages[1:]):
        held = lax.optimization_barrier(
            ([chain.other for chain in before], [chain.block for chain in after])
        )
        for chain, other in zip(before, held[0]):
            chain.other = other
        for chain, block in zip(after, held[1]):
            chain.block = block
            chain.send()
    while stages[0][0].place < steps:
        for chain in stages[0]:
            chain.take()

    stream = to_local(group_rows(cross(tokens_in))).astype(F32)

    stash = []
    normed = layer_norm(stream, rows_every[0, 0], rows_every[0, 1]).astype(BF16)
    for number in range(layers):
        rows = rows_every[number]
        stage = stages[number + 1]
        weights = [chain.block for chain in fetches[number]]
        weights = weights[: len(weights) - 2] + [None, None]
        biases = (qv_local[number, 0], jnp.zeros_like(qv_local[number, 0]), qv_local[number, 1])
        if number:
            biases = (jnp.concatenate(biases),)
        packed = [
            (jnp.dot(normed, weight, preferred_element_type=F32) + bias).astype(BF16)
            for weight, bias in zip(weights[:-3], biases)
        ]
        if number == 0:
            packed = tick(packed, stage)
            packed, cotangent = lax.optimization_barrier((packed, cotangent))
            upstream_low = to_local(group_rows(cross(cotangent)))
        attended = attention_forward(packed, seg_col, seg_row, slopes)
        if number == 0:
            attended = tick(attended, stage)
        middle = stream + (
            group_sum(jnp.dot(attended, weights[-3], preferred_element_type=F32)) + rows[2]
        )
        normed_two = layer_norm(middle, rows[3], rows[4]).astype(BF16)
        while stage[0].place + 1 < steps:
            normed_two = tick(normed_two, stage)
        following = stages[number + 2] if number + 2 < len(stages) else []
        if following:
            normed_two = tick(normed_two, stage)
            weights_two, others = lax.optimization_barrier(
                ([chain.block for chain in stage], [chain.other for chain in following])
            )
            for chain, block in zip(stage, weights_two):
                chain.block = block
            for chain, other in zip(following, others):
                chain.other = other
                chain.take()
        else:
            for chain in stage:
                chain.take()
        weights = [chain.block for chain in fetches[number]]
        pre_gelu = (
            jnp.dot(normed_two, weights[-2], preferred_element_type=F32) + up_bias_local[number]
        )
        hidden = gelu_tanh(pre_gelu).astype(BF16)
        if following:
            hidden = tick(hidden, following)
        stash.append(
            (stream, normed, packed, attended, middle, normed_two, pre_gelu, hidden, weights)
        )
        stream = middle + (
            group_sum(jnp.dot(hidden, weights[-1], preferred_element_type=F32)) + rows[5]
        )
        if number + 1 < layers:
            after = rows_every[number + 1]
            normed = layer_norm(stream, after[0], after[1]).astype(BF16)
            if following[0].place + 1 < steps:
                normed = tick(normed, following)

    def give_back(values):
        at = (core * inner_size + inner) * shard_rows
        return cross(lax.dynamic_slice_in_dim(from_local(values), at, shard_rows, 0))

    output = give_back(stream.astype(BF16))

    upstream = upstream_low.astype(F32)
    reductions = [None] * layers
    small_grads = [None] * layers
    running = []
    for number in reversed(range(layers)):
        (
            stream_in,
            normed,
            packed,
            attended,
            middle,
            normed_two,
            pre_gelu,
            hidden,
            weights,
        ) = stash[number]
        rows = rows_every[number]
        apart = len(packed) == 3

        down_bias_grad = jnp.sum(upstream, axis=0)
        down_in = upstream.astype(BF16)
        down_chain = Reduce(down_in, hidden, 1, 1)
        hidden_grad = dot_nt(down_in, weights[-1])
        pre_grad = jax.vjp(gelu_tanh, pre_gelu)[1](hidden_grad)[0]
        up_bias_grad = jnp.sum(pre_grad, axis=0)
        pre_low = pre_grad.astype(BF16)
        pre_low = advance(pre_low, running)
        up_chain = Reduce(normed_two, pre_low, 0, 0)
        normed_two_grad = group_sum(dot_nt(pre_low, weights[-2]))
        normed_two_grad = advance(normed_two_grad, running)
        middle_grad, gain_two_grad, shift_two_grad = norm_back(middle, rows[3], normed_two_grad)
        middle_grad = middle_grad + upstream
        out_bias_grad = jnp.sum(middle_grad, axis=0)
        out_in = middle_grad.astype(BF16)
        attended_grad = dot_nt(out_in, weights[-3]).astype(BF16)
        attended_grad = advance(attended_grad, running + [down_chain])
        out_chain = Reduce(out_in, attended, 1, 2)
        packed_grad, qv_sums = attention_backward(packed, attended_grad, seg_col, seg_row, slopes)
        packed_grad = advance(packed_grad, running + [down_chain, up_chain, out_chain])
        if apart:
            qkv_chains = [Reduce(normed, packed_grad[at], 0, at) for at in range(3)]
            normed_grad = (
                dot_nt(packed_grad[0], weights[0])
                + dot_nt(packed_grad[1], weights[1])
                + dot_nt(packed_grad[2], weights[2])
            )
        else:
            beside = jnp.concatenate([packed_grad[at] for at in range(3)], axis=1)
            qkv_chains = [Reduce(normed, beside, 0, 2, 3)]
            normed_grad = dot_nt(beside, weights[0])
        normed_grad = group_sum(normed_grad)
        stream_grad, gain_one_grad, shift_one_grad = norm_back(stream_in, rows[0], normed_grad)
        upstream = middle_grad + stream_grad
        if number:
            upstream = advance(upstream, running + [down_chain, up_chain, out_chain])
        running = running + [down_chain, up_chain, out_chain] + qkv_chains
        reductions[number] = qkv_chains + [out_chain, up_chain, down_chain]

        row_grads = from_local(
            jnp.stack(
                [
                    gain_one_grad,
                    shift_one_grad,
                    out_bias_grad,
                    gain_two_grad,
                    shift_two_grad,
                    down_bias_grad,
                ]
            )
        )
        qv_units = qv_sums.transpose(1, 0, 2).reshape(2, spans, half_width)
        units = jnp.concatenate(
            [qv_units.transpose(1, 0, 2).reshape(spans, -1), up_bias_grad.reshape(spans, -1)],
            axis=1,
        )
        units = jnp.concatenate(
            [
                lax.dynamic_slice_in_dim(units, span ^ true_span, 1, 0)
                for true_span in range(spans)
            ],
            axis=0,
        )
        small_grads[number] = jnp.concatenate([row_grads.reshape(-1), units.reshape(-1)])
    def own_grads(number):
        found = [chain.result for chain in reductions[number]]
        low, high = join_cores(jnp.concatenate(found[:-3], axis=1), 0)
        row_count = low.shape[0]
        qkv_own = jnp.concatenate(
            [low.reshape(row_count, 3, half_width), high.reshape(row_count, 3, half_width)], axis=2
        ).transpose(1, 0, 2)
        return (
            qkv_own,
            jnp.concatenate(join_cores(found[-3], 1), axis=0),
            jnp.concatenate(join_cores(found[-2], 0), axis=1),
            jnp.concatenate(join_cores(found[-1], 1), axis=0),
        )

    weight_grads = [
        own_grads(number) if all(chain.place > steps for chain in reductions[number]) else None
        for number in range(layers)
    ]
    summed = jnp.stack(small_grads)
    upstream, summed, weight_grads = lax.optimization_barrier((upstream, summed, weight_grads))
    grad_input = give_back(upstream.astype(BF16))
    small_masks = [span_masks[bit] for bit in span_bits] + [pair_masks[bit] for bit in pair_bits]
    running = [chain for chain in running if chain.place <= steps]
    while running or small_masks:
        if small_masks:
            passed = swap(summed, small_masks[0])
        passed = advance(passed, running)
        if small_masks:
            summed = summed + passed
            small_masks = small_masks[1:]
        running = [chain for chain in running if chain.place <= steps]
    weight_grads = [
        own_grads(number) if weight_grads[number] is None else weight_grads[number]
        for number in range(layers)
    ]

    row_total = 6 * features
    own = features // devices
    row_summed = lax.dynamic_slice_in_dim(
        summed[:, :row_total].reshape(layers, 6, features),
        (dp_at * tensor_size + tensor_at) * own,
        own,
        2,
    )
    units = summed[:, row_total:].reshape(layers, spans, -1)
    units = lax.dynamic_slice_in_dim(units, span, 1, 1)[:, 0]
    other_units = swap(units, core_mask)
    units = jnp.where(core_one == (dp_at >= pairs), units, other_units)
    place = dp_at % pairs
    qv_part = units[:, : 2 * half_width].reshape(layers, 2, pairs, -1)
    up_part = units[:, 2 * half_width :].reshape(layers, pairs, -1)
    qv_own = lax.dynamic_slice_in_dim(qv_part, place, 1, 2)[:, :, 0]
    up_own = lax.dynamic_slice_in_dim(up_part, place, 1, 1)[:, 0]

    joined = [
        jnp.stack([weight_grads[number][member] for number in range(layers)]) for member in range(4)
    ]
    return (
        output,
        grad_input.astype(F32),
        joined[0],
        qv_own,
        joined[1],
        joined[2],
        up_own,
        joined[3],
        row_summed,
    )


def solution(mesh):
    placed = (
        P(("dp", "tensor"), None),
        P("dp", None),
        P(None, None, "dp", "tensor"),
        P(None, None, ("tensor", "dp")),
        P(None, "tensor", "dp"),
        P(None, "dp", "tensor"),
        P(None, ("tensor", "dp")),
        P(None, "tensor", "dp"),
        P(None, None, ("dp", "tensor")),
        P(("dp", "tensor"), None),
    )
    return jax.shard_map(
        functools.partial(body, mesh.shape["dp"], mesh.shape["tensor"]),
        mesh=mesh,
        in_specs=placed,
        out_specs=(
            P(("dp", "tensor"), None),
            P(("dp", "tensor"), None),
            P(None, None, "dp", "tensor"),
            P(None, None, ("tensor", "dp")),
            P(None, "tensor", "dp"),
            P(None, "dp", "tensor"),
            P(None, ("tensor", "dp")),
            P(None, "tensor", "dp"),
            P(None, None, ("dp", "tensor")),
        ),
        check_vma=False,
    )
```

time: 1130 us -> 1400 us (1.24)
  Pallas kernels: 90.9 us -> 604 us
  waiting for transfers between devices: 388 us -> 250 us
  matrix products: 242 us -> 141 us
  starting transfers between devices: 236 us -> 165 us
  local copies, waits for them, and re-layouts: 40.1 us -> 85.6 us
  other arithmetic: 107 us -> 137 us
    pallas_call x0 -> x4, Pallas kernels: none -> 513 us  [merge(): pl.pallas_call(functools.partial(merge_kernel, size, count, axis), in_spe...]
    ppermute x169 -> x117, waiting for transfers between devices: 388 us -> 250 us  [swap(): lax.ppermute(values, BOTH, [(at, at ^ mask) for at in range(devices)])]
    ppermute x169 -> x117, starting transfers between devices: 207 us -> 134 us  [swap(): lax.ppermute(values, BOTH, [(at, at ^ mask) for at in range(devices)])]
    dot_general x8 -> x10, matrix products: 101 us -> 48.4 us  [dot_nt(): lax.dot_general(left, right, (((1,), (1,)), ((), ())), preferred_element_...]
    dot_general x8 -> x10, matrix products: 77.4 us -> 45.1 us  [the longest x2 22.7 us: body(): jnp.dot(normed_two, weights[-2], preferred_element_type=F32)]
    slice x1 -> x48, local copies, waits for them, and re-layouts: 0.03 us -> 31.5 us  [the longest x27 28.2 us: halves_of(): lax.slice_in_dim(values, (2 * at + which) * size, (2 * at + which + 1) *...]
    add x8 -> x17, other arithmetic: 0.05 us -> 16 us  [the longest x2 10.4 us: body(): upstream = middle_grad + stream_grad]
    dot_general x32 -> x20, matrix products: 62.7 us -> 47.9 us  [dot_tn(): lax.dot_general(left, right, (((0,), (0,)), ((), ())), preferred_element_...]
  transfers between devices with their start and end apart: 173 -> 121, of which waited for: 81 -> 44; matrix products, arithmetic and copies ran while one was open for 23% -> 22% of each run, Pallas kernels for 8% -> 34%
where the time goes in v2:
time: 1400 us; the launch traced here: 1390 us
  Pallas kernels  604 us (43%)
  waiting for transfers between devices  250 us (18%)
  starting transfers between devices  165 us (12%)
  matrix products  141 us (10%)
  other arithmetic  137 us (10%)
  local copies, waits for them, and re-layouts  85.6 us (6%)
    pallas_call x4, Pallas kernels, merge(): pl.pallas_call(functools.partial(merge_kernel, size, count, axis), in_spe...  513 us
    ppermute x117, waiting for transfers between devices, swap(): lax.ppermute(values, BOTH, [(at, at ^ mask) for at in range(devices)])  250 us
    ppermute x117, starting transfers between devices, swap(): lax.ppermute(values, BOTH, [(at, at ^ mask) for at in range(devices)])  134 us
    pallas_call x2, Pallas kernels, attention_backward(): pl.pallas_call(backward_kernel, grid=(groups,), in_specs=[pl.BlockSpec(me...  55.2 us
    dot_general x10, matrix products, dot_nt(): lax.dot_general(left, right, (((1,), (1,)), ((), ())), preferred_element_...  48.4 us
    dot_general x20, matrix products, dot_tn(): lax.dot_general(left, right, (((0,), (0,)), ((), ())), preferred_element_...  47.9 us
    pallas_call x2, Pallas kernels, attention_forward(): pl.pallas_call(forward_kernel, grid=(groups,), in_specs=[pl.BlockSpec(mem...  36.5 us
    convert_element_type x40, other arithmetic, take(): (first.astype(F32) + second.astype(F32)).astype(BF16)  30.7 us
  transfers between devices with their start and end apart: 121, of which 44 were waited for; matrix products, arithmetic and copies ran while one was open for 22% of the time, Pallas kernels for 34%

profile of v2, /device:TPU:9, one launch (start us, length us, event | category | flops | bytes accessed | tf_op | source)
XLA Modules:
  0.0 1387.3 jit_solution(12237691390823082461)
XLA Ops:
  11.9 9.5 collective-permute-start.2
  66.1 5.1 collective-permute-done.25
  71.5 5.3 collective-permute-done.38
  100.9 8.9 collective-permute-done.26
  109.8 11.2 collective-permute-done.39
  135.1 18.2 %shard_map.169 = bf16[1024,512]{1,0:T(8,128)(2,1)S(1)} custom-call(f32[4,2]{1,0:T(4,128)S(1)} %multiply_power_fusion.slopes, bf16[1024,512]{1,0:T(8,128)(2,1)S(1)} %add_convert_fusion.15.query_in, bf16[1024,512]{1,0:T(8,128)(2,1)S(1)} %convolution_convert_fusion.18.key_in, bf16[1024,512]{1,0:T(8,128)(2,1)S(1)} %add_convert_fusion.14.value_in, ...), custom_call_target="tpu_custom_call" | custom-call | flops 10737418240 | bytes 4194304 | tf_op jit(solution)/shard_map/pallas_call | solution.py:170
  161.2 5.2 fusion.166
  169.1 14.4 %collective-permute-done.44 = bf16[256,512]{1,0:T(8,128)(2,1)S(1)} collective-permute-done((bf16[256,512]{1,0:T(8,128)(2,1)S(1)}, bf16[256,512]{1,0:T(8,128)(2,1)S(1)}, u32[]{:S(2)}, u32[]{:S(2)}) %collective-permute-start.44) | collective-permute-done | bytes 262176 | tf_op jit(solution)/shard_map/ppermute | solution.py:341
  197.0 42.5 %collective-permute-done.48 = bf16[256,1024]{1,0:T(8,128)(2,1)S(1)} collective-permute-done((bf16[256,1024]{1,0:T(8,128)(2,1)S(1)}, bf16[256,1024]{1,0:T(8,128)(2,1)S(1)}, u32[]{:S(2)}, u32[]{:S(2)}) %collective-permute-start.48) | collective-permute-done | bytes 524320 | tf_op jit(solution)/shard_map/ppermute | solution.py:341
  247.7 128.2 %shard_map.170 = bf16[1024,2048]{1,0:T(8,128)(2,1)} custom-call(bf16[512,2048]{1,0:T(8,128)(2,1)} %pad_maximum_fusion.1.first, bf16[512,2048]{1,0:T(8,128)(2,1)} %collective-permute-done.45.second), custom_call_target="tpu_custom_call" | custom-call | bytes 8388608 | tf_op jit(solution)/shard_map/pallas_call | solution.py:258
  375.9 128.2 %shard_map.171 = bf16[2048,1024]{1,0:T(8,128)(2,1)} custom-call(bf16[2048,512]{1,0:T(8,128)(2,1)} %pad_maximum_fusion.2.first, bf16[2048,512]{1,0:T(8,128)(2,1)} %collective-permute-done.46.second), custom_call_target="tpu_custom_call" | custom-call | bytes 8388608 | tf_op jit(solution)/shard_map/pallas_call | solution.py:258
  509.0 13.0 multiply_convert_fusion.1
  522.1 6.0 convolution_convert_fusion.12
  533.8 9.4 collective-permute-start.61
  546.2 4.1 collective-permute-start.62
  558.1 17.1 %collective-permute-done.54 = bf16[512,1024]{1,0:T(8,128)(2,1)S(1)} collective-permute-done((bf16[512,1024]{1,0:T(8,128)(2,1)S(1)}, bf16[512,1024]{1,0:T(8,128)(2,1)S(1)}, u32[]{:S(2)}, u32[]{:S(2)}) %collective-permute-start.54) | collective-permute-done | bytes 1048608 | tf_op jit(solution)/shard_map/ppermute | solution.py:341
  575.9 3.9 add_convert_fusion.query_in.key_in.value_in
  579.8 18.3 %shard_map.172 = bf16[1024,512]{1,0:T(8,128)(2,1)S(1)} custom-call(f32[4,2]{1,0:T(4,128)S(1)} %multiply_power_fusion.slopes, bf16[1024,1536]{1,0:T(8,128)(2,1)S(1)} %add_convert_fusion.query_in.key_in.value_in, bf16[1024,1536]{1,0:T(8,128)(2,1)S(1)} %add_convert_fusion.query_in.key_in.value_in, ...), custom_call_target="tpu_custom_call" | custom-call | flops 10737418240 | bytes 4194304 | tf_op jit(solution)/shard_map/pallas_call | solution.py:170
  606.7 6.1 pad_maximum_fusion.4.first
  618.0 31.0 %collective-permute-done.57.second = bf16[512,2048]{1,0:T(8,128)(2,1)} collective-permute-done((bf16[512,2048]{1,0:T(8,128)(2,1)S(1)}, bf16[512,2048]{1,0:T(8,128)(2,1)}, u32[]{:S(2)}, u32[]{:S(2)}) %collective-permute-start.57) | collective-permute-done | bytes 2097184 | tf_op jit(solution)/shard_map/ppermute | solution.py:341
  649.0 128.2 %shard_map.173 = bf16[1024,2048]{1,0:T(8,128)(2,1)} custom-call(bf16[512,2048]{1,0:T(8,128)(2,1)} %copy-done.28, bf16[512,2048]{1,0:T(8,128)(2,1)} %collective-permute-done.57.second), custom_call_target="tpu_custom_call" | custom-call | bytes 8388608 | tf_op jit(solution)/shard_map/pallas_call | solution.py:258
  783.6 9.7 multiply_convert_fusion
  793.3 128.2 %shard_map.174 = bf16[2048,1024]{1,0:T(8,128)(2,1)} custom-call(bf16[2048,512]{1,0:T(8,128)(2,1)} %copy-done.29, bf16[2048,512]{1,0:T(8,128)(2,1)} %collective-permute-done.58.second), custom_call_target="tpu_custom_call" | custom-call | bytes 8388608 | tf_op jit(solution)/shard_map/pallas_call | solution.py:258
  921.5 13.4 fusion.214
  934.9 4.8 convolution_convert_fusion.9
  940.6 6.0 convolution_convert_fusion.10
  962.9 4.8 convolution_convert_fusion.6
  967.7 4.6 multiply_reduce_fusion
  972.3 7.0 fusion.163
  980.6 9.6 collective-permute-start.60
  991.5 13.2 collective-permute-done.64
  1010.1 27.7 %shard_map.175 = (bf16[3,1024,512]{2,1,0:T(8,128)(2,1)S(1)}, f32[4,2,128]{2,1,0:T(2,128)S(1)}) custom-call(f32[4,2]{1,0:T(4,128)S(1)} %multiply_power_fusion.slopes, bf16[1024,1536]{1,0:T(8,128)(2,1)} %copy-done.6, bf16[1024,1536]{1,0:T(8,128)(2,1)} %copy-done.6, bf16[1024,1536]{1,0:T(8,128)(2,1)} %copy-done.6, ...), custom_call_target="tpu_custom_call" | custom-call | flops 17179869184 | bytes 7340032 | tf_op jit(solution)/shard_map/pallas_call | solution.py:196
  1070.6 4.5 multiply_reduce_fusion.1
  1078.8 7.1 collective-permute-done.70
  1096.6 12.1 fusion.161
  1110.9 3.9 convolution_convert_fusion.3
  1126.8 8.0 convolution_convert_fusion.8
  1147.5 4.2 convolution_convert_fusion.1
  1155.3 21.7 %collective-permute-done.79 = bf16[512,768]{1,0:T(8,128)(2,1)S(1)} collective-permute-done((bf16[512,768]{1,0:T(8,128)(2,1)S(1)}, bf16[512,768]{1,0:T(8,128)(2,1)S(1)}, u32[]{:S(2)}, u32[]{:S(2)}) %collective-permute-start.79) | collective-permute-done | bytes 786464 | tf_op jit(solution)/shard_map/ppermute | solution.py:341
  1198.2 11.3 collective-permute-done.80
  1212.8 27.5 %shard_map.176 = (bf16[3,1024,512]{2,1,0:T(8,128)(2,1)}, f32[4,2,128]{2,1,0:T(2,128)S(1)}) custom-call(f32[4,2]{1,0:T(4,128)S(1)} %multiply_power_fusion.slopes, bf16[1024,512]{1,0:T(8,128)(2,1)S(1)} %copy-done.3, bf16[1024,512]{1,0:T(8,128)(2,1)S(1)} %copy-done.5, bf16[1024,512]{1,0:T(8,128)(2,1)S(1)} %copy-done.1, ...), custom_call_target="tpu_custom_call" | custom-call | flops 17179869184 | bytes 7340032 | tf_op jit(solution)/shard_map/pallas_call | solution.py:196
  1244.6 5.2 collective-permute-done.82
  1284.4 5.8 fusion.24
  1301.4 6.8 fusion.23
  1335.4 4.6 collective-permute-start.107
  1341.5 4.8 collective-permute-start.120
  1348.5 5.0 collective-permute-done.108
  1368.4 8.8 collective-permute-start.119
  (1004 shorter events, 398.5 us)
Async XLA Ops:
  5.8 42.4 %collective-permute-start.9 = (bf16[256,128]{1,0:T(8,128)(2,1)S(1)}, bf16[256,128]{1,0:T(8,128)(2,1)S(1)}, u32[]{:S(2)}, u32[]{:S(2)}) collective-permute-start(bf16[256,128]{1,0:T(8,128)(2,1)S(1)} %get-tuple-element.139), channel_id=1, source_target_pairs={{0,2},{1,3},{2,0},{3,1},{4,6},{5,7},{6,4},{7,5},{8,10},{9,11},{10,... | collective-permute-start | bytes 196616 | tf_op jit(solution)/shard_map/ppermute | solution.py:341
  11.9 83.4 %collective-permute-start.2 = (bf16[512,1024]{0,1:T(8,128)(2,1)}, bf16[512,1024]{0,1:T(8,128)(2,1)}, u32[]{:S(2)}, u32[]{:S(2)}) collective-permute-start(bf16[512,1024]{0,1:T(8,128)(2,1)} %copy.43), channel_id=1, source_target_pairs={{0,0},{1,4},{2,2},{3,6},{4,1},{5,5},{6,3},{7,7},{8,8},{9,12},{10,1... | collective-permute-start | bytes 3145736 | tf_op jit(solution)/shard_map/ppermute | solution.py:349
  21.4 28.3 %collective-permute-start.13 = (bf16[256,128]{1,0:T(8,128)(2,1)S(1)}, bf16[256,128]{1,0:T(8,128)(2,1)}, u32[]{:S(2)}, u32[]{:S(2)}) collective-permute-start(bf16[256,128]{1,0:T(8,128)(2,1)S(1)} %get-tuple-element.141), channel_id=1, source_target_pairs={{0,2},{1,3},{2,0},{3,1},{4,6},{5,7},{6,4},{7,5},{8,10},{9,11},{10,... | collective-permute-start | bytes 196616 | tf_op jit(solution)/shard_map/ppermute | solution.py:341
  21.4 29.8 %collective-permute-start.15 = (bf16[128,256]{1,0:T(8,128)(2,1)S(1)}, bf16[128,256]{1,0:T(8,128)(2,1)}, u32[]{:S(2)}, u32[]{:S(2)}) collective-permute-start(bf16[128,256]{1,0:T(8,128)(2,1)S(1)} %pad_maximum_fusion.51), channel_id=1, source_target_pairs={{0,2},{1,3},{2,0},{3,1},{4,6},{5,7},{6,4},{7,5},{8,10},{9,11},{10,... | collective-permute-start | bytes 196616 | tf_op jit(solution)/shard_map/ppermute | solution.py:341
  63.0 34.3 %collective-permute-start.27 = (bf16[256,512]{1,0:T(8,128)(2,1)S(1)}, bf16[256,512]{1,0:T(8,128)(2,1)S(1)}, u32[]{:S(2)}, u32[]{:S(2)}) collective-permute-start(bf16[256,512]{1,0:T(8,128)(2,1)S(1)} %pad_maximum_fusion.31), channel_id=1, source_target_pairs={{0,2},{1,3},{2,0},{3,1},{4,6},{5,7},{6,4},{7,5},{8,10},{9,11},{10,... | collective-permute-start | bytes 786440 | tf_op jit(solution)/shard_map/ppermute | solution.py:341
  95.3 25.8 %collective-permute-start.3 = (bf16[512,1024]{0,1:T(8,128)(2,1)}, bf16[512,1024]{0,1:T(8,128)(2,1)S(1)}, u32[]{:S(2)}, u32[]{:S(2)}) collective-permute-start(bf16[512,1024]{0,1:T(8,128)(2,1)} %collective-permute-done.2), channel_id=1, source_target_pairs={{0,4},{1,5},{2,6},{3,7},{4,0},{5,1},{6,2},{7,3},{8,12},{9,13},{10,... | collective-permute-start | bytes 3145736 | tf_op jit(solution)/shard_map/ppermute | solution.py:341
  99.6 28.4 %collective-permute-start.22 = (bf16[512,512]{1,0:T(8,128)(2,1)S(1)}, bf16[512,512]{1,0:T(8,128)(2,1)S(1)}, u32[]{:S(2)}, u32[]{:S(2)}) collective-permute-start(bf16[512,512]{1,0:T(8,128)(2,1)S(1)} %pad_maximum_fusion.20), channel_id=1, source_target_pairs={{0,16},{1,17},{2,18},{3,19},{4,20},{5,21},{6,22},{7,23},{8,24},{9,... | collective-permute-start | bytes 1572872 | tf_op jit(solution)/shard_map/ppermute | solution.py:341
  157.5 26.1 %collective-permute-start.41 = (bf16[512,1024]{1,0:T(8,128)(2,1)S(1)}, bf16[512,1024]{1,0:T(8,128)(2,1)S(1)}, u32[]{:S(2)}, u32[]{:S(2)}) collective-permute-start(bf16[512,1024]{1,0:T(8,128)(2,1)S(1)} %pad_maximum_fusion.7), channel_id=1, source_target_pairs={{0,1},{1,0},{2,3},{3,2},{4,5},{5,4},{6,7},{7,6},{8,9},{9,8},{10,11... | collective-permute-start | bytes 3145736 | tf_op jit(solution)/shard_map/ppermute | solution.py:341
  157.7 25.9 %collective-permute-start.42 = (bf16[2048,256]{1,0:T(8,128)(2,1)S(1)}, bf16[2048,256]{1,0:T(8,128)(2,1)S(1)}, u32[]{:S(2)}, u32[]{:S(2)}) collective-permute-start(bf16[2048,256]{1,0:T(8,128)(2,1)S(1)} %pad_maximum_fusion.13), channel_id=1, source_target_pairs={{0,16},{1,17},{2,18},{3,19},{4,20},{5,21},{6,22},{7,23},{8,24},{9,... | collective-permute-start | bytes 3145736 | tf_op jit(solution)/shard_map/ppermute | solution.py:341
  159.1 24.5 %collective-permute-start.43 = (bf16[512,768]{1,0:T(8,128)(2,1)S(1)}, bf16[512,768]{1,0:T(8,128)(2,1)S(1)}, u32[]{:S(2)}, u32[]{:S(2)}) collective-permute-start(bf16[512,768]{1,0:T(8,128)(2,1)S(1)} %pad_maximum_fusion.18), channel_id=1, source_target_pairs={{0,8},{1,9},{2,10},{3,11},{4,12},{5,13},{6,14},{7,15},{8,0},{9,1},... | collective-permute-start | bytes 2359304 | tf_op jit(solution)/shard_map/ppermute | solution.py:341
  185.3 54.2 %collective-permute-start.45 = (bf16[512,2048]{1,0:T(8,128)(2,1)}, bf16[512,2048]{1,0:T(8,128)(2,1)}, u32[]{:S(2)}, u32[]{:S(2)}) collective-permute-start(bf16[512,2048]{1,0:T(8,128)(2,1)} %pad_maximum_fusion.1.first), channel_id=1, source_target_pairs={{0,16},{1,17},{2,18},{3,19},{4,20},{5,21},{6,22},{7,23},{8,24},{9,... | collective-permute-start | bytes 6291464 | tf_op jit(solution)/shard_map/ppermute | solution.py:341
  187.0 52.5 %collective-permute-start.46 = (bf16[2048,512]{1,0:T(8,128)(2,1)}, bf16[2048,512]{1,0:T(8,128)(2,1)}, u32[]{:S(2)}, u32[]{:S(2)}) collective-permute-start(bf16[2048,512]{1,0:T(8,128)(2,1)} %pad_maximum_fusion.2.first), channel_id=1, source_target_pairs={{0,8},{1,9},{2,10},{3,11},{4,12},{5,13},{6,14},{7,15},{8,0},{9,1},... | collective-permute-start | bytes 6291464 | tf_op jit(solution)/shard_map/ppermute | solution.py:341
  188.4 51.1 %collective-permute-start.47 = (bf16[1024,768]{1,0:T(8,128)(2,1)S(1)}, bf16[1024,768]{1,0:T(8,128)(2,1)}, u32[]{:S(2)}, u32[]{:S(2)}) collective-permute-start(bf16[1024,768]{1,0:T(8,128)(2,1)S(1)} %pad_maximum_fusion.6), channel_id=1, source_target_pairs={{0,1},{1,0},{2,3},{3,2},{4,5},{5,4},{6,7},{7,6},{8,9},{9,8},{10,11... | collective-permute-start | bytes 4718600 | tf_op jit(solution)/shard_map/ppermute | solution.py:341
  192.9 313.0 %collective-permute-start.49 = (bf16[256,512]{1,0:T(8,128)(2,1)}, bf16[256,512]{1,0:T(8,128)(2,1)}, u32[]{:S(2)}, u32[]{:S(2)}) collective-permute-start(bf16[256,512]{1,0:T(8,128)(2,1)} %pad_maximum_fusion.35), channel_id=1, source_target_pairs={{0,2},{1,3},{2,0},{3,1},{4,6},{5,7},{6,4},{7,5},{8,10},{9,11},{10,... | collective-permute-start | bytes 786440 | tf_op jit(solution)/shard_map/ppermute | solution.py:341
  194.8 44.7 %collective-permute-start.48 = (bf16[256,1024]{1,0:T(8,128)(2,1)S(1)}, bf16[256,1024]{1,0:T(8,128)(2,1)S(1)}, u32[]{:S(2)}, u32[]{:S(2)}) collective-permute-start(bf16[256,1024]{1,0:T(8,128)(2,1)S(1)} %pad_maximum_fusion.25), channel_id=1, source_target_pairs={{0,1},{1,0},{2,3},{3,2},{4,5},{5,4},{6,7},{7,6},{8,9},{9,8},{10,11... | collective-permute-start | bytes 1572872 | tf_op jit(solution)/shard_map/ppermute | solution.py:341
  239.5 266.3 %collective-permute-start.50 = (bf16[512,256]{1,0:T(8,128)(2,1)S(1)}, bf16[512,256]{1,0:T(8,128)(2,1)}, u32[]{:S(2)}, u32[]{:S(2)}) collective-permute-start(bf16[512,256]{1,0:T(8,128)(2,1)S(1)} %pad_maximum_fusion.36), channel_id=1, source_target_pairs={{0,2},{1,3},{2,0},{3,1},{4,6},{5,7},{6,4},{7,5},{8,10},{9,11},{10,... | collective-permute-start | bytes 786440 | tf_op jit(solution)/shard_map/ppermute | solution.py:341
  528.1 25.1 %collective-permute-start.53 = (bf16[1024,1024]{0,1:T(8,128)(2,1)}, bf16[1024,1024]{0,1:T(8,128)(2,1)}, u32[]{:S(2)}, u32[]{:S(2)}) collective-permute-start(bf16[1024,1024]{0,1:T(8,128)(2,1)} %convolution_convert_fusion.12), channel_id=1, source_target_pairs={{0,4},{1,5},{2,6},{3,7},{4,0},{5,1},{6,2},{7,3},{8,12},{9,13},{10,... | collective-permute-start | bytes 6291464 | tf_op jit(solution)/shard_map/ppermute | solution.py:341
  546.2 57.7 %collective-permute-start.62 = (bf16[512,1024]{0,1:T(8,128)(2,1)}, bf16[512,1024]{0,1:T(8,128)(2,1)S(1)}, u32[]{:S(2)}, u32[]{:S(2)}) collective-permute-start(bf16[512,1024]{0,1:T(8,128)(2,1)} %collective-permute-done.61), channel_id=1, source_target_pairs={{0,4},{1,5},{2,6},{3,7},{4,0},{5,1},{6,2},{7,3},{8,12},{9,13},{10,... | collective-permute-start | bytes 3145736 | tf_op jit(solution)/shard_map/ppermute | solution.py:341
  550.3 24.9 %collective-permute-start.54 = (bf16[512,1024]{1,0:T(8,128)(2,1)S(1)}, bf16[512,1024]{1,0:T(8,128)(2,1)S(1)}, u32[]{:S(2)}, u32[]{:S(2)}) collective-permute-start(bf16[512,1024]{1,0:T(8,128)(2,1)S(1)} %pad_maximum_fusion.8), channel_id=1, source_target_pairs={{0,1},{1,0},{2,3},{3,2},{4,5},{5,4},{6,7},{7,6},{8,9},{9,8},{10,11... | collective-permute-start | bytes 3145736 | tf_op jit(solution)/shard_map/ppermute | solution.py:341
  551.9 24.0 %collective-permute-start.55 = (bf16[2048,256]{1,0:T(8,128)(2,1)S(1)}, bf16[2048,256]{1,0:T(8,128)(2,1)S(1)}, u32[]{:S(2)}, u32[]{:S(2)}) collective-permute-start(bf16[2048,256]{1,0:T(8,128)(2,1)S(1)} %pad_maximum_fusion.15), channel_id=1, source_target_pairs={{0,16},{1,17},{2,18},{3,19},{4,20},{5,21},{6,22},{7,23},{8,24},{9,... | collective-permute-start | bytes 3145736 | tf_op jit(solution)/shard_map/ppermute | solution.py:341
  601.6 47.4 %collective-permute-start.57 = (bf16[512,2048]{1,0:T(8,128)(2,1)S(1)}, bf16[512,2048]{1,0:T(8,128)(2,1)}, u32[]{:S(2)}, u32[]{:S(2)}) collective-permute-start(bf16[512,2048]{1,0:T(8,128)(2,1)S(1)} %pad_maximum_fusion.3.first), channel_id=1, source_target_pairs={{0,16},{1,17},{2,18},{3,19},{4,20},{5,21},{6,22},{7,23},{8,24},{9,... | collective-permute-start | bytes 6291464 | tf_op jit(solution)/shard_map/ppermute | solution.py:341
  612.8 180.5 %collective-permute-start.58 = (bf16[2048,512]{1,0:T(8,128)(2,1)S(1)}, bf16[2048,512]{1,0:T(8,128)(2,1)}, u32[]{:S(2)}, u32[]{:S(2)}) collective-permute-start(bf16[2048,512]{1,0:T(8,128)(2,1)S(1)} %pad_maximum_fusion.4.first), channel_id=1, source_target_pairs={{0,8},{1,9},{2,10},{3,11},{4,12},{5,13},{6,14},{7,15},{8,0},{9,1},... | collective-permute-start | bytes 6291464 | tf_op jit(solution)/shard_map/ppermute | solution.py:341
  939.7 28.0 %collective-permute-start.63 = (bf16[1024,1024]{0,1:T(8,128)(2,1)S(1)}, bf16[1024,1024]{0,1:T(8,128)(2,1)}, u32[]{:S(2)}, u32[]{:S(2)}) collective-permute-start(bf16[1024,1024]{0,1:T(8,128)(2,1)S(1)} %convolution_convert_fusion.9), channel_id=1, source_target_pairs={{0,4},{1,5},{2,6},{3,7},{4,0},{5,1},{6,2},{7,3},{8,12},{9,13},{10,... | collective-permute-start | bytes 6291464 | tf_op jit(solution)/shard_map/ppermute | solution.py:341
  957.6 47.0 %collective-permute-start.64 = (bf16[2048,512]{1,0:T(8,128)(2,1)}, bf16[2048,512]{1,0:T(8,128)(2,1)}, u32[]{:S(2)}, u32[]{:S(2)}) collective-permute-start(bf16[2048,512]{1,0:T(8,128)(2,1)} %convolution_convert_fusion.7), channel_id=1, source_target_pairs={{0,8},{1,9},{2,10},{3,11},{4,12},{5,13},{6,14},{7,15},{8,0},{9,1},... | collective-permute-start | bytes 6291464 | tf_op jit(solution)/shard_map/ppermute | solution.py:341
  958.9 81.2 %collective-permute-start.66 = (bf16[512,2048]{1,0:T(8,128)(2,1)}, bf16[512,2048]{1,0:T(8,128)(2,1)}, u32[]{:S(2)}, u32[]{:S(2)}) collective-permute-start(bf16[512,2048]{1,0:T(8,128)(2,1)} %convolution_convert_fusion.5), channel_id=1, source_target_pairs={{0,16},{1,17},{2,18},{3,19},{4,20},{5,21},{6,22},{7,23},{8,24},{9,... | collective-permute-start | bytes 6291464 | tf_op jit(solution)/shard_map/ppermute | solution.py:341
  980.6 80.7 %collective-permute-start.60 = (bf16[512,1024]{0,1:T(8,128)(2,1)}, bf16[512,1024]{0,1:T(8,128)(2,1)}, u32[]{:S(2)}, u32[]{:S(2)}) collective-permute-start(bf16[512,1024]{0,1:T(8,128)(2,1)} %fusion.49), channel_id=1, source_target_pairs={{0,0},{1,4},{2,2},{3,6},{4,1},{5,5},{6,3},{7,7},{8,8},{9,12},{10,1... | collective-permute-start | bytes 3145736 | tf_op jit(solution)/shard_map/ppermute | solution.py:349
  1006.8 33.2 %collective-permute-start.65 = (bf16[2048,256]{1,0:T(8,128)(2,1)S(1)}, bf16[2048,256]{1,0:T(8,128)(2,1)S(1)}, u32[]{:S(2)}, u32[]{:S(2)}) collective-permute-start(bf16[2048,256]{1,0:T(8,128)(2,1)S(1)} %get-tuple-element.311), channel_id=1, source_target_pairs={{0,16},{1,17},{2,18},{3,19},{4,20},{5,21},{6,22},{7,23},{8,24},{9,... | collective-permute-start | bytes 3145736 | tf_op jit(solution)/shard_map/ppermute | solution.py:341
  1009.0 31.1 %collective-permute-start.67 = (bf16[256,1024]{1,0:T(8,128)(2,1)S(1)}, bf16[256,1024]{1,0:T(8,128)(2,1)S(1)}, u32[]{:S(2)}, u32[]{:S(2)}) collective-permute-start(bf16[256,1024]{1,0:T(8,128)(2,1)S(1)} %convolution_convert_fusion.24), channel_id=1, source_target_pairs={{0,1},{1,0},{2,3},{3,2},{4,5},{5,4},{6,7},{7,6},{8,9},{9,8},{10,11... | collective-permute-start | bytes 1572872 | tf_op jit(solution)/shard_map/ppermute | solution.py:341
  1045.8 24.7 %collective-permute-start.68 = (bf16[1024,1024]{0,1:T(8,128)(2,1)S(1)}, bf16[1024,1024]{0,1:T(8,128)(2,1)}, u32[]{:S(2)}, u32[]{:S(2)}) collective-permute-start(bf16[1024,1024]{0,1:T(8,128)(2,1)S(1)} %fusion.41), channel_id=1, source_target_pairs={{0,4},{1,5},{2,6},{3,7},{4,0},{5,1},{6,2},{7,3},{8,12},{9,13},{10,... | collective-permute-start | bytes 6291464 | tf_op jit(solution)/shard_map/ppermute | solution.py:341
  1049.6 29.2 %collective-permute-start.69 = (bf16[1024,256]{1,0:T(8,128)(2,1)}, bf16[1024,256]{1,0:T(8,128)(2,1)}, u32[]{:S(2)}, u32[]{:S(2)}) collective-permute-start(bf16[1024,256]{1,0:T(8,128)(2,1)} %add_convert_fusion.25), channel_id=1, source_target_pairs={{0,1},{1,0},{2,3},{3,2},{4,5},{5,4},{6,7},{7,6},{8,9},{9,8},{10,11... | collective-permute-start | bytes 1572872 | tf_op jit(solution)/shard_map/ppermute | solution.py:341
  1053.9 32.0 %collective-permute-start.70 = (bf16[512,1024]{1,0:T(8,128)(2,1)}, bf16[512,1024]{1,0:T(8,128)(2,1)}, u32[]{:S(2)}, u32[]{:S(2)}) collective-permute-start(bf16[512,1024]{1,0:T(8,128)(2,1)} %add_convert_fusion.11), channel_id=1, source_target_pairs={{0,1},{1,0},{2,3},{3,2},{4,5},{5,4},{6,7},{7,6},{8,9},{9,8},{10,11... | collective-permute-start | bytes 3145736 | tf_op jit(solution)/shard_map/ppermute | solution.py:341
  1061.3 62.1 %collective-permute-start.75 = (bf16[1024,768]{1,0:T(8,128)(2,1)}, bf16[1024,768]{1,0:T(8,128)(2,1)}, u32[]{:S(2)}, u32[]{:S(2)}) collective-permute-start(bf16[1024,768]{1,0:T(8,128)(2,1)} %convolution_convert_fusion.15), channel_id=1, source_target_pairs={{0,1},{1,0},{2,3},{3,2},{4,5},{5,4},{6,7},{7,6},{8,9},{9,8},{10,11... | collective-permute-start | bytes 4718600 | tf_op jit(solution)/shard_map/ppermute | solution.py:341
  1088.2 38.7 %collective-permute-start.72 = (bf16[512,256]{1,0:T(8,128)(2,1)}, bf16[512,256]{1,0:T(8,128)(2,1)}, u32[]{:S(2)}, u32[]{:S(2)}) collective-permute-start(bf16[512,256]{1,0:T(8,128)(2,1)} %add_convert_fusion.44), channel_id=1, source_target_pairs={{0,2},{1,3},{2,0},{3,1},{4,6},{5,7},{6,4},{7,5},{8,10},{9,11},{10,... | collective-permute-start | bytes 786440 | tf_op jit(solution)/shard_map/ppermute | solution.py:341
  1093.4 33.5 %collective-permute-start.73 = (bf16[256,1024]{1,0:T(8,128)(2,1)}, bf16[256,1024]{1,0:T(8,128)(2,1)}, u32[]{:S(2)}, u32[]{:S(2)}) collective-permute-start(bf16[256,1024]{1,0:T(8,128)(2,1)} %get-tuple-element.339), channel_id=1, source_target_pairs={{0,8},{1,9},{2,10},{3,11},{4,12},{5,13},{6,14},{7,15},{8,0},{9,1},... | collective-permute-start | bytes 1572872 | tf_op jit(solution)/shard_map/ppermute | solution.py:341
  1096.3 27.1 %collective-permute-start.74 = (bf16[256,256]{1,0:T(8,128)(2,1)}, bf16[256,256]{1,0:T(8,128)(2,1)}, u32[]{:S(2)}, u32[]{:S(2)}) collective-permute-start(bf16[256,256]{1,0:T(8,128)(2,1)} %get-tuple-element.473), channel_id=1, source_target_pairs={{0,16},{1,17},{2,18},{3,19},{4,20},{5,21},{6,22},{7,23},{8,24},{9,... | collective-permute-start | bytes 393224 | tf_op jit(solution)/shard_map/ppermute | solution.py:341
  1114.8 83.5 %collective-permute-start.81 = (bf16[2048,512]{1,0:T(8,128)(2,1)}, bf16[2048,512]{1,0:T(8,128)(2,1)S(1)}, u32[]{:S(2)}, u32[]{:S(2)}) collective-permute-start(bf16[2048,512]{1,0:T(8,128)(2,1)} %convolution_convert_fusion.3), channel_id=1, source_target_pairs={{0,8},{1,9},{2,10},{3,11},{4,12},{5,13},{6,14},{7,15},{8,0},{9,1},... | collective-permute-start | bytes 6291464 | tf_op jit(solution)/shard_map/ppermute | solution.py:341
  1151.9 25.1 %collective-permute-start.79 = (bf16[512,768]{1,0:T(8,128)(2,1)S(1)}, bf16[512,768]{1,0:T(8,128)(2,1)S(1)}, u32[]{:S(2)}, u32[]{:S(2)}) collective-permute-start(bf16[512,768]{1,0:T(8,128)(2,1)S(1)} %add_convert_fusion.17), channel_id=1, source_target_pairs={{0,8},{1,9},{2,10},{3,11},{4,12},{5,13},{6,14},{7,15},{8,0},{9,1},... | collective-permute-start | bytes 2359304 | tf_op jit(solution)/shard_map/ppermute | solution.py:341
  1154.1 90.5 %collective-permute-start.84 = (bf16[512,2048]{1,0:T(8,128)(2,1)}, bf16[512,2048]{1,0:T(8,128)(2,1)}, u32[]{:S(2)}, u32[]{:S(2)}) collective-permute-start(bf16[512,2048]{1,0:T(8,128)(2,1)} %convolution_convert_fusion.1), channel_id=1, source_target_pairs={{0,16},{1,17},{2,18},{3,19},{4,20},{5,21},{6,22},{7,23},{8,24},{9,... | collective-permute-start | bytes 6291464 | tf_op jit(solution)/shard_map/ppermute | solution.py:341
  1180.1 29.4 %collective-permute-start.80 = (bf16[256,768]{1,0:T(8,128)(2,1)S(1)}, bf16[256,768]{1,0:T(8,128)(2,1)S(1)}, u32[]{:S(2)}, u32[]{:S(2)}) collective-permute-start(bf16[256,768]{1,0:T(8,128)(2,1)S(1)} %get-tuple-element.365), channel_id=1, source_target_pairs={{0,16},{1,17},{2,18},{3,19},{4,20},{5,21},{6,22},{7,23},{8,24},{9,... | collective-permute-start | bytes 1179656 | tf_op jit(solution)/shard_map/ppermute | solution.py:341
  1186.4 58.1 %collective-permute-start.85 = (bf16[256,1024]{1,0:T(8,128)(2,1)}, bf16[256,1024]{1,0:T(8,128)(2,1)}, u32[]{:S(2)}, u32[]{:S(2)}) collective-permute-start(bf16[256,1024]{1,0:T(8,128)(2,1)} %convolution_convert_fusion.22), channel_id=1, source_target_pairs={{0,1},{1,0},{2,3},{3,2},{4,5},{5,4},{6,7},{7,6},{8,9},{9,8},{10,11... | collective-permute-start | bytes 1572872 | tf_op jit(solution)/shard_map/ppermute | solution.py:341
  1212.2 37.5 %collective-permute-start.83 = (bf16[2048,256]{1,0:T(8,128)(2,1)}, bf16[2048,256]{1,0:T(8,128)(2,1)}, u32[]{:S(2)}, u32[]{:S(2)}) collective-permute-start(bf16[2048,256]{1,0:T(8,128)(2,1)} %get-tuple-element.308), channel_id=1, source_target_pairs={{0,16},{1,17},{2,18},{3,19},{4,20},{5,21},{6,22},{7,23},{8,24},{9,... | collective-permute-start | bytes 3145736 | tf_op jit(solution)/shard_map/ppermute | solution.py:341
  1257.3 25.8 %collective-permute-start.86 = (bf16[1024,1024]{0,1:T(8,128)(2,1)S(1)}, bf16[1024,1024]{0,1:T(8,128)(2,1)}, u32[]{:S(2)}, u32[]{:S(2)}) collective-permute-start(bf16[1024,1024]{0,1:T(8,128)(2,1)S(1)} %add_convert_fusion.1), channel_id=1, source_target_pairs={{0,4},{1,5},{2,6},{3,7},{4,0},{5,1},{6,2},{7,3},{8,12},{9,13},{10,... | collective-permute-start | bytes 6291464 | tf_op jit(solution)/shard_map/ppermute | solution.py:341
  1260.4 48.0 %collective-permute-start.93 = (bf16[1024,256]{1,0:T(8,128)(2,1)}, bf16[1024,256]{1,0:T(8,128)(2,1)}, u32[]{:S(2)}, u32[]{:S(2)}) collective-permute-start(bf16[1024,256]{1,0:T(8,128)(2,1)} %add_convert_fusion.21), channel_id=1, source_target_pairs={{0,1},{1,0},{2,3},{3,2},{4,5},{5,4},{6,7},{7,6},{8,9},{9,8},{10,11... | collective-permute-start | bytes 1572872 | tf_op jit(solution)/shard_map/ppermute | solution.py:341
  1265.2 46.8 %collective-permute-start.94 = (bf16[512,1024]{1,0:T(8,128)(2,1)}, bf16[512,1024]{1,0:T(8,128)(2,1)}, u32[]{:S(2)}, u32[]{:S(2)}) collective-permute-start(bf16[512,1024]{1,0:T(8,128)(2,1)} %add_convert_fusion.7), channel_id=1, source_target_pairs={{0,1},{1,0},{2,3},{3,2},{4,5},{5,4},{6,7},{7,6},{8,9},{9,8},{10,11... | collective-permute-start | bytes 3145736 | tf_op jit(solution)/shard_map/ppermute | solution.py:341
  1267.1 32.8 %collective-permute-start.95 = (bf16[256,512]{1,0:T(8,128)(2,1)}, bf16[256,512]{1,0:T(8,128)(2,1)}, u32[]{:S(2)}, u32[]{:S(2)}) collective-permute-start(bf16[256,512]{1,0:T(8,128)(2,1)} %add_convert_fusion.39), channel_id=1, source_target_pairs={{0,8},{1,9},{2,10},{3,11},{4,12},{5,13},{6,14},{7,15},{8,0},{9,1},... | collective-permute-start | bytes 786440 | tf_op jit(solution)/shard_map/ppermute | solution.py:341
  1279.4 30.2 %collective-permute-start.96 = (bf16[512,512]{1,0:T(8,128)(2,1)}, bf16[512,512]{1,0:T(8,128)(2,1)}, u32[]{:S(2)}, u32[]{:S(2)}) collective-permute-start(bf16[512,512]{1,0:T(8,128)(2,1)} %convolution_convert_fusion.27), channel_id=1, source_target_pairs={{0,16},{1,17},{2,18},{3,19},{4,20},{5,21},{6,22},{7,23},{8,24},{9,... | collective-permute-start | bytes 1572872 | tf_op jit(solution)/shard_map/ppermute | solution.py:341
  1283.1 26.4 %collective-permute-start.97 = (bf16[512,512]{1,0:T(8,128)(2,1)}, bf16[512,512]{1,0:T(8,128)(2,1)}, u32[]{:S(2)}, u32[]{:S(2)}) collective-permute-start(bf16[512,512]{1,0:T(8,128)(2,1)} %convolution_convert_fusion.26), channel_id=1, source_target_pairs={{0,8},{1,9},{2,10},{3,11},{4,12},{5,13},{6,14},{7,15},{8,0},{9,1},... | collective-permute-start | bytes 1572872 | tf_op jit(solution)/shard_map/ppermute | solution.py:341
  1355.2 30.2 %collective-permute-start.91 = (bf16[512,1024]{0,1:T(8,128)(2,1)}, bf16[512,1024]{0,1:T(8,128)(2,1)S(1)}, u32[]{:S(2)}, u32[]{:S(2)}) collective-permute-start(bf16[512,1024]{0,1:T(8,128)(2,1)} %fusion.46), channel_id=1, source_target_pairs={{0,0},{1,4},{2,2},{3,6},{4,1},{5,5},{6,3},{7,7},{8,8},{9,12},{10,1... | collective-permute-start | bytes 3145736 | tf_op jit(solution)/shard_map/ppermute | solution.py:349
  (279 other events, 4117.6 us)

commit v3 on v2

--- a/solution.py
+++ b/solution.py
@@ -225,42 +225,42 @@
     )(slopes, *packed, upstream, seg_col, seg_row)
 
 
-def merge_kernel(size, count, axis, first, second, joined, done):
-    copies = []
-    for at in range(count):
-        for which, source in enumerate((first, second)):
-            near = [slice(None), slice(None)]
-            far = [slice(None), slice(None)]
-            near[axis] = pl.ds(at * size, size)
-            far[axis] = pl.ds((2 * at + which) * size, size)
-            copies.append(
-                pltpu.make_async_copy(
-                    source.at[tuple(near)], joined.at[tuple(far)], done.at[2 * at + which]
-                )
-            )
-    for copy in copies:
-        copy.start()
-    for copy in copies:
-        copy.wait()
+def merge_kernel(axis, first, second, joined):
+    size = first.shape[axis]
+    for which, source in enumerate((first, second)):
+        at = pl.ds(which * size, size)
+        if axis == 0:
+            joined[at, :] = source[...]
+        else:
+            joined[:, at] = source[...]
 
 
 def merge(first, second, size, count, axis):
     shape = list(first.shape)
     shape[axis] *= 2
     grain = LANES if axis == 1 else 16
-    if first.size < 2**20 or size % grain or shape[1] % LANES or shape[0] % 16:
+    if first.size < 2**20 or size % grain or shape[1] % (4 * LANES) or shape[0] % 64:
         parts = []
         for at in range(count):
             for values in (first, second):
                 parts.append(lax.slice_in_dim(values, at * size, (at + 1) * size, axis=axis))
         return jnp.concatenate(parts, axis=axis)
-    anywhere = pl.BlockSpec(memory_space=pl.ANY)
+    cuts = 4
+    if axis == 0:
+        block = (size, shape[1] // cuts)
+        wide = (2 * size, shape[1] // cuts)
+        place = lambda cut, at: (at, cut)
+    else:
+        block = (shape[0] // cuts, size)
+        wide = (shape[0] // cuts, 2 * size)
+        place = lambda cut, at: (cut, at)
     return pl.pallas_call(
-        functools.partial(merge_kernel, size, count, axis),
-        in_specs=[anywhere, anywhere],
-        out_specs=anywhere,
+        functools.partial(merge_kernel, axis),
+        grid=(cuts, count),
+        in_specs=[pl.BlockSpec(block, place)] * 2,
+        out_specs=pl.BlockSpec(wide, place),
         out_shape=jax.ShapeDtypeStruct(tuple(shape), first.dtype),
-        scratch_shapes=[pltpu.SemaphoreType.DMA((2 * count,))],
+        compiler_params=pltpu.CompilerParams(vmem_limit_bytes=24 * 2**20),
         cost_estimate=pl.CostEstimate(
             flops=0, bytes_accessed=8 * first.size, transcendentals=0
         ),
@@ -524,39 +524,59 @@
         other = swap(jnp.where(core_one, first, second).astype(BF16), core_mask).astype(F32)
         return jnp.where(core_one, other, mine), jnp.where(core_one, mine, other)
 
-    first_blocks, first_rests = zip(*[(found[0], found[1:]) for found in blocks_of(0, 0)])
-    (
-        first_blocks,
-        tokens_in,
-        segment_ids,
-        qkv_weight,
-        qv_bias,
-        out_weight,
-        up_weight,
-        up_bias,
-        down_weight,
-        row_params,
-    ) = lax.optimization_barrier(
+    steps = len(orders[0])
+
+    def fetches_of(blocks):
+        return [Fetch(block, axis, order, outer) for block, axis, order, outer in blocks]
+
+    early = fetches_of(blocks_of(0, 0))
+    for chain in early:
+        chain.send()
+    others, rest = lax.optimization_barrier(
         (
-            first_blocks,
-            tokens_in,
-            segment_ids,
-            qkv_weight,
-            qv_bias,
-            out_weight,
-            up_weight,
-            up_bias,
-            down_weight,
-            row_params,
+            [chain.other for chain in early],
+            (tokens_in, segment_ids, out_weight, qkv_weight, up_weight, down_weight),
         )
     )
-
-    small_local = jnp.concatenate(
+    for chain, other in zip(early, others):
+        chain.other = other
+    tokens_in, segment_ids, out_weight, qkv_weight, up_weight, down_weight = rest
+    small = jnp.concatenate(
         [row_params.reshape(-1), qv_bias.reshape(-1), up_bias.reshape(-1)]
     )[None]
-    small = small_local
-    for mask in bits_of(devices):
-        small = ordered(small, mask, (dp_at * tensor_size + tensor_at) & mask != 0, 0)
+
+    def small_hop(values, mask):
+        return ordered(values, mask, (dp_at * tensor_size + tensor_at) & mask != 0, 0)
+
+    small_hops = bits_of(devices)
+    small = small_hop(small, small_hops[0])
+    small = tick(small, early)
+    tokens_here = cross(tokens_in)
+    first_stage = fetches_of(blocks_of(0, 1))
+    next_fetches = []
+    if layers > 1:
+        next_fetches = fetches_of(blocks_of(1, 0))
+    first_stage = first_stage + next_fetches
+    small = small_hop(small, small_hops[1])
+    small, tokens_here, first_blocks = tick(
+        (small, tokens_here, [chain.block for chain in first_stage]), early
+    )
+    for chain, block in zip(first_stage, first_blocks):
+        chain.block = block
+        chain.send()
+    stream = group_rows(tokens_here)
+    small = small_hop(small, small_hops[2])
+    small, stream = tick((small, stream), early)
+    stream = to_local(stream).astype(F32)
+    for mask in small_hops[3:]:
+        small = small_hop(small, mask)
+    later_others, small = tick(([chain.other for chain in first_stage], small), early)
+    for chain, other in zip(first_stage, later_others):
+        chain.other = other
+    while early[0].place < steps:
+        for chain in early:
+            chain.take()
+
     row_size, qv_size = row_params.size, qv_bias.size
     rows_every = to_local(
         small[:, :row_size]
@@ -588,25 +608,16 @@
     seg_row = jnp.where(core == span % 2, own_segment, swap(own_segment, core_mask))
     seg_col = seg_row.reshape(-1, 1)
 
-    steps = len(orders[0])
-
-    def fetches_of(blocks):
-        return [Fetch(block, axis, order, outer) for block, axis, order, outer in blocks]
-
-    stages = [fetches_of([(block, *rest) for block, rest in zip(first_blocks, first_rests)])]
-    for chain in stages[0]:
-        chain.send()
-    fetches = [stages[0]]
-    for number in range(layers):
+    fetches = [early + first_stage[:2], first_stage[2:]]
+    stages = [early, first_stage]
+    for number in range(1, layers):
         late = fetches_of(blocks_of(number, 1))
         fetches[number] = fetches[number] + late
         if number + 1 < layers:
             fetches.append(fetches_of(blocks_of(number + 1, 0)))
             late = late + fetches[number + 1]
         stages.append(late)
-    for chain in stages[0]:
-        chain.take()
-    for before, after in zip(stages[:-1], stages[1:]):
+    for before, after in zip(stages[1:-1], stages[2:]):
         held = lax.optimization_barrier(
             ([chain.other for chain in before], [chain.block for chain in after])
         )
@@ -615,11 +626,6 @@
         for chain, block in zip(after, held[1]):
             chain.block = block
             chain.send()
-    while stages[0][0].place < steps:
-        for chain in stages[0]:
-            chain.take()
-
-    stream = to_local(group_rows(cross(tokens_in))).astype(F32)
 
     stash = []
     normed = layer_norm(stream, rows_every[0, 0], rows_every[0, 1]).astype(BF16)

time: 1400 us -> 900 us (0.64)
  Pallas kernels: 604 us -> 102 us
  local copies, waits for them, and re-layouts: 85.6 us -> 100 us
    pallas_call x4, Pallas kernels: 513 us -> 10.9 us  [merge(): pl.pallas_call(functools.partial(merge_kernel, axis), grid=(cuts, count),...]
    unnamed x449 -> x529, local copies, waits for them, and re-layouts: 24.2 us -> 33.5 us
  transfers between devices with their start and end apart: 121 -> 121, of which waited for: 44 -> 38; matrix products, arithmetic and copies ran while one was open for 22% -> 35% of each run, Pallas kernels for 34% -> 11%
where the time goes in v3:
time: 900 us; the launch traced here: 890 us
  waiting for transfers between devices  249 us (28%)
  starting transfers between devices  162 us (18%)
  matrix products  138 us (15%)
  other arithmetic  133 us (15%)
  Pallas kernels  102 us (11%)
  local copies, waits for them, and re-layouts  100 us (11%)
    ppermute x117, waiting for transfers between devices, swap(): lax.ppermute(values, BOTH, [(at, at ^ mask) for at in range(devices)])  249 us
    ppermute x117, starting transfers between devices, swap(): lax.ppermute(values, BOTH, [(at, at ^ mask) for at in range(devices)])  139 us
    pallas_call x2, Pallas kernels, attention_backward(): pl.pallas_call(backward_kernel, grid=(groups,), in_specs=[pl.BlockSpec(me...  55 us
    dot_general x10, matrix products, dot_nt(): lax.dot_general(left, right, (((1,), (1,)), ((), ())), preferred_element_...  49.1 us
    dot_general x20, matrix products, dot_tn(): lax.dot_general(left, right, (((0,), (0,)), ((), ())), preferred_element_...  47.8 us
    pallas_call x2, Pallas kernels, attention_forward(): pl.pallas_call(forward_kernel, grid=(groups,), in_specs=[pl.BlockSpec(mem...  36.5 us
    unnamed x529, local copies, waits for them, and re-layouts  33.5 us
    convert_element_type x40, other arithmetic, take(): (first.astype(F32) + second.astype(F32)).astype(BF16)  31.3 us
  transfers between devices with their start and end apart: 121, of which 38 were waited for; matrix products, arithmetic and copies ran while one was open for 35% of the time, Pallas kernels for 11%

profile of v3, /device:TPU:9, one launch (start us, length us, event | category | flops | bytes accessed | tf_op | source)
XLA Modules:
  0.0 889.8 jit_solution(18407834016305409141)
XLA Ops:
  13.4 5.7 collective-permute-done.2
  65.0 4.5 collective-permute-start.25
  75.8 4.4 collective-permute-done.26
  82.0 11.7 %collective-permute-done.28 = bf16[16,768]{1,0:T(8,128)(2,1)S(1)} collective-permute-done((bf16[16,768]{1,0:T(8,128)(2,1)S(1)}, bf16[16,768]{1,0:T(8,128)(2,1)S(1)}, u32[]{:S(2)}, u32[]{:S(2)}) %collective-permute-start.28) | collective-permute-done | bytes 24608 | tf_op jit(solution)/shard_map/ppermute | solution.py:341
  96.7 10.1 %collective-permute-done.24 = bf16[512,256]{1,0:T(8,128)(2,1)S(1)} collective-permute-done((bf16[512,256]{1,0:T(8,128)(2,1)S(1)}, bf16[512,256]{1,0:T(8,128)(2,1)S(1)}, u32[]{:S(2)}, u32[]{:S(2)}) %collective-permute-start.24) | collective-permute-done | bytes 262176 | tf_op jit(solution)/shard_map/ppermute | solution.py:341
  127.5 18.2 %shard_map.169 = bf16[1024,512]{1,0:T(8,128)(2,1)S(1)} custom-call(f32[4,2]{1,0:T(4,128)S(1)} %multiply_power_fusion.slopes, bf16[1024,512]{1,0:T(8,128)(2,1)S(1)} %add_convert_fusion.15.query_in, bf16[1024,512]{1,0:T(8,128)(2,1)S(1)} %convolution_convert_fusion.18.key_in, bf16[1024,512]{1,0:T(8,128)(2,1)S(1)} %add_convert_fusion.14.value_in, ...), custom_call_target="tpu_custom_call" | custom-call | flops 10737418240 | bytes 4194304 | tf_op jit(solution)/shard_map/pallas_call | solution.py:170
  154.4 5.2 fusion.156
  162.3 14.5 %collective-permute-done.44 = bf16[256,512]{1,0:T(8,128)(2,1)S(1)} collective-permute-done((bf16[256,512]{1,0:T(8,128)(2,1)S(1)}, bf16[256,512]{1,0:T(8,128)(2,1)S(1)}, u32[]{:S(2)}, u32[]{:S(2)}) %collective-permute-start.44) | collective-permute-done | bytes 262176 | tf_op jit(solution)/shard_map/ppermute | solution.py:341
  194.4 38.3 %collective-permute-done.48 = bf16[256,1024]{1,0:T(8,128)(2,1)S(1)} collective-permute-done((bf16[256,1024]{1,0:T(8,128)(2,1)S(1)}, bf16[256,1024]{1,0:T(8,128)(2,1)S(1)}, u32[]{:S(2)}, u32[]{:S(2)}) %collective-permute-start.48) | collective-permute-done | bytes 524320 | tf_op jit(solution)/shard_map/ppermute | solution.py:341
  249.8 6.1 shard_map.171
  258.9 9.0 %multiply_convert_fusion.1 = (bf16[1024,2048]{1,0:T(8,128)(2,1)S(1)}, f32[1024,2048]{1,0:T(8,128)}) fusion(f32[2048]{0:T(1024)S(1)} %bitcast.265, bf16[1024,1024]{0,1:T(8,128)(2,1)S(1)} %copy-done.53, bf16[1024,2048]{1,0:T(8,128)(2,1)S(1)} %shard_map.170), kind=kOutput, calls=%fused_computation.17 | convolution fusion | flops 4315938816 | bytes 18882560 | tf_op jit(solution)/shard_map/dot_general | solution.py:673
  270.1 5.8 convolution_convert_fusion.12
  281.6 9.5 %collective-permute-start.61 = (bf16[512,1024]{0,1:T(8,128)(2,1)}, bf16[512,1024]{0,1:T(8,128)(2,1)}, u32[]{:S(2)}, u32[]{:S(2)}) collective-permute-start(bf16[512,1024]{0,1:T(8,128)(2,1)} %copy.56), channel_id=1, source_target_pairs={{0,0},{1,4},{2,2},{3,6},{4,1},{5,5},{6,3},{7,7},{8,8},{9,12},{10,1... | collective-permute-start | bytes 3145736 | tf_op jit(solution)/shard_map/ppermute | solution.py:349
  292.6 5.6 collective-permute-start.62
  305.0 18.1 %collective-permute-done.54 = bf16[512,1024]{1,0:T(8,128)(2,1)S(1)} collective-permute-done((bf16[512,1024]{1,0:T(8,128)(2,1)S(1)}, bf16[512,1024]{1,0:T(8,128)(2,1)S(1)}, u32[]{:S(2)}, u32[]{:S(2)}) %collective-permute-start.54) | collective-permute-done | bytes 1048608 | tf_op jit(solution)/shard_map/ppermute | solution.py:341
  323.1 4.0 add_convert_fusion.query_in.key_in.value_in
  327.1 18.3 %shard_map.172 = bf16[1024,512]{1,0:T(8,128)(2,1)S(1)} custom-call(f32[4,2]{1,0:T(4,128)S(1)} %multiply_power_fusion.slopes, bf16[1024,1536]{1,0:T(8,128)(2,1)S(1)} %add_convert_fusion.query_in.key_in.value_in, bf16[1024,1536]{1,0:T(8,128)(2,1)S(1)} %add_convert_fusion.query_in.key_in.value_in, ...), custom_call_target="tpu_custom_call" | custom-call | flops 10737418240 | bytes 4194304 | tf_op jit(solution)/shard_map/pallas_call | solution.py:170
  356.8 39.1 %collective-permute-done.57.second = bf16[512,2048]{1,0:T(8,128)(2,1)S(1)} collective-permute-done((bf16[512,2048]{1,0:T(8,128)(2,1)S(1)}, bf16[512,2048]{1,0:T(8,128)(2,1)S(1)}, u32[]{:S(2)}, u32[]{:S(2)}) %collective-permute-start.57) | collective-permute-done | bytes 2097184 | tf_op jit(solution)/shard_map/ppermute | solution.py:341
  398.3 9.9 %multiply_convert_fusion = (bf16[1024,2048]{1,0:T(8,128)(2,1)}, f32[1024,2048]{1,0:T(8,128)}) fusion(f32[2048]{0:T(1024)S(1)} %bitcast.267, bf16[1024,1024]{0,1:T(8,128)(2,1)S(1)} %add_convert_fusion.3, bf16[1024,2048]{1,0:T(8,128)(2,1)S(1)} %shard_map.173), kind=kOutput, calls=%fused_computation.16 | convolution fusion | flops 4315938816 | bytes 18882560 | tf_op jit(solution)/shard_map/dot_general | solution.py:673
  409.3 12.2 %fusion.205 = (f32[2048]{0:T(1024)S(1)}, bf16[1024,2048]{1,0:T(8,128)(2,1)S(1)}) fusion(f32[1024,2048]{1,0:T(8,128)} %get-tuple-element.660, f32[2048]{0:T(1024)S(1)} %bitcast.268, bf16[2048,1024]{1,0:T(8,128)(2,1)S(1)} %shard_map.174, bf16[1024,256]{0,1:T(8,128)(2,1)S(1)} %get-tuple-element.389, bf16[1024,256]{0,1:T(8,128)(2,1)S(1)} %get-tuple-element.388, ...), kind=kOutput, calls=%fused_computation.635 | convolution fusion | flops 4349491200 | bytes 18890752 | tf_op jit(solution)/shard_map/dot_general | solution.py:23
  421.5 4.8 convolution_convert_fusion.9
  427.1 6.2 convolution_convert_fusion.10
  440.7 3.7 convolution_convert_fusion.7
  449.8 4.7 convolution_convert_fusion.6
  454.6 4.4 multiply_reduce_fusion
  459.0 7.0 fusion.153
  467.3 9.6 %collective-permute-start.60 = (bf16[512,1024]{0,1:T(8,128)(2,1)}, bf16[512,1024]{0,1:T(8,128)(2,1)}, u32[]{:S(2)}, u32[]{:S(2)}) collective-permute-start(bf16[512,1024]{0,1:T(8,128)(2,1)} %fusion.49), channel_id=1, source_target_pairs={{0,0},{1,4},{2,2},{3,6},{4,1},{5,5},{6,3},{7,7},{8,8},{9,12},{10,1... | collective-permute-start | bytes 3145736 | tf_op jit(solution)/shard_map/ppermute | solution.py:349
  478.2 13.3 %collective-permute-done.64 = bf16[2048,512]{1,0:T(8,128)(2,1)} collective-permute-done((bf16[2048,512]{1,0:T(8,128)(2,1)}, bf16[2048,512]{1,0:T(8,128)(2,1)}, u32[]{:S(2)}, u32[]{:S(2)}) %collective-permute-start.64) | collective-permute-done | bytes 2097184 | tf_op jit(solution)/shard_map/ppermute | solution.py:341
  491.5 27.4 %shard_map.175 = (bf16[3,1024,512]{2,1,0:T(8,128)(2,1)S(1)}, f32[4,2,128]{2,1,0:T(2,128)S(1)}) custom-call(f32[4,2]{1,0:T(4,128)S(1)} %multiply_power_fusion.slopes, bf16[1024,1536]{1,0:T(8,128)(2,1)} %copy-done.13, bf16[1024,1536]{1,0:T(8,128)(2,1)} %copy-done.13, bf16[1024,1536]{1,0:T(8,128)(2,1)} %copy-done.13, ...), custom_call_target="tpu_custom_call" | custom-call | flops 17179869184 | bytes 7340032 | tf_op jit(solution)/shard_map/pallas_call | solution.py:196
  532.3 5.0 collective-permute-done.67
  537.2 8.8 collective-permute-done.65
  547.9 3.9 fusion.41
  578.9 4.4 multiply_reduce_fusion.1
  586.9 6.5 collective-permute-done.70
  595.9 12.3 %fusion.151 = (f32[2048]{0:T(1024)}, bf16[1024,2048]{1,0:T(8,128)(2,1)}) fusion(f32[1024,2048]{1,0:T(8,128)S(1)} %bitcast.276, f32[2048]{0:T(1024)S(1)} %bitcast.266, bf16[1024,1024]{0,1:T(8,128)(2,1)S(1)} %convert_element_type.951, bf16[2048,1024]{1,0:T(8,128)(2,1)S(1)} %copy-done.2), kind=kOutput, calls=%fused_computation.582 | convolution fusion | flops 4341102592 | bytes 18890752 | tf_op jit(solution)/shard_map/dot_general | solution.py:23
  616.6 3.8 convolution_convert_fusion.3
  620.7 3.8 convolution_convert_fusion.2
  633.3 8.0 convolution_convert_fusion.8
  661.9 24.9 %collective-permute-done.79 = bf16[512,768]{1,0:T(8,128)(2,1)S(1)} collective-permute-done((bf16[512,768]{1,0:T(8,128)(2,1)S(1)}, bf16[512,768]{1,0:T(8,128)(2,1)S(1)}, u32[]{:S(2)}, u32[]{:S(2)}) %collective-permute-start.79) | collective-permute-done | bytes 786464 | tf_op jit(solution)/shard_map/ppermute | solution.py:341
  706.9 9.0 %collective-permute-done.80 = bf16[256,768]{1,0:T(8,128)(2,1)S(1)} collective-permute-done((bf16[256,768]{1,0:T(8,128)(2,1)S(1)}, bf16[256,768]{1,0:T(8,128)(2,1)S(1)}, u32[]{:S(2)}, u32[]{:S(2)}) %collective-permute-start.80) | collective-permute-done | bytes 393248 | tf_op jit(solution)/shard_map/ppermute | solution.py:341
  718.0 27.6 %shard_map.176 = (bf16[3,1024,512]{2,1,0:T(8,128)(2,1)}, f32[4,2,128]{2,1,0:T(2,128)S(1)}) custom-call(f32[4,2]{1,0:T(4,128)S(1)} %multiply_power_fusion.slopes, bf16[1024,512]{1,0:T(8,128)(2,1)S(1)} %copy-done.10, bf16[1024,512]{1,0:T(8,128)(2,1)S(1)} %copy-done.12, bf16[1024,512]{1,0:T(8,128)(2,1)S(1)} %copy-done.8, ...), custom_call_target="tpu_custom_call" | custom-call | flops 17179869184 | bytes 7340032 | tf_op jit(solution)/shard_map/pallas_call | solution.py:196
  748.9 6.9 collective-permute-done.82
  790.8 5.8 fusion.24
  805.1 6.7 fusion.23
  833.4 4.9 collective-permute-done.103
  844.4 5.6 collective-permute-start.120
  851.4 3.8 collective-permute-done.108
  871.0 8.4 collective-permute-start.119
  (1087 shorter events, 393.1 us)
Async XLA Ops:
  26.3 25.3 %collective-permute-start.8 = (bf16[512,1024]{0,1:T(8,128)(2,1)}, bf16[512,1024]{0,1:T(8,128)(2,1)S(1)}, u32[]{:S(2)}, u32[]{:S(2)}) collective-permute-start(bf16[512,1024]{0,1:T(8,128)(2,1)} %copy.44), channel_id=1, source_target_pairs={{0,0},{1,4},{2,2},{3,6},{4,1},{5,5},{6,3},{7,7},{8,8},{9,12},{10,1... | collective-permute-start | bytes 3145736 | tf_op jit(solution)/shard_map/ppermute | solution.py:349
  51.6 30.0 %collective-permute-start.23 = (bf16[256,512]{1,0:T(8,128)(2,1)S(1)}, bf16[256,512]{1,0:T(8,128)(2,1)S(1)}, u32[]{:S(2)}, u32[]{:S(2)}) collective-permute-start(bf16[256,512]{1,0:T(8,128)(2,1)S(1)} %pad_maximum_fusion.31), channel_id=1, source_target_pairs={{0,2},{1,3},{2,0},{3,1},{4,6},{5,7},{6,4},{7,5},{8,10},{9,11},{10,... | collective-permute-start | bytes 786440 | tf_op jit(solution)/shard_map/ppermute | solution.py:341
  70.7 36.2 %collective-permute-start.31 = (bf16[1024,256]{1,0:T(8,128)(2,1)S(1)}, bf16[1024,256]{1,0:T(8,128)(2,1)S(1)}, u32[]{:S(2)}, u32[]{:S(2)}) collective-permute-start(bf16[1024,256]{1,0:T(8,128)(2,1)S(1)} %pad_maximum_fusion.23), channel_id=1, source_target_pairs={{0,1},{1,0},{2,3},{3,2},{4,5},{5,4},{6,7},{7,6},{8,9},{9,8},{10,11... | collective-permute-start | bytes 1572872 | tf_op jit(solution)/shard_map/ppermute | solution.py:341
  74.8 32.1 %collective-permute-start.32 = (bf16[256,1024]{1,0:T(8,128)(2,1)S(1)}, bf16[256,1024]{1,0:T(8,128)(2,1)S(1)}, u32[]{:S(2)}, u32[]{:S(2)}) collective-permute-start(bf16[256,1024]{1,0:T(8,128)(2,1)S(1)} %pad_maximum_fusion.24), channel_id=1, source_target_pairs={{0,1},{1,0},{2,3},{3,2},{4,5},{5,4},{6,7},{7,6},{8,9},{9,8},{10,11... | collective-permute-start | bytes 1572872 | tf_op jit(solution)/shard_map/ppermute | solution.py:341
  80.2 26.7 %collective-permute-start.29 = (bf16[512,512]{1,0:T(8,128)(2,1)S(1)}, bf16[512,512]{1,0:T(8,128)(2,1)S(1)}, u32[]{:S(2)}, u32[]{:S(2)}) collective-permute-start(bf16[512,512]{1,0:T(8,128)(2,1)S(1)} %pad_maximum_fusion.21), channel_id=1, source_target_pairs={{0,16},{1,17},{2,18},{3,19},{4,20},{5,21},{6,22},{7,23},{8,24},{9,... | collective-permute-start | bytes 1572872 | tf_op jit(solution)/shard_map/ppermute | solution.py:341
  81.4 25.5 %collective-permute-start.30 = (bf16[512,512]{1,0:T(8,128)(2,1)S(1)}, bf16[512,512]{1,0:T(8,128)(2,1)S(1)}, u32[]{:S(2)}, u32[]{:S(2)}) collective-permute-start(bf16[512,512]{1,0:T(8,128)(2,1)S(1)} %pad_maximum_fusion.22), channel_id=1, source_target_pairs={{0,8},{1,9},{2,10},{3,11},{4,12},{5,13},{6,14},{7,15},{8,0},{9,1},... | collective-permute-start | bytes 1572872 | tf_op jit(solution)/shard_map/ppermute | solution.py:341
  149.9 26.9 %collective-permute-start.41 = (bf16[512,1024]{1,0:T(8,128)(2,1)S(1)}, bf16[512,1024]{1,0:T(8,128)(2,1)S(1)}, u32[]{:S(2)}, u32[]{:S(2)}) collective-permute-start(bf16[512,1024]{1,0:T(8,128)(2,1)S(1)} %pad_maximum_fusion.8), channel_id=1, source_target_pairs={{0,1},{1,0},{2,3},{3,2},{4,5},{5,4},{6,7},{7,6},{8,9},{9,8},{10,11... | collective-permute-start | bytes 3145736 | tf_op jit(solution)/shard_map/ppermute | solution.py:341
  151.3 25.5 %collective-permute-start.42 = (bf16[2048,256]{1,0:T(8,128)(2,1)S(1)}, bf16[2048,256]{1,0:T(8,128)(2,1)S(1)}, u32[]{:S(2)}, u32[]{:S(2)}) collective-permute-start(bf16[2048,256]{1,0:T(8,128)(2,1)S(1)} %pad_maximum_fusion.14), channel_id=1, source_target_pairs={{0,16},{1,17},{2,18},{3,19},{4,20},{5,21},{6,22},{7,23},{8,24},{9,... | collective-permute-start | bytes 3145736 | tf_op jit(solution)/shard_map/ppermute | solution.py:341
  152.6 24.2 %collective-permute-start.43 = (bf16[512,768]{1,0:T(8,128)(2,1)S(1)}, bf16[512,768]{1,0:T(8,128)(2,1)S(1)}, u32[]{:S(2)}, u32[]{:S(2)}) collective-permute-start(bf16[512,768]{1,0:T(8,128)(2,1)S(1)} %pad_maximum_fusion.19), channel_id=1, source_target_pairs={{0,8},{1,9},{2,10},{3,11},{4,12},{5,13},{6,14},{7,15},{8,0},{9,1},... | collective-permute-start | bytes 2359304 | tf_op jit(solution)/shard_map/ppermute | solution.py:341
  153.9 22.9 %collective-permute-start.44 = (bf16[256,512]{1,0:T(8,128)(2,1)S(1)}, bf16[256,512]{1,0:T(8,128)(2,1)S(1)}, u32[]{:S(2)}, u32[]{:S(2)}) collective-permute-start(bf16[256,512]{1,0:T(8,128)(2,1)S(1)} %pad_maximum_fusion.39), channel_id=1, source_target_pairs={{0,8},{1,9},{2,10},{3,11},{4,12},{5,13},{6,14},{7,15},{8,0},{9,1},... | collective-permute-start | bytes 786440 | tf_op jit(solution)/shard_map/ppermute | solution.py:341
  177.5 58.3 %collective-permute-start.45 = (bf16[512,2048]{1,0:T(8,128)(2,1)S(1)}, bf16[512,2048]{1,0:T(8,128)(2,1)}, u32[]{:S(2)}, u32[]{:S(2)}) collective-permute-start(bf16[512,2048]{1,0:T(8,128)(2,1)S(1)} %pad_maximum_fusion.2.first), channel_id=1, source_target_pairs={{0,16},{1,17},{2,18},{3,19},{4,20},{5,21},{6,22},{7,23},{8,24},{9,... | collective-permute-start | bytes 6291464 | tf_op jit(solution)/shard_map/ppermute | solution.py:341
  179.3 56.5 %collective-permute-start.46 = (bf16[2048,512]{1,0:T(8,128)(2,1)}, bf16[2048,512]{1,0:T(8,128)(2,1)}, u32[]{:S(2)}, u32[]{:S(2)}) collective-permute-start(bf16[2048,512]{1,0:T(8,128)(2,1)} %pad_maximum_fusion.3.first), channel_id=1, source_target_pairs={{0,8},{1,9},{2,10},{3,11},{4,12},{5,13},{6,14},{7,15},{8,0},{9,1},... | collective-permute-start | bytes 6291464 | tf_op jit(solution)/shard_map/ppermute | solution.py:341
  181.7 54.0 %collective-permute-start.47 = (bf16[1024,768]{1,0:T(8,128)(2,1)}, bf16[1024,768]{1,0:T(8,128)(2,1)}, u32[]{:S(2)}, u32[]{:S(2)}) collective-permute-start(bf16[1024,768]{1,0:T(8,128)(2,1)} %pad_maximum_fusion.7), channel_id=1, source_target_pairs={{0,1},{1,0},{2,3},{3,2},{4,5},{5,4},{6,7},{7,6},{8,9},{9,8},{10,11... | collective-permute-start | bytes 4718600 | tf_op jit(solution)/shard_map/ppermute | solution.py:341
  185.1 72.0 %collective-permute-start.49 = (bf16[256,512]{1,0:T(8,128)(2,1)}, bf16[256,512]{1,0:T(8,128)(2,1)S(1)}, u32[]{:S(2)}, u32[]{:S(2)}) collective-permute-start(bf16[256,512]{1,0:T(8,128)(2,1)} %pad_maximum_fusion.37), channel_id=1, source_target_pairs={{0,2},{1,3},{2,0},{3,1},{4,6},{5,7},{6,4},{7,5},{8,10},{9,11},{10,... | collective-permute-start | bytes 786440 | tf_op jit(solution)/shard_map/ppermute | solution.py:341
  190.8 41.8 %collective-permute-start.48 = (bf16[256,1024]{1,0:T(8,128)(2,1)S(1)}, bf16[256,1024]{1,0:T(8,128)(2,1)S(1)}, u32[]{:S(2)}, u32[]{:S(2)}) collective-permute-start(bf16[256,1024]{1,0:T(8,128)(2,1)S(1)} %pad_maximum_fusion.26), channel_id=1, source_target_pairs={{0,1},{1,0},{2,3},{3,2},{4,5},{5,4},{6,7},{7,6},{8,9},{9,8},{10,11... | collective-permute-start | bytes 1572872 | tf_op jit(solution)/shard_map/ppermute | solution.py:341
  232.7 24.5 %collective-permute-start.50 = (bf16[512,256]{1,0:T(8,128)(2,1)S(1)}, bf16[512,256]{1,0:T(8,128)(2,1)S(1)}, u32[]{:S(2)}, u32[]{:S(2)}) collective-permute-start(bf16[512,256]{1,0:T(8,128)(2,1)S(1)} %pad_maximum_fusion.38), channel_id=1, source_target_pairs={{0,2},{1,3},{2,0},{3,1},{4,6},{5,7},{6,4},{7,5},{8,10},{9,11},{10,... | collective-permute-start | bytes 786440 | tf_op jit(solution)/shard_map/ppermute | solution.py:341
  275.9 24.2 %collective-permute-start.53 = (bf16[1024,1024]{0,1:T(8,128)(2,1)}, bf16[1024,1024]{0,1:T(8,128)(2,1)}, u32[]{:S(2)}, u32[]{:S(2)}) collective-permute-start(bf16[1024,1024]{0,1:T(8,128)(2,1)} %convolution_convert_fusion.12), channel_id=1, source_target_pairs={{0,4},{1,5},{2,6},{3,7},{4,0},{5,1},{6,2},{7,3},{8,12},{9,13},{10,... | collective-permute-start | bytes 6291464 | tf_op jit(solution)/shard_map/ppermute | solution.py:341
  292.6 58.3 %collective-permute-start.62 = (bf16[512,1024]{0,1:T(8,128)(2,1)}, bf16[512,1024]{0,1:T(8,128)(2,1)S(1)}, u32[]{:S(2)}, u32[]{:S(2)}) collective-permute-start(bf16[512,1024]{0,1:T(8,128)(2,1)} %collective-permute-done.61), channel_id=1, source_target_pairs={{0,4},{1,5},{2,6},{3,7},{4,0},{5,1},{6,2},{7,3},{8,12},{9,13},{10,... | collective-permute-start | bytes 3145736 | tf_op jit(solution)/shard_map/ppermute | solution.py:341
  298.3 24.8 %collective-permute-start.54 = (bf16[512,1024]{1,0:T(8,128)(2,1)S(1)}, bf16[512,1024]{1,0:T(8,128)(2,1)S(1)}, u32[]{:S(2)}, u32[]{:S(2)}) collective-permute-start(bf16[512,1024]{1,0:T(8,128)(2,1)S(1)} %pad_maximum_fusion.9), channel_id=1, source_target_pairs={{0,1},{1,0},{2,3},{3,2},{4,5},{5,4},{6,7},{7,6},{8,9},{9,8},{10,11... | collective-permute-start | bytes 3145736 | tf_op jit(solution)/shard_map/ppermute | solution.py:341
  298.9 24.2 %collective-permute-start.55 = (bf16[2048,256]{1,0:T(8,128)(2,1)S(1)}, bf16[2048,256]{1,0:T(8,128)(2,1)S(1)}, u32[]{:S(2)}, u32[]{:S(2)}) collective-permute-start(bf16[2048,256]{1,0:T(8,128)(2,1)S(1)} %pad_maximum_fusion.16), channel_id=1, source_target_pairs={{0,16},{1,17},{2,18},{3,19},{4,20},{5,21},{6,22},{7,23},{8,24},{9,... | collective-permute-start | bytes 3145736 | tf_op jit(solution)/shard_map/ppermute | solution.py:341
  348.6 47.3 %collective-permute-start.57 = (bf16[512,2048]{1,0:T(8,128)(2,1)S(1)}, bf16[512,2048]{1,0:T(8,128)(2,1)S(1)}, u32[]{:S(2)}, u32[]{:S(2)}) collective-permute-start(bf16[512,2048]{1,0:T(8,128)(2,1)S(1)} %pad_maximum_fusion.4.first), channel_id=1, source_target_pairs={{0,16},{1,17},{2,18},{3,19},{4,20},{5,21},{6,22},{7,23},{8,24},{9,... | collective-permute-start | bytes 6291464 | tf_op jit(solution)/shard_map/ppermute | solution.py:341
  353.7 54.5 %collective-permute-start.58 = (bf16[2048,512]{1,0:T(8,128)(2,1)S(1)}, bf16[2048,512]{1,0:T(8,128)(2,1)S(1)}, u32[]{:S(2)}, u32[]{:S(2)}) collective-permute-start(bf16[2048,512]{1,0:T(8,128)(2,1)S(1)} %pad_maximum_fusion.5.first), channel_id=1, source_target_pairs={{0,8},{1,9},{2,10},{3,11},{4,12},{5,13},{6,14},{7,15},{8,0},{9,1},... | collective-permute-start | bytes 6291464 | tf_op jit(solution)/shard_map/ppermute | solution.py:341
  426.3 28.3 %collective-permute-start.63 = (bf16[1024,1024]{0,1:T(8,128)(2,1)S(1)}, bf16[1024,1024]{0,1:T(8,128)(2,1)}, u32[]{:S(2)}, u32[]{:S(2)}) collective-permute-start(bf16[1024,1024]{0,1:T(8,128)(2,1)S(1)} %convolution_convert_fusion.9), channel_id=1, source_target_pairs={{0,4},{1,5},{2,6},{3,7},{4,0},{5,1},{6,2},{7,3},{8,12},{9,13},{10,... | collective-permute-start | bytes 6291464 | tf_op jit(solution)/shard_map/ppermute | solution.py:341
  437.0 22.0 %collective-permute-start.59 = (bf16[1024,1024]{0,1:T(8,128)(2,1)}, bf16[1024,1024]{0,1:T(8,128)(2,1)}, u32[]{:S(2)}, u32[]{:S(2)}) collective-permute-start(bf16[1024,1024]{0,1:T(8,128)(2,1)} %convolution_convert_fusion.10), channel_id=1, source_target_pairs={{0,4},{1,5},{2,6},{3,7},{4,0},{5,1},{6,2},{7,3},{8,12},{9,13},{10,... | collective-permute-start | bytes 6291464 | tf_op jit(solution)/shard_map/ppermute | solution.py:341
  444.4 47.0 %collective-permute-start.64 = (bf16[2048,512]{1,0:T(8,128)(2,1)}, bf16[2048,512]{1,0:T(8,128)(2,1)}, u32[]{:S(2)}, u32[]{:S(2)}) collective-permute-start(bf16[2048,512]{1,0:T(8,128)(2,1)} %convolution_convert_fusion.7), channel_id=1, source_target_pairs={{0,8},{1,9},{2,10},{3,11},{4,12},{5,13},{6,14},{7,15},{8,0},{9,1},... | collective-permute-start | bytes 6291464 | tf_op jit(solution)/shard_map/ppermute | solution.py:341
  445.6 86.7 %collective-permute-start.66 = (bf16[512,2048]{1,0:T(8,128)(2,1)}, bf16[512,2048]{1,0:T(8,128)(2,1)}, u32[]{:S(2)}, u32[]{:S(2)}) collective-permute-start(bf16[512,2048]{1,0:T(8,128)(2,1)} %convolution_convert_fusion.5), channel_id=1, source_target_pairs={{0,16},{1,17},{2,18},{3,19},{4,20},{5,21},{6,22},{7,23},{8,24},{9,... | collective-permute-start | bytes 6291464 | tf_op jit(solution)/shard_map/ppermute | solution.py:341
  467.3 102.6 %collective-permute-start.60 = (bf16[512,1024]{0,1:T(8,128)(2,1)}, bf16[512,1024]{0,1:T(8,128)(2,1)}, u32[]{:S(2)}, u32[]{:S(2)}) collective-permute-start(bf16[512,1024]{0,1:T(8,128)(2,1)} %fusion.49), channel_id=1, source_target_pairs={{0,0},{1,4},{2,2},{3,6},{4,1},{5,5},{6,3},{7,7},{8,8},{9,12},{10,1... | collective-permute-start | bytes 3145736 | tf_op jit(solution)/shard_map/ppermute | solution.py:349
  522.3 23.7 %collective-permute-start.65 = (bf16[2048,256]{1,0:T(8,128)(2,1)}, bf16[2048,256]{1,0:T(8,128)(2,1)}, u32[]{:S(2)}, u32[]{:S(2)}) collective-permute-start(bf16[2048,256]{1,0:T(8,128)(2,1)} %get-tuple-element.349), channel_id=1, source_target_pairs={{0,16},{1,17},{2,18},{3,19},{4,20},{5,21},{6,22},{7,23},{8,24},{9,... | collective-permute-start | bytes 3145736 | tf_op jit(solution)/shard_map/ppermute | solution.py:341
  551.8 27.1 %collective-permute-start.68 = (bf16[1024,1024]{0,1:T(8,128)(2,1)S(1)}, bf16[1024,1024]{0,1:T(8,128)(2,1)}, u32[]{:S(2)}, u32[]{:S(2)}) collective-permute-start(bf16[1024,1024]{0,1:T(8,128)(2,1)S(1)} %fusion.41), channel_id=1, source_target_pairs={{0,4},{1,5},{2,6},{3,7},{4,0},{5,1},{6,2},{7,3},{8,12},{9,13},{10,... | collective-permute-start | bytes 6291464 | tf_op jit(solution)/shard_map/ppermute | solution.py:341
  557.1 29.9 %collective-permute-start.69 = (bf16[1024,256]{1,0:T(8,128)(2,1)}, bf16[1024,256]{1,0:T(8,128)(2,1)}, u32[]{:S(2)}, u32[]{:S(2)}) collective-permute-start(bf16[1024,256]{1,0:T(8,128)(2,1)} %add_convert_fusion.25), channel_id=1, source_target_pairs={{0,1},{1,0},{2,3},{3,2},{4,5},{5,4},{6,7},{7,6},{8,9},{9,8},{10,11... | collective-permute-start | bytes 1572872 | tf_op jit(solution)/shard_map/ppermute | solution.py:341
  562.1 31.3 %collective-permute-start.70 = (bf16[512,1024]{1,0:T(8,128)(2,1)}, bf16[512,1024]{1,0:T(8,128)(2,1)}, u32[]{:S(2)}, u32[]{:S(2)}) collective-permute-start(bf16[512,1024]{1,0:T(8,128)(2,1)} %add_convert_fusion.11), channel_id=1, source_target_pairs={{0,1},{1,0},{2,3},{3,2},{4,5},{5,4},{6,7},{7,6},{8,9},{9,8},{10,11... | collective-permute-start | bytes 3145736 | tf_op jit(solution)/shard_map/ppermute | solution.py:341
  565.1 21.9 %collective-permute-start.71 = (bf16[256,512]{1,0:T(8,128)(2,1)}, bf16[256,512]{1,0:T(8,128)(2,1)}, u32[]{:S(2)}, u32[]{:S(2)}) collective-permute-start(bf16[256,512]{1,0:T(8,128)(2,1)} %add_convert_fusion.45), channel_id=1, source_target_pairs={{0,8},{1,9},{2,10},{3,11},{4,12},{5,13},{6,14},{7,15},{8,0},{9,1},... | collective-permute-start | bytes 786440 | tf_op jit(solution)/shard_map/ppermute | solution.py:341
  569.9 61.6 %collective-permute-start.75 = (bf16[1024,768]{1,0:T(8,128)(2,1)}, bf16[1024,768]{1,0:T(8,128)(2,1)}, u32[]{:S(2)}, u32[]{:S(2)}) collective-permute-start(bf16[1024,768]{1,0:T(8,128)(2,1)} %convolution_convert_fusion.15), channel_id=1, source_target_pairs={{0,1},{1,0},{2,3},{3,2},{4,5},{5,4},{6,7},{7,6},{8,9},{9,8},{10,11... | collective-permute-start | bytes 4718600 | tf_op jit(solution)/shard_map/ppermute | solution.py:341
  610.1 22.3 %collective-permute-start.72 = (bf16[512,256]{1,0:T(8,128)(2,1)}, bf16[512,256]{1,0:T(8,128)(2,1)}, u32[]{:S(2)}, u32[]{:S(2)}) collective-permute-start(bf16[512,256]{1,0:T(8,128)(2,1)} %add_convert_fusion.44), channel_id=1, source_target_pairs={{0,2},{1,3},{2,0},{3,1},{4,6},{5,7},{6,4},{7,5},{8,10},{9,11},{10,... | collective-permute-start | bytes 786440 | tf_op jit(solution)/shard_map/ppermute | solution.py:341
  620.5 86.4 %collective-permute-start.81 = (bf16[2048,512]{1,0:T(8,128)(2,1)}, bf16[2048,512]{1,0:T(8,128)(2,1)S(1)}, u32[]{:S(2)}, u32[]{:S(2)}) collective-permute-start(bf16[2048,512]{1,0:T(8,128)(2,1)} %convolution_convert_fusion.3), channel_id=1, source_target_pairs={{0,8},{1,9},{2,10},{3,11},{4,12},{5,13},{6,14},{7,15},{8,0},{9,1},... | collective-permute-start | bytes 6291464 | tf_op jit(solution)/shard_map/ppermute | solution.py:341
  658.2 28.6 %collective-permute-start.79 = (bf16[512,768]{1,0:T(8,128)(2,1)S(1)}, bf16[512,768]{1,0:T(8,128)(2,1)S(1)}, u32[]{:S(2)}, u32[]{:S(2)}) collective-permute-start(bf16[512,768]{1,0:T(8,128)(2,1)S(1)} %add_convert_fusion.17), channel_id=1, source_target_pairs={{0,8},{1,9},{2,10},{3,11},{4,12},{5,13},{6,14},{7,15},{8,0},{9,1},... | collective-permute-start | bytes 2359304 | tf_op jit(solution)/shard_map/ppermute | solution.py:341
  660.4 88.5 %collective-permute-start.84 = (bf16[512,2048]{1,0:T(8,128)(2,1)}, bf16[512,2048]{1,0:T(8,128)(2,1)}, u32[]{:S(2)}, u32[]{:S(2)}) collective-permute-start(bf16[512,2048]{1,0:T(8,128)(2,1)} %convolution_convert_fusion.1), channel_id=1, source_target_pairs={{0,16},{1,17},{2,18},{3,19},{4,20},{5,21},{6,22},{7,23},{8,24},{9,... | collective-permute-start | bytes 6291464 | tf_op jit(solution)/shard_map/ppermute | solution.py:341
  689.7 26.2 %collective-permute-start.80 = (bf16[256,768]{1,0:T(8,128)(2,1)S(1)}, bf16[256,768]{1,0:T(8,128)(2,1)S(1)}, u32[]{:S(2)}, u32[]{:S(2)}) collective-permute-start(bf16[256,768]{1,0:T(8,128)(2,1)S(1)} %get-tuple-element.403), channel_id=1, source_target_pairs={{0,16},{1,17},{2,18},{3,19},{4,20},{5,21},{6,22},{7,23},{8,24},{9,... | collective-permute-start | bytes 1179656 | tf_op jit(solution)/shard_map/ppermute | solution.py:341
  695.7 53.2 %collective-permute-start.85 = (bf16[256,1024]{1,0:T(8,128)(2,1)}, bf16[256,1024]{1,0:T(8,128)(2,1)}, u32[]{:S(2)}, u32[]{:S(2)}) collective-permute-start(bf16[256,1024]{1,0:T(8,128)(2,1)} %convolution_convert_fusion.22), channel_id=1, source_target_pairs={{0,1},{1,0},{2,3},{3,2},{4,5},{5,4},{6,7},{7,6},{8,9},{9,8},{10,11... | collective-permute-start | bytes 1572872 | tf_op jit(solution)/shard_map/ppermute | solution.py:341
  717.4 38.5 %collective-permute-start.83 = (bf16[2048,256]{1,0:T(8,128)(2,1)}, bf16[2048,256]{1,0:T(8,128)(2,1)S(1)}, u32[]{:S(2)}, u32[]{:S(2)}) collective-permute-start(bf16[2048,256]{1,0:T(8,128)(2,1)} %get-tuple-element.346), channel_id=1, source_target_pairs={{0,16},{1,17},{2,18},{3,19},{4,20},{5,21},{6,22},{7,23},{8,24},{9,... | collective-permute-start | bytes 3145736 | tf_op jit(solution)/shard_map/ppermute | solution.py:341
  763.4 26.5 %collective-permute-start.86 = (bf16[1024,1024]{0,1:T(8,128)(2,1)S(1)}, bf16[1024,1024]{0,1:T(8,128)(2,1)}, u32[]{:S(2)}, u32[]{:S(2)}) collective-permute-start(bf16[1024,1024]{0,1:T(8,128)(2,1)S(1)} %add_convert_fusion.1), channel_id=1, source_target_pairs={{0,4},{1,5},{2,6},{3,7},{4,0},{5,1},{6,2},{7,3},{8,12},{9,13},{10,... | collective-permute-start | bytes 6291464 | tf_op jit(solution)/shard_map/ppermute | solution.py:341
  765.3 21.7 %collective-permute-start.87 = (bf16[128,384]{1,0:T(8,128)(2,1)S(1)}, bf16[128,384]{1,0:T(8,128)(2,1)S(1)}, u32[]{:S(2)}, u32[]{:S(2)}) collective-permute-start(bf16[128,384]{1,0:T(8,128)(2,1)S(1)} %select_convert_fusion.5), channel_id=1, source_target_pairs={{0,4},{1,5},{2,6},{3,7},{4,0},{5,1},{6,2},{7,3},{8,12},{9,13},{10,... | collective-permute-start | bytes 294920 | tf_op jit(solution)/shard_map/ppermute | solution.py:341
  766.4 45.7 %collective-permute-start.93 = (bf16[1024,256]{1,0:T(8,128)(2,1)}, bf16[1024,256]{1,0:T(8,128)(2,1)}, u32[]{:S(2)}, u32[]{:S(2)}) collective-permute-start(bf16[1024,256]{1,0:T(8,128)(2,1)} %add_convert_fusion.21), channel_id=1, source_target_pairs={{0,1},{1,0},{2,3},{3,2},{4,5},{5,4},{6,7},{7,6},{8,9},{9,8},{10,11... | collective-permute-start | bytes 1572872 | tf_op jit(solution)/shard_map/ppermute | solution.py:341
  772.0 43.7 %collective-permute-start.94 = (bf16[512,1024]{1,0:T(8,128)(2,1)}, bf16[512,1024]{1,0:T(8,128)(2,1)}, u32[]{:S(2)}, u32[]{:S(2)}) collective-permute-start(bf16[512,1024]{1,0:T(8,128)(2,1)} %add_convert_fusion.7), channel_id=1, source_target_pairs={{0,1},{1,0},{2,3},{3,2},{4,5},{5,4},{6,7},{7,6},{8,9},{9,8},{10,11... | collective-permute-start | bytes 3145736 | tf_op jit(solution)/shard_map/ppermute | solution.py:341
  773.9 29.7 %collective-permute-start.95 = (bf16[256,512]{1,0:T(8,128)(2,1)}, bf16[256,512]{1,0:T(8,128)(2,1)}, u32[]{:S(2)}, u32[]{:S(2)}) collective-permute-start(bf16[256,512]{1,0:T(8,128)(2,1)} %add_convert_fusion.39), channel_id=1, source_target_pairs={{0,8},{1,9},{2,10},{3,11},{4,12},{5,13},{6,14},{7,15},{8,0},{9,1},... | collective-permute-start | bytes 786440 | tf_op jit(solution)/shard_map/ppermute | solution.py:341
  787.0 26.3 %collective-permute-start.96 = (bf16[512,512]{1,0:T(8,128)(2,1)}, bf16[512,512]{1,0:T(8,128)(2,1)}, u32[]{:S(2)}, u32[]{:S(2)}) collective-permute-start(bf16[512,512]{1,0:T(8,128)(2,1)} %convolution_convert_fusion.27), channel_id=1, source_target_pairs={{0,16},{1,17},{2,18},{3,19},{4,20},{5,21},{6,22},{7,23},{8,24},{9,... | collective-permute-start | bytes 1572872 | tf_op jit(solution)/shard_map/ppermute | solution.py:341
  789.9 23.3 %collective-permute-start.97 = (bf16[512,512]{1,0:T(8,128)(2,1)}, bf16[512,512]{1,0:T(8,128)(2,1)}, u32[]{:S(2)}, u32[]{:S(2)}) collective-permute-start(bf16[512,512]{1,0:T(8,128)(2,1)} %convolution_convert_fusion.26), channel_id=1, source_target_pairs={{0,8},{1,9},{2,10},{3,11},{4,12},{5,13},{6,14},{7,15},{8,0},{9,1},... | collective-permute-start | bytes 1572872 | tf_op jit(solution)/shard_map/ppermute | solution.py:341
  857.6 30.1 %collective-permute-start.91 = (bf16[512,1024]{0,1:T(8,128)(2,1)}, bf16[512,1024]{0,1:T(8,128)(2,1)S(1)}, u32[]{:S(2)}, u32[]{:S(2)}) collective-permute-start(bf16[512,1024]{0,1:T(8,128)(2,1)} %fusion.46), channel_id=1, source_target_pairs={{0,0},{1,4},{2,2},{3,6},{4,1},{5,5},{6,3},{7,7},{8,8},{9,12},{10,1... | collective-permute-start | bytes 3145736 | tf_op jit(solution)/shard_map/ppermute | solution.py:349
  (320 other events, 3652.1 us)

commit v4 on v3

--- a/solution.py
+++ b/solution.py
@@ -346,7 +346,8 @@
         return at if at_core == at_span % 2 else at ^ (core_mask | inner_size)
 
     def cross(values):
-        return lax.ppermute(values, BOTH, [(at, crossed(at)) for at in range(devices)])
+        moves = [(at, crossed(at)) for at in range(devices) if at != crossed(at)]
+        return jnp.where(core == span % 2, values, lax.ppermute(values, BOTH, moves))
 
     def ordered(values, mask, is_high, axis):
         other = swap(values, mask)
@@ -722,13 +723,12 @@
         pre_low = advance(pre_low, running)
         up_chain = Reduce(normed_two, pre_low, 0, 0)
         normed_two_grad = group_sum(dot_nt(pre_low, weights[-2]))
-        normed_two_grad = advance(normed_two_grad, running)
         middle_grad, gain_two_grad, shift_two_grad = norm_back(middle, rows[3], normed_two_grad)
         middle_grad = middle_grad + upstream
         out_bias_grad = jnp.sum(middle_grad, axis=0)
         out_in = middle_grad.astype(BF16)
         attended_grad = dot_nt(out_in, weights[-3]).astype(BF16)
-        attended_grad = advance(attended_grad, running + [down_chain])
+        attended_grad = advance(attended_grad, running if number else running + [down_chain])
         out_chain = Reduce(out_in, attended, 1, 2)
         packed_grad, qv_sums = attention_backward(packed, attended_grad, seg_col, seg_row, slopes)
         packed_grad = advance(packed_grad, running + [down_chain, up_chain, out_chain])
@@ -790,6 +790,7 @@
             jnp.concatenate(join_cores(found[-1], 1), axis=0),
         )
 
+    upstream = advance(upstream, [chain for chains in reductions[1:] for chain in chains])
     weight_grads = [
         own_grads(number) if all(chain.place > steps for chain in reductions[number]) else None
         for number in range(layers)

time: 900 us -> 860 us (0.956)
  waiting for transfers between devices: 249 us -> 218 us
  starting transfers between devices: 162 us -> 152 us
    ppermute x117, waiting for transfers between devices: 249 us -> 218 us  [swap(): lax.ppermute(values, BOTH, [(at, at ^ mask) for at in range(devices)])]
    ppermute x4, starting transfers between devices: 22.8 us -> 6.6 us  [cross(): lax.ppermute(values, BOTH, moves)]
    unnamed x529 -> x589, local copies, waits for them, and re-layouts: 33.5 us -> 40.6 us
  transfers between devices with their start and end apart: 121 -> 121, of which waited for: 38 -> 34; matrix products, arithmetic and copies ran while one was open for 35% -> 36% of each run, Pallas kernels for 11% -> 12%
where the time goes in v4:
time: 860 us; the launch traced here: 849 us
  waiting for transfers between devices  218 us (25%)
  starting transfers between devices  152 us (18%)
  matrix products  142 us (17%)
  other arithmetic  127 us (15%)
  local copies, waits for them, and re-layouts  103 us (12%)
  Pallas kernels  102 us (12%)
    ppermute x117, waiting for transfers between devices, swap(): lax.ppermute(values, BOTH, [(at, at ^ mask) for at in range(devices)])  218 us
    ppermute x117, starting transfers between devices, swap(): lax.ppermute(values, BOTH, [(at, at ^ mask) for at in range(devices)])  146 us
    pallas_call x2, Pallas kernels, attention_backward(): pl.pallas_call(backward_kernel, grid=(groups,), in_specs=[pl.BlockSpec(me...  54.8 us
    dot_general x20, matrix products, dot_tn(): lax.dot_general(left, right, (((0,), (0,)), ((), ())), preferred_element_...  52.8 us
    dot_general x10, matrix products, dot_nt(): lax.dot_general(left, right, (((1,), (1,)), ((), ())), preferred_element_...  47.6 us
    unnamed x589, local copies, waits for them, and re-layouts  40.6 us
    pallas_call x2, Pallas kernels, attention_forward(): pl.pallas_call(forward_kernel, grid=(groups,), in_specs=[pl.BlockSpec(mem...  36.5 us
    slice x27, local copies, waits for them, and re-layouts, halves_of(): lax.slice_in_dim(values, (2 * at + which) * size, (2 * at + which + 1) *...  28 us
  transfers between devices with their start and end apart: 121, of which 34 were waited for; matrix products, arithmetic and copies ran while one was open for 36% of the time, Pallas kernels for 12%

profile of v4, /device:TPU:9, one launch (start us, length us, event | category | flops | bytes accessed | tf_op | source)
XLA Modules:
  0.0 849.4 jit_solution(17695795476092707836)
XLA Ops:
  13.3 5.7 collective-permute-done.2
  60.4 4.7 collective-permute-done.19
  65.1 4.6 collective-permute-start.25
  75.9 4.5 collective-permute-done.26
  82.5 11.4 %collective-permute-done.28 = bf16[16,768]{1,0:T(8,128)(2,1)S(1)} collective-permute-done((bf16[16,768]{1,0:T(8,128)(2,1)S(1)}, bf16[16,768]{1,0:T(8,128)(2,1)S(1)}, u32[]{:S(2)}, u32[]{:S(2)}) %collective-permute-start.28) | collective-permute-done | bytes 24608 | tf_op jit(solution)/shard_map/ppermute | solution.py:341
  97.0 10.2 %collective-permute-done.24 = bf16[512,256]{1,0:T(8,128)(2,1)S(1)} collective-permute-done((bf16[512,256]{1,0:T(8,128)(2,1)S(1)}, bf16[512,256]{1,0:T(8,128)(2,1)S(1)}, u32[]{:S(2)}, u32[]{:S(2)}) %collective-permute-start.24) | collective-permute-done | bytes 262176 | tf_op jit(solution)/shard_map/ppermute | solution.py:341
  130.1 18.2 %shard_map.169 = bf16[1024,512]{1,0:T(8,128)(2,1)S(1)} custom-call(f32[4,2]{1,0:T(4,128)S(1)} %multiply_power_fusion.slopes, bf16[1024,512]{1,0:T(8,128)(2,1)S(1)} %add_convert_fusion.15.query_in, bf16[1024,512]{1,0:T(8,128)(2,1)S(1)} %convolution_convert_fusion.18.key_in, bf16[1024,512]{1,0:T(8,128)(2,1)S(1)} %add_convert_fusion.14.value_in, ...), custom_call_target="tpu_custom_call" | custom-call | flops 10737418240 | bytes 4194304 | tf_op jit(solution)/shard_map/pallas_call | solution.py:170
  157.1 5.2 fusion.159
  164.9 14.6 %collective-permute-done.44 = bf16[256,512]{1,0:T(8,128)(2,1)S(1)} collective-permute-done((bf16[256,512]{1,0:T(8,128)(2,1)S(1)}, bf16[256,512]{1,0:T(8,128)(2,1)S(1)}, u32[]{:S(2)}, u32[]{:S(2)}) %collective-permute-start.44) | collective-permute-done | bytes 262176 | tf_op jit(solution)/shard_map/ppermute | solution.py:341
  197.2 38.3 %collective-permute-done.48 = bf16[256,1024]{1,0:T(8,128)(2,1)S(1)} collective-permute-done((bf16[256,1024]{1,0:T(8,128)(2,1)S(1)}, bf16[256,1024]{1,0:T(8,128)(2,1)S(1)}, u32[]{:S(2)}, u32[]{:S(2)}) %collective-permute-start.48) | collective-permute-done | bytes 524320 | tf_op jit(solution)/shard_map/ppermute | solution.py:341
  252.6 6.1 shard_map.171
  261.7 9.0 %multiply_convert_fusion.1 = (bf16[1024,2048]{1,0:T(8,128)(2,1)S(1)}, f32[1024,2048]{1,0:T(8,128)}) fusion(f32[2048]{0:T(1024)S(1)} %bitcast.265, bf16[1024,1024]{0,1:T(8,128)(2,1)S(1)} %copy-done.58, bf16[1024,2048]{1,0:T(8,128)(2,1)S(1)} %shard_map.170), kind=kOutput, calls=%fused_computation.17 | convolution fusion | flops 4315938816 | bytes 18882560 | tf_op jit(solution)/shard_map/dot_general | solution.py:674
  272.8 5.8 convolution_convert_fusion.12
  278.6 3.6 collective-permute-start.53
  288.0 14.5 %collective-permute-start.62 = (bf16[512,1024]{0,1:T(8,128)(2,1)S(1)}, bf16[512,1024]{0,1:T(8,128)(2,1)S(1)}, u32[]{:S(2)}, u32[]{:S(2)}) collective-permute-start(bf16[512,1024]{0,1:T(8,128)(2,1)S(1)} %broadcast_select_fusion.4), channel_id=1, source_target_pairs={{0,4},{1,5},{2,6},{3,7},{4,0},{5,1},{6,2},{7,3},{8,12},{9,13},{10,... | collective-permute-start | bytes 3145736 | tf_op jit(solution)/shard_map/ppermute | solution.py:341
  309.2 18.1 %collective-permute-done.54 = bf16[512,1024]{1,0:T(8,128)(2,1)S(1)} collective-permute-done((bf16[512,1024]{1,0:T(8,128)(2,1)S(1)}, bf16[512,1024]{1,0:T(8,128)(2,1)S(1)}, u32[]{:S(2)}, u32[]{:S(2)}) %collective-permute-start.54) | collective-permute-done | bytes 1048608 | tf_op jit(solution)/shard_map/ppermute | solution.py:341
  327.4 4.0 add_convert_fusion.query_in.key_in.value_in
  331.4 18.3 %shard_map.172 = bf16[1024,512]{1,0:T(8,128)(2,1)S(1)} custom-call(f32[4,2]{1,0:T(4,128)S(1)} %multiply_power_fusion.slopes, bf16[1024,1536]{1,0:T(8,128)(2,1)S(1)} %add_convert_fusion.query_in.key_in.value_in, bf16[1024,1536]{1,0:T(8,128)(2,1)S(1)} %add_convert_fusion.query_in.key_in.value_in, ...), custom_call_target="tpu_custom_call" | custom-call | flops 10737418240 | bytes 4194304 | tf_op jit(solution)/shard_map/pallas_call | solution.py:170
  359.9 40.2 %collective-permute-done.57.second = bf16[512,2048]{1,0:T(8,128)(2,1)S(1)} collective-permute-done((bf16[512,2048]{1,0:T(8,128)(2,1)S(1)}, bf16[512,2048]{1,0:T(8,128)(2,1)S(1)}, u32[]{:S(2)}, u32[]{:S(2)}) %collective-permute-start.57) | collective-permute-done | bytes 2097184 | tf_op jit(solution)/shard_map/ppermute | solution.py:341
  402.5 9.9 %multiply_convert_fusion = (bf16[1024,2048]{1,0:T(8,128)(2,1)}, f32[1024,2048]{1,0:T(8,128)}) fusion(f32[2048]{0:T(1024)S(1)} %bitcast.267, bf16[1024,1024]{0,1:T(8,128)(2,1)S(1)} %add_convert_fusion.3, bf16[1024,2048]{1,0:T(8,128)(2,1)S(1)} %shard_map.173), kind=kOutput, calls=%fused_computation.16 | convolution fusion | flops 4315938816 | bytes 18882560 | tf_op jit(solution)/shard_map/dot_general | solution.py:674
  413.5 12.2 %fusion.208 = (f32[2048]{0:T(1024)S(1)}, bf16[1024,2048]{1,0:T(8,128)(2,1)S(1)}) fusion(f32[1024,2048]{1,0:T(8,128)} %get-tuple-element.658, f32[2048]{0:T(1024)S(1)} %bitcast.268, bf16[2048,1024]{1,0:T(8,128)(2,1)S(1)} %shard_map.174, bf16[1024,256]{0,1:T(8,128)(2,1)S(1)} %get-tuple-element.387, bf16[1024,256]{0,1:T(8,128)(2,1)S(1)} %get-tuple-element.386, ...), kind=kOutput, calls=%fused_computation.641 | convolution fusion | flops 4349491200 | bytes 18890752 | tf_op jit(solution)/shard_map/dot_general | solution.py:23
  425.7 4.8 convolution_convert_fusion.9
  431.3 6.2 convolution_convert_fusion.10
  437.5 3.7 convolution_convert_fusion.6
  441.2 3.7 convolution_convert_fusion.4
  444.9 3.7 convolution_convert_fusion.7
  454.1 6.1 convolution_convert_fusion.5
  460.2 4.4 multiply_reduce_fusion
  464.6 7.2 fusion.156
  480.4 27.3 %shard_map.175 = (bf16[3,1024,512]{2,1,0:T(8,128)(2,1)S(1)}, f32[4,2,128]{2,1,0:T(2,128)S(1)}) custom-call(f32[4,2]{1,0:T(4,128)S(1)} %multiply_power_fusion.slopes, bf16[1024,1536]{1,0:T(8,128)(2,1)} %copy-done.13, bf16[1024,1536]{1,0:T(8,128)(2,1)} %copy-done.13, bf16[1024,1536]{1,0:T(8,128)(2,1)} %copy-done.13, ...), custom_call_target="tpu_custom_call" | custom-call | flops 17179869184 | bytes 7340032 | tf_op jit(solution)/shard_map/pallas_call | solution.py:196
  513.3 4.1 fusion.44
  541.6 5.5 multiply_reduce_fusion.1
  547.1 3.6 multiply_add_fusion.1
  555.4 12.0 %fusion.154 = (f32[2048]{0:T(1024)}, bf16[1024,2048]{1,0:T(8,128)(2,1)}) fusion(f32[1024,2048]{1,0:T(8,128)S(1)} %bitcast.276, f32[2048]{0:T(1024)S(1)} %bitcast.266, bf16[1024,1024]{0,1:T(8,128)(2,1)S(1)} %convert_element_type.945, bf16[2048,1024]{1,0:T(8,128)(2,1)S(1)} %copy-done.2), kind=kOutput, calls=%fused_computation.588 | convolution fusion | flops 4341102592 | bytes 18890752 | tf_op jit(solution)/shard_map/dot_general | solution.py:23
  576.9 3.9 convolution_convert_fusion.3
  581.6 6.1 convolution_convert_fusion.2
  588.5 4.6 collective-permute-done.71
  594.8 8.1 convolution_convert_fusion.8
  615.8 3.7 convolution_convert_fusion.1
  631.4 16.0 %collective-permute-done.79 = bf16[512,768]{1,0:T(8,128)(2,1)S(1)} collective-permute-done((bf16[512,768]{1,0:T(8,128)(2,1)S(1)}, bf16[512,768]{1,0:T(8,128)(2,1)S(1)}, u32[]{:S(2)}, u32[]{:S(2)}) %collective-permute-start.79) | collective-permute-done | bytes 786464 | tf_op jit(solution)/shard_map/ppermute | solution.py:341
  648.3 27.5 %shard_map.176 = (bf16[3,1024,512]{2,1,0:T(8,128)(2,1)}, f32[4,2,128]{2,1,0:T(2,128)S(1)}) custom-call(f32[4,2]{1,0:T(4,128)S(1)} %multiply_power_fusion.slopes, bf16[1024,512]{1,0:T(8,128)(2,1)S(1)} %copy-done.10, bf16[1024,512]{1,0:T(8,128)(2,1)S(1)} %copy-done.12, bf16[1024,512]{1,0:T(8,128)(2,1)S(1)} %copy-done.8, ...), custom_call_target="tpu_custom_call" | custom-call | flops 17179869184 | bytes 7340032 | tf_op jit(solution)/shard_map/pallas_call | solution.py:196
  698.1 9.9 %collective-permute-done.82 = bf16[2048,256]{1,0:T(8,128)(2,1)S(1)} collective-permute-done((bf16[2048,256]{1,0:T(8,128)(2,1)S(1)}, bf16[2048,256]{1,0:T(8,128)(2,1)S(1)}, u32[]{:S(2)}, u32[]{:S(2)}) %collective-permute-start.82) | collective-permute-done | bytes 1048608 | tf_op jit(solution)/shard_map/ppermute | solution.py:341
  739.2 4.8 fusion.24
  744.1 5.4 fusion.23
  765.1 7.9 collective-permute-done.97
  803.5 3.8 collective-permute-start.120
  808.5 6.0 collective-permute-done.108
  830.1 8.7 %collective-permute-start.119 = (bf16[128,512]{1,0:T(8,128)(2,1)S(1)}, bf16[128,512]{1,0:T(8,128)(2,1)S(1)}, u32[]{:S(2)}, u32[]{:S(2)}) collective-permute-start(bf16[128,512]{1,0:T(8,128)(2,1)S(1)} %select_convert_fusion.2), channel_id=1, source_target_pairs={{0,4},{1,5},{2,6},{3,7},{4,0},{5,1},{6,2},{7,3},{8,12},{9,13},{10,... | collective-permute-start | bytes 393224 | tf_op jit(solution)/shard_map/ppermute | solution.py:341
  (1150 shorter events, 376.5 us)
Async XLA Ops:
  51.8 30.1 %collective-permute-start.23 = (bf16[256,512]{1,0:T(8,128)(2,1)S(1)}, bf16[256,512]{1,0:T(8,128)(2,1)S(1)}, u32[]{:S(2)}, u32[]{:S(2)}) collective-permute-start(bf16[256,512]{1,0:T(8,128)(2,1)S(1)} %pad_maximum_fusion.31), channel_id=1, source_target_pairs={{0,2},{1,3},{2,0},{3,1},{4,6},{5,7},{6,4},{7,5},{8,10},{9,11},{10,... | collective-permute-start | bytes 786440 | tf_op jit(solution)/shard_map/ppermute | solution.py:341
  70.8 36.4 %collective-permute-start.31 = (bf16[1024,256]{1,0:T(8,128)(2,1)S(1)}, bf16[1024,256]{1,0:T(8,128)(2,1)S(1)}, u32[]{:S(2)}, u32[]{:S(2)}) collective-permute-start(bf16[1024,256]{1,0:T(8,128)(2,1)S(1)} %pad_maximum_fusion.23), channel_id=1, source_target_pairs={{0,1},{1,0},{2,3},{3,2},{4,5},{5,4},{6,7},{7,6},{8,9},{9,8},{10,11... | collective-permute-start | bytes 1572872 | tf_op jit(solution)/shard_map/ppermute | solution.py:341
  75.0 32.2 %collective-permute-start.32 = (bf16[256,1024]{1,0:T(8,128)(2,1)S(1)}, bf16[256,1024]{1,0:T(8,128)(2,1)S(1)}, u32[]{:S(2)}, u32[]{:S(2)}) collective-permute-start(bf16[256,1024]{1,0:T(8,128)(2,1)S(1)} %pad_maximum_fusion.24), channel_id=1, source_target_pairs={{0,1},{1,0},{2,3},{3,2},{4,5},{5,4},{6,7},{7,6},{8,9},{9,8},{10,11... | collective-permute-start | bytes 1572872 | tf_op jit(solution)/shard_map/ppermute | solution.py:341
  80.4 26.8 %collective-permute-start.29 = (bf16[512,512]{1,0:T(8,128)(2,1)S(1)}, bf16[512,512]{1,0:T(8,128)(2,1)S(1)}, u32[]{:S(2)}, u32[]{:S(2)}) collective-permute-start(bf16[512,512]{1,0:T(8,128)(2,1)S(1)} %pad_maximum_fusion.21), channel_id=1, source_target_pairs={{0,16},{1,17},{2,18},{3,19},{4,20},{5,21},{6,22},{7,23},{8,24},{9,... | collective-permute-start | bytes 1572872 | tf_op jit(solution)/shard_map/ppermute | solution.py:341
  81.6 25.5 %collective-permute-start.30 = (bf16[512,512]{1,0:T(8,128)(2,1)S(1)}, bf16[512,512]{1,0:T(8,128)(2,1)S(1)}, u32[]{:S(2)}, u32[]{:S(2)}) collective-permute-start(bf16[512,512]{1,0:T(8,128)(2,1)S(1)} %pad_maximum_fusion.22), channel_id=1, source_target_pairs={{0,8},{1,9},{2,10},{3,11},{4,12},{5,13},{6,14},{7,15},{8,0},{9,1},... | collective-permute-start | bytes 1572872 | tf_op jit(solution)/shard_map/ppermute | solution.py:341
  125.3 23.1 %collective-permute-start.36 = (bf16[256,1024]{1,0:T(8,128)(2,1)S(1)}, bf16[256,1024]{1,0:T(8,128)(2,1)S(1)}, u32[]{:S(2)}, u32[]{:S(2)}) collective-permute-start(bf16[256,1024]{1,0:T(8,128)(2,1)S(1)} %constant_dynamic-update-slice_fusion), channel_id=1, source_target_pairs={{0,8},{1,9},{2,10},{3,11},{4,12},{5,13},{6,14},{7,15},{8,0},{9,1},... | collective-permute-start | bytes 1572872 | tf_op jit(solution)/shard_map/ppermute | solution.py:341
  125.7 22.7 %collective-permute-start.37 = (bf16[1024,256]{1,0:T(8,128)(2,1)S(1)}, bf16[1024,256]{1,0:T(8,128)(2,1)S(1)}, u32[]{:S(2)}, u32[]{:S(2)}) collective-permute-start(bf16[1024,256]{1,0:T(8,128)(2,1)S(1)} %pad_maximum_fusion.25), channel_id=1, source_target_pairs={{0,1},{1,0},{2,3},{3,2},{4,5},{5,4},{6,7},{7,6},{8,9},{9,8},{10,11... | collective-permute-start | bytes 1572872 | tf_op jit(solution)/shard_map/ppermute | solution.py:341
  152.5 27.0 %collective-permute-start.41 = (bf16[512,1024]{1,0:T(8,128)(2,1)S(1)}, bf16[512,1024]{1,0:T(8,128)(2,1)S(1)}, u32[]{:S(2)}, u32[]{:S(2)}) collective-permute-start(bf16[512,1024]{1,0:T(8,128)(2,1)S(1)} %pad_maximum_fusion.8), channel_id=1, source_target_pairs={{0,1},{1,0},{2,3},{3,2},{4,5},{5,4},{6,7},{7,6},{8,9},{9,8},{10,11... | collective-permute-start | bytes 3145736 | tf_op jit(solution)/shard_map/ppermute | solution.py:341
  154.0 25.6 %collective-permute-start.42 = (bf16[2048,256]{1,0:T(8,128)(2,1)S(1)}, bf16[2048,256]{1,0:T(8,128)(2,1)S(1)}, u32[]{:S(2)}, u32[]{:S(2)}) collective-permute-start(bf16[2048,256]{1,0:T(8,128)(2,1)S(1)} %pad_maximum_fusion.14), channel_id=1, source_target_pairs={{0,16},{1,17},{2,18},{3,19},{4,20},{5,21},{6,22},{7,23},{8,24},{9,... | collective-permute-start | bytes 3145736 | tf_op jit(solution)/shard_map/ppermute | solution.py:341
  155.3 24.2 %collective-permute-start.43 = (bf16[512,768]{1,0:T(8,128)(2,1)S(1)}, bf16[512,768]{1,0:T(8,128)(2,1)S(1)}, u32[]{:S(2)}, u32[]{:S(2)}) collective-permute-start(bf16[512,768]{1,0:T(8,128)(2,1)S(1)} %pad_maximum_fusion.19), channel_id=1, source_target_pairs={{0,8},{1,9},{2,10},{3,11},{4,12},{5,13},{6,14},{7,15},{8,0},{9,1},... | collective-permute-start | bytes 2359304 | tf_op jit(solution)/shard_map/ppermute | solution.py:341
  156.6 22.9 %collective-permute-start.44 = (bf16[256,512]{1,0:T(8,128)(2,1)S(1)}, bf16[256,512]{1,0:T(8,128)(2,1)S(1)}, u32[]{:S(2)}, u32[]{:S(2)}) collective-permute-start(bf16[256,512]{1,0:T(8,128)(2,1)S(1)} %pad_maximum_fusion.39), channel_id=1, source_target_pairs={{0,8},{1,9},{2,10},{3,11},{4,12},{5,13},{6,14},{7,15},{8,0},{9,1},... | collective-permute-start | bytes 786440 | tf_op jit(solution)/shard_map/ppermute | solution.py:341
  180.2 58.4 %collective-permute-start.45 = (bf16[512,2048]{1,0:T(8,128)(2,1)S(1)}, bf16[512,2048]{1,0:T(8,128)(2,1)}, u32[]{:S(2)}, u32[]{:S(2)}) collective-permute-start(bf16[512,2048]{1,0:T(8,128)(2,1)S(1)} %pad_maximum_fusion.2.first), channel_id=1, source_target_pairs={{0,16},{1,17},{2,18},{3,19},{4,20},{5,21},{6,22},{7,23},{8,24},{9,... | collective-permute-start | bytes 6291464 | tf_op jit(solution)/shard_map/ppermute | solution.py:341
  182.0 56.6 %collective-permute-start.46 = (bf16[2048,512]{1,0:T(8,128)(2,1)}, bf16[2048,512]{1,0:T(8,128)(2,1)}, u32[]{:S(2)}, u32[]{:S(2)}) collective-permute-start(bf16[2048,512]{1,0:T(8,128)(2,1)} %pad_maximum_fusion.3.first), channel_id=1, source_target_pairs={{0,8},{1,9},{2,10},{3,11},{4,12},{5,13},{6,14},{7,15},{8,0},{9,1},... | collective-permute-start | bytes 6291464 | tf_op jit(solution)/shard_map/ppermute | solution.py:341
  184.5 54.1 %collective-permute-start.47 = (bf16[1024,768]{1,0:T(8,128)(2,1)}, bf16[1024,768]{1,0:T(8,128)(2,1)}, u32[]{:S(2)}, u32[]{:S(2)}) collective-permute-start(bf16[1024,768]{1,0:T(8,128)(2,1)} %pad_maximum_fusion.7), channel_id=1, source_target_pairs={{0,1},{1,0},{2,3},{3,2},{4,5},{5,4},{6,7},{7,6},{8,9},{9,8},{10,11... | collective-permute-start | bytes 4718600 | tf_op jit(solution)/shard_map/ppermute | solution.py:341
  187.6 72.3 %collective-permute-start.49 = (bf16[256,512]{1,0:T(8,128)(2,1)}, bf16[256,512]{1,0:T(8,128)(2,1)S(1)}, u32[]{:S(2)}, u32[]{:S(2)}) collective-permute-start(bf16[256,512]{1,0:T(8,128)(2,1)} %pad_maximum_fusion.37), channel_id=1, source_target_pairs={{0,2},{1,3},{2,0},{3,1},{4,6},{5,7},{6,4},{7,5},{8,10},{9,11},{10,... | collective-permute-start | bytes 786440 | tf_op jit(solution)/shard_map/ppermute | solution.py:341
  193.6 41.9 %collective-permute-start.48 = (bf16[256,1024]{1,0:T(8,128)(2,1)S(1)}, bf16[256,1024]{1,0:T(8,128)(2,1)S(1)}, u32[]{:S(2)}, u32[]{:S(2)}) collective-permute-start(bf16[256,1024]{1,0:T(8,128)(2,1)S(1)} %pad_maximum_fusion.26), channel_id=1, source_target_pairs={{0,1},{1,0},{2,3},{3,2},{4,5},{5,4},{6,7},{7,6},{8,9},{9,8},{10,11... | collective-permute-start | bytes 1572872 | tf_op jit(solution)/shard_map/ppermute | solution.py:341
  235.5 24.5 %collective-permute-start.50 = (bf16[512,256]{1,0:T(8,128)(2,1)S(1)}, bf16[512,256]{1,0:T(8,128)(2,1)S(1)}, u32[]{:S(2)}, u32[]{:S(2)}) collective-permute-start(bf16[512,256]{1,0:T(8,128)(2,1)S(1)} %pad_maximum_fusion.38), channel_id=1, source_target_pairs={{0,2},{1,3},{2,0},{3,1},{4,6},{5,7},{6,4},{7,5},{8,10},{9,11},{10,... | collective-permute-start | bytes 786440 | tf_op jit(solution)/shard_map/ppermute | solution.py:341
  278.6 25.7 %collective-permute-start.53 = (bf16[1024,1024]{0,1:T(8,128)(2,1)}, bf16[1024,1024]{0,1:T(8,128)(2,1)}, u32[]{:S(2)}, u32[]{:S(2)}) collective-permute-start(bf16[1024,1024]{0,1:T(8,128)(2,1)} %convolution_convert_fusion.12), channel_id=1, source_target_pairs={{0,4},{1,5},{2,6},{3,7},{4,0},{5,1},{6,2},{7,3},{8,12},{9,13},{10,... | collective-permute-start | bytes 6291464 | tf_op jit(solution)/shard_map/ppermute | solution.py:341
  288.0 67.2 %collective-permute-start.62 = (bf16[512,1024]{0,1:T(8,128)(2,1)S(1)}, bf16[512,1024]{0,1:T(8,128)(2,1)S(1)}, u32[]{:S(2)}, u32[]{:S(2)}) collective-permute-start(bf16[512,1024]{0,1:T(8,128)(2,1)S(1)} %broadcast_select_fusion.4), channel_id=1, source_target_pairs={{0,4},{1,5},{2,6},{3,7},{4,0},{5,1},{6,2},{7,3},{8,12},{9,13},{10,... | collective-permute-start | bytes 3145736 | tf_op jit(solution)/shard_map/ppermute | solution.py:341
  302.6 24.8 %collective-permute-start.54 = (bf16[512,1024]{1,0:T(8,128)(2,1)S(1)}, bf16[512,1024]{1,0:T(8,128)(2,1)S(1)}, u32[]{:S(2)}, u32[]{:S(2)}) collective-permute-start(bf16[512,1024]{1,0:T(8,128)(2,1)S(1)} %pad_maximum_fusion.9), channel_id=1, source_target_pairs={{0,1},{1,0},{2,3},{3,2},{4,5},{5,4},{6,7},{7,6},{8,9},{9,8},{10,11... | collective-permute-start | bytes 3145736 | tf_op jit(solution)/shard_map/ppermute | solution.py:341
  303.0 24.4 %collective-permute-start.55 = (bf16[2048,256]{1,0:T(8,128)(2,1)S(1)}, bf16[2048,256]{1,0:T(8,128)(2,1)S(1)}, u32[]{:S(2)}, u32[]{:S(2)}) collective-permute-start(bf16[2048,256]{1,0:T(8,128)(2,1)S(1)} %pad_maximum_fusion.16), channel_id=1, source_target_pairs={{0,16},{1,17},{2,18},{3,19},{4,20},{5,21},{6,22},{7,23},{8,24},{9,... | collective-permute-start | bytes 3145736 | tf_op jit(solution)/shard_map/ppermute | solution.py:341
  352.8 47.3 %collective-permute-start.57 = (bf16[512,2048]{1,0:T(8,128)(2,1)S(1)}, bf16[512,2048]{1,0:T(8,128)(2,1)S(1)}, u32[]{:S(2)}, u32[]{:S(2)}) collective-permute-start(bf16[512,2048]{1,0:T(8,128)(2,1)S(1)} %pad_maximum_fusion.4.first), channel_id=1, source_target_pairs={{0,16},{1,17},{2,18},{3,19},{4,20},{5,21},{6,22},{7,23},{8,24},{9,... | collective-permute-start | bytes 6291464 | tf_op jit(solution)/shard_map/ppermute | solution.py:341
  356.7 55.7 %collective-permute-start.58 = (bf16[2048,512]{1,0:T(8,128)(2,1)S(1)}, bf16[2048,512]{1,0:T(8,128)(2,1)S(1)}, u32[]{:S(2)}, u32[]{:S(2)}) collective-permute-start(bf16[2048,512]{1,0:T(8,128)(2,1)S(1)} %pad_maximum_fusion.5.first), channel_id=1, source_target_pairs={{0,8},{1,9},{2,10},{3,11},{4,12},{5,13},{6,14},{7,15},{8,0},{9,1},... | collective-permute-start | bytes 6291464 | tf_op jit(solution)/shard_map/ppermute | solution.py:341
  430.5 29.8 %collective-permute-start.63 = (bf16[1024,1024]{0,1:T(8,128)(2,1)S(1)}, bf16[1024,1024]{0,1:T(8,128)(2,1)}, u32[]{:S(2)}, u32[]{:S(2)}) collective-permute-start(bf16[1024,1024]{0,1:T(8,128)(2,1)S(1)} %convolution_convert_fusion.9), channel_id=1, source_target_pairs={{0,4},{1,5},{2,6},{3,7},{4,0},{5,1},{6,2},{7,3},{8,12},{9,13},{10,... | collective-permute-start | bytes 6291464 | tf_op jit(solution)/shard_map/ppermute | solution.py:341
  441.2 23.4 %collective-permute-start.59 = (bf16[1024,1024]{0,1:T(8,128)(2,1)}, bf16[1024,1024]{0,1:T(8,128)(2,1)}, u32[]{:S(2)}, u32[]{:S(2)}) collective-permute-start(bf16[1024,1024]{0,1:T(8,128)(2,1)} %convolution_convert_fusion.10), channel_id=1, source_target_pairs={{0,4},{1,5},{2,6},{3,7},{4,0},{5,1},{6,2},{7,3},{8,12},{9,13},{10,... | collective-permute-start | bytes 6291464 | tf_op jit(solution)/shard_map/ppermute | solution.py:341
  448.7 62.7 %collective-permute-start.64 = (bf16[2048,512]{1,0:T(8,128)(2,1)}, bf16[2048,512]{1,0:T(8,128)(2,1)}, u32[]{:S(2)}, u32[]{:S(2)}) collective-permute-start(bf16[2048,512]{1,0:T(8,128)(2,1)} %convolution_convert_fusion.7), channel_id=1, source_target_pairs={{0,8},{1,9},{2,10},{3,11},{4,12},{5,13},{6,14},{7,15},{8,0},{9,1},... | collective-permute-start | bytes 6291464 | tf_op jit(solution)/shard_map/ppermute | solution.py:341
  449.9 61.6 %collective-permute-start.65 = (bf16[512,2048]{1,0:T(8,128)(2,1)}, bf16[512,2048]{1,0:T(8,128)(2,1)}, u32[]{:S(2)}, u32[]{:S(2)}) collective-permute-start(bf16[512,2048]{1,0:T(8,128)(2,1)} %convolution_convert_fusion.6), channel_id=1, source_target_pairs={{0,16},{1,17},{2,18},{3,19},{4,20},{5,21},{6,22},{7,23},{8,24},{9,... | collective-permute-start | bytes 6291464 | tf_op jit(solution)/shard_map/ppermute | solution.py:341
  473.1 63.3 %collective-permute-start.60 = (bf16[512,1024]{0,1:T(8,128)(2,1)}, bf16[512,1024]{0,1:T(8,128)(2,1)}, u32[]{:S(2)}, u32[]{:S(2)}) collective-permute-start(bf16[512,1024]{0,1:T(8,128)(2,1)} %fusion.52), channel_id=1, source_target_pairs={{1,4},{3,6},{4,1},{6,3},{9,12},{11,14},{12,9},{14,11},{17,20},{19,... | collective-permute-start | bytes 3145736 | tf_op jit(solution)/shard_map/ppermute | solution.py:350
  477.7 33.7 %collective-permute-start.66 = (bf16[256,1024]{1,0:T(8,128)(2,1)}, bf16[256,1024]{1,0:T(8,128)(2,1)}, u32[]{:S(2)}, u32[]{:S(2)}) collective-permute-start(bf16[256,1024]{1,0:T(8,128)(2,1)} %convolution_convert_fusion.24), channel_id=1, source_target_pairs={{0,1},{1,0},{2,3},{3,2},{4,5},{5,4},{6,7},{7,6},{8,9},{9,8},{10,11... | collective-permute-start | bytes 1572872 | tf_op jit(solution)/shard_map/ppermute | solution.py:341
  517.4 24.1 %collective-permute-start.67 = (bf16[1024,1024]{0,1:T(8,128)(2,1)S(1)}, bf16[1024,1024]{0,1:T(8,128)(2,1)}, u32[]{:S(2)}, u32[]{:S(2)}) collective-permute-start(bf16[1024,1024]{0,1:T(8,128)(2,1)S(1)} %fusion.44), channel_id=1, source_target_pairs={{0,4},{1,5},{2,6},{3,7},{4,0},{5,1},{6,2},{7,3},{8,12},{9,13},{10,... | collective-permute-start | bytes 6291464 | tf_op jit(solution)/shard_map/ppermute | solution.py:341
  520.6 30.1 %collective-permute-start.68 = (bf16[2048,256]{1,0:T(8,128)(2,1)}, bf16[2048,256]{1,0:T(8,128)(2,1)}, u32[]{:S(2)}, u32[]{:S(2)}) collective-permute-start(bf16[2048,256]{1,0:T(8,128)(2,1)} %get-tuple-element.347), channel_id=1, source_target_pairs={{0,16},{1,17},{2,18},{3,19},{4,20},{5,21},{6,22},{7,23},{8,24},{9,... | collective-permute-start | bytes 3145736 | tf_op jit(solution)/shard_map/ppermute | solution.py:341
  523.9 26.9 %collective-permute-start.69 = (bf16[512,1024]{1,0:T(8,128)(2,1)}, bf16[512,1024]{1,0:T(8,128)(2,1)}, u32[]{:S(2)}, u32[]{:S(2)}) collective-permute-start(bf16[512,1024]{1,0:T(8,128)(2,1)} %add_convert_fusion.12), channel_id=1, source_target_pairs={{0,1},{1,0},{2,3},{3,2},{4,5},{5,4},{6,7},{7,6},{8,9},{9,8},{10,11... | collective-permute-start | bytes 3145736 | tf_op jit(solution)/shard_map/ppermute | solution.py:341
  526.1 24.6 %collective-permute-start.70 = (bf16[256,512]{1,0:T(8,128)(2,1)}, bf16[256,512]{1,0:T(8,128)(2,1)}, u32[]{:S(2)}, u32[]{:S(2)}) collective-permute-start(bf16[256,512]{1,0:T(8,128)(2,1)} %add_convert_fusion.45), channel_id=1, source_target_pairs={{0,8},{1,9},{2,10},{3,11},{4,12},{5,13},{6,14},{7,15},{8,0},{9,1},... | collective-permute-start | bytes 786440 | tf_op jit(solution)/shard_map/ppermute | solution.py:341
  536.4 52.1 %collective-permute-start.74 = (bf16[1024,768]{1,0:T(8,128)(2,1)}, bf16[1024,768]{1,0:T(8,128)(2,1)}, u32[]{:S(2)}, u32[]{:S(2)}) collective-permute-start(bf16[1024,768]{1,0:T(8,128)(2,1)} %convolution_convert_fusion.15), channel_id=1, source_target_pairs={{0,1},{1,0},{2,3},{3,2},{4,5},{5,4},{6,7},{7,6},{8,9},{9,8},{10,11... | collective-permute-start | bytes 4718600 | tf_op jit(solution)/shard_map/ppermute | solution.py:341
  569.7 23.4 %collective-permute-start.71 = (bf16[1024,256]{1,0:T(8,128)(2,1)}, bf16[1024,256]{1,0:T(8,128)(2,1)S(1)}, u32[]{:S(2)}, u32[]{:S(2)}) collective-permute-start(bf16[1024,256]{1,0:T(8,128)(2,1)} %add_convert_fusion.25), channel_id=1, source_target_pairs={{0,1},{1,0},{2,3},{3,2},{4,5},{5,4},{6,7},{7,6},{8,9},{9,8},{10,11... | collective-permute-start | bytes 1572872 | tf_op jit(solution)/shard_map/ppermute | solution.py:341
  580.8 67.5 %collective-permute-start.80 = (bf16[2048,512]{1,0:T(8,128)(2,1)}, bf16[2048,512]{1,0:T(8,128)(2,1)}, u32[]{:S(2)}, u32[]{:S(2)}) collective-permute-start(bf16[2048,512]{1,0:T(8,128)(2,1)} %convolution_convert_fusion.3), channel_id=1, source_target_pairs={{0,8},{1,9},{2,10},{3,11},{4,12},{5,13},{6,14},{7,15},{8,0},{9,1},... | collective-permute-start | bytes 6291464 | tf_op jit(solution)/shard_map/ppermute | solution.py:341
  604.5 26.9 %collective-permute-start.76 = (bf16[512,256]{1,0:T(8,128)(2,1)S(1)}, bf16[512,256]{1,0:T(8,128)(2,1)S(1)}, u32[]{:S(2)}, u32[]{:S(2)}) collective-permute-start(bf16[512,256]{1,0:T(8,128)(2,1)S(1)} %add_convert_fusion.43), channel_id=1, source_target_pairs={{0,2},{1,3},{2,0},{3,1},{4,6},{5,7},{6,4},{7,5},{8,10},{9,11},{10,... | collective-permute-start | bytes 786440 | tf_op jit(solution)/shard_map/ppermute | solution.py:341
  604.7 26.7 %collective-permute-start.77 = (bf16[256,512]{1,0:T(8,128)(2,1)S(1)}, bf16[256,512]{1,0:T(8,128)(2,1)S(1)}, u32[]{:S(2)}, u32[]{:S(2)}) collective-permute-start(bf16[256,512]{1,0:T(8,128)(2,1)S(1)} %add_convert_fusion.42), channel_id=1, source_target_pairs={{0,2},{1,3},{2,0},{3,1},{4,6},{5,7},{6,4},{7,5},{8,10},{9,11},{10,... | collective-permute-start | bytes 786440 | tf_op jit(solution)/shard_map/ppermute | solution.py:341
  619.5 27.9 %collective-permute-start.79 = (bf16[512,768]{1,0:T(8,128)(2,1)S(1)}, bf16[512,768]{1,0:T(8,128)(2,1)S(1)}, u32[]{:S(2)}, u32[]{:S(2)}) collective-permute-start(bf16[512,768]{1,0:T(8,128)(2,1)S(1)} %add_convert_fusion.17), channel_id=1, source_target_pairs={{0,8},{1,9},{2,10},{3,11},{4,12},{5,13},{6,14},{7,15},{8,0},{9,1},... | collective-permute-start | bytes 2359304 | tf_op jit(solution)/shard_map/ppermute | solution.py:341
  630.2 67.9 %collective-permute-start.83 = (bf16[512,2048]{1,0:T(8,128)(2,1)}, bf16[512,2048]{1,0:T(8,128)(2,1)}, u32[]{:S(2)}, u32[]{:S(2)}) collective-permute-start(bf16[512,2048]{1,0:T(8,128)(2,1)} %convolution_convert_fusion.1), channel_id=1, source_target_pairs={{0,16},{1,17},{2,18},{3,19},{4,20},{5,21},{6,22},{7,23},{8,24},{9,... | collective-permute-start | bytes 6291464 | tf_op jit(solution)/shard_map/ppermute | solution.py:341
  680.0 27.9 %collective-permute-start.82 = (bf16[2048,256]{1,0:T(8,128)(2,1)S(1)}, bf16[2048,256]{1,0:T(8,128)(2,1)S(1)}, u32[]{:S(2)}, u32[]{:S(2)}) collective-permute-start(bf16[2048,256]{1,0:T(8,128)(2,1)S(1)} %get-tuple-element.344), channel_id=1, source_target_pairs={{0,16},{1,17},{2,18},{3,19},{4,20},{5,21},{6,22},{7,23},{8,24},{9,... | collective-permute-start | bytes 3145736 | tf_op jit(solution)/shard_map/ppermute | solution.py:341
  713.3 24.7 %collective-permute-start.85 = (bf16[1024,1024]{0,1:T(8,128)(2,1)S(1)}, bf16[1024,1024]{0,1:T(8,128)(2,1)S(1)}, u32[]{:S(2)}, u32[]{:S(2)}) collective-permute-start(bf16[1024,1024]{0,1:T(8,128)(2,1)S(1)} %add_convert_fusion.1), channel_id=1, source_target_pairs={{0,4},{1,5},{2,6},{3,7},{4,0},{5,1},{6,2},{7,3},{8,12},{9,13},{10,... | collective-permute-start | bytes 6291464 | tf_op jit(solution)/shard_map/ppermute | solution.py:341
  718.2 31.3 %collective-permute-start.86 = (bf16[256,384]{1,0:T(8,128)(2,1)S(1)}, bf16[256,384]{1,0:T(8,128)(2,1)S(1)}, u32[]{:S(2)}, u32[]{:S(2)}) collective-permute-start(bf16[256,384]{1,0:T(8,128)(2,1)S(1)} %add_convert_fusion.47), channel_id=1, source_target_pairs={{0,2},{1,3},{2,0},{3,1},{4,6},{5,7},{6,4},{7,5},{8,10},{9,11},{10,... | collective-permute-start | bytes 589832 | tf_op jit(solution)/shard_map/ppermute | solution.py:341
  720.7 42.6 %collective-permute-start.93 = (bf16[1024,256]{1,0:T(8,128)(2,1)}, bf16[1024,256]{1,0:T(8,128)(2,1)}, u32[]{:S(2)}, u32[]{:S(2)}) collective-permute-start(bf16[1024,256]{1,0:T(8,128)(2,1)} %add_convert_fusion.21), channel_id=1, source_target_pairs={{0,1},{1,0},{2,3},{3,2},{4,5},{5,4},{6,7},{7,6},{8,9},{9,8},{10,11... | collective-permute-start | bytes 1572872 | tf_op jit(solution)/shard_map/ppermute | solution.py:341
  723.9 50.0 %collective-permute-start.94 = (bf16[512,1024]{1,0:T(8,128)(2,1)}, bf16[512,1024]{1,0:T(8,128)(2,1)}, u32[]{:S(2)}, u32[]{:S(2)}) collective-permute-start(bf16[512,1024]{1,0:T(8,128)(2,1)} %add_convert_fusion.7), channel_id=1, source_target_pairs={{0,1},{1,0},{2,3},{3,2},{4,5},{5,4},{6,7},{7,6},{8,9},{9,8},{10,11... | collective-permute-start | bytes 3145736 | tf_op jit(solution)/shard_map/ppermute | solution.py:341
  727.1 31.9 %collective-permute-start.95 = (bf16[256,512]{1,0:T(8,128)(2,1)}, bf16[256,512]{1,0:T(8,128)(2,1)}, u32[]{:S(2)}, u32[]{:S(2)}) collective-permute-start(bf16[256,512]{1,0:T(8,128)(2,1)} %add_convert_fusion.39), channel_id=1, source_target_pairs={{0,8},{1,9},{2,10},{3,11},{4,12},{5,13},{6,14},{7,15},{8,0},{9,1},... | collective-permute-start | bytes 786440 | tf_op jit(solution)/shard_map/ppermute | solution.py:341
  738.0 27.0 %collective-permute-start.96 = (bf16[512,512]{1,0:T(8,128)(2,1)}, bf16[512,512]{1,0:T(8,128)(2,1)}, u32[]{:S(2)}, u32[]{:S(2)}) collective-permute-start(bf16[512,512]{1,0:T(8,128)(2,1)} %convolution_convert_fusion.27), channel_id=1, source_target_pairs={{0,16},{1,17},{2,18},{3,19},{4,20},{5,21},{6,22},{7,23},{8,24},{9,... | collective-permute-start | bytes 1572872 | tf_op jit(solution)/shard_map/ppermute | solution.py:341
  816.9 30.3 %collective-permute-start.91 = (bf16[512,1024]{0,1:T(8,128)(2,1)S(1)}, bf16[512,1024]{0,1:T(8,128)(2,1)}, u32[]{:S(2)}, u32[]{:S(2)}) collective-permute-start(bf16[512,1024]{0,1:T(8,128)(2,1)S(1)} %fusion.49), channel_id=1, source_target_pairs={{1,4},{3,6},{4,1},{6,3},{9,12},{11,14},{12,9},{14,11},{17,20},{19,... | collective-permute-start | bytes 3145736 | tf_op jit(solution)/shard_map/ppermute | solution.py:350
  (350 other events, 3823.4 us)

commit v5 on v4

--- a/solution.py
+++ b/solution.py
@@ -645,14 +645,17 @@
         if number == 0:
             packed = tick(packed, stage)
             packed, cotangent = lax.optimization_barrier((packed, cotangent))
-            upstream_low = to_local(group_rows(cross(cotangent)))
+            upstream_low = cross(cotangent)
         attended = attention_forward(packed, seg_col, seg_row, slopes)
         if number == 0:
-            attended = tick(attended, stage)
+            attended, upstream_low = tick((attended, upstream_low), stage)
+            upstream_low = group_rows(upstream_low)
         middle = stream + (
             group_sum(jnp.dot(attended, weights[-3], preferred_element_type=F32)) + rows[2]
         )
         normed_two = layer_norm(middle, rows[3], rows[4]).astype(BF16)
+        if number == 0:
+            normed_two, upstream_low = lax.optimization_barrier((normed_two, upstream_low))
         while stage[0].place + 1 < steps:
             normed_two = tick(normed_two, stage)
         following = stages[number + 2] if number + 2 < len(stages) else []
@@ -694,7 +697,7 @@
 
     output = give_back(stream.astype(BF16))
 
-    upstream = upstream_low.astype(F32)
+    upstream = to_local(upstream_low).astype(F32)
     reductions = [None] * layers
     small_grads = [None] * layers
     running = []

time: 860 us -> 862 us (level)
  starting transfers between devices: 152 us -> 143 us
    ppermute x117, starting transfers between devices: 146 us -> 137 us  [swap(): lax.ppermute(values, BOTH, [(at, at ^ mask) for at in range(devices)])]
    unnamed x589 -> x573, local copies, waits for them, and re-layouts: 40.6 us -> 42.8 us
  transfers between devices with their start and end apart: 121 -> 121, of which waited for: 34 -> 36; matrix products, arithmetic and copies ran while one was open for 36% -> 36% of each run, Pallas kernels for 12% -> 10%
where the time goes in v5:
time: 862 us; the launch traced here: 849 us
  waiting for transfers between devices  212 us (25%)
  matrix products  144 us (17%)
  starting transfers between devices  143 us (17%)
  other arithmetic  134 us (16%)
  local copies, waits for them, and re-layouts  109 us (13%)
  Pallas kernels  102 us (12%)
    ppermute x117, waiting for transfers between devices, swap(): lax.ppermute(values, BOTH, [(at, at ^ mask) for at in range(devices)])  212 us
    ppermute x117, starting transfers between devices, swap(): lax.ppermute(values, BOTH, [(at, at ^ mask) for at in range(devices)])  137 us
    pallas_call x2, Pallas kernels, attention_backward(): pl.pallas_call(backward_kernel, grid=(groups,), in_specs=[pl.BlockSpec(me...  54.8 us
    dot_general x20, matrix products, dot_tn(): lax.dot_general(left, right, (((0,), (0,)), ((), ())), preferred_element_...  52.8 us
    dot_general x10, matrix products, dot_nt(): lax.dot_general(left, right, (((1,), (1,)), ((), ())), preferred_element_...  48.1 us
    unnamed x573, local copies, waits for them, and re-layouts  42.8 us
    pallas_call x2, Pallas kernels, attention_forward(): pl.pallas_call(forward_kernel, grid=(groups,), in_specs=[pl.BlockSpec(mem...  36.7 us
    slice x27, local copies, waits for them, and re-layouts, halves_of(): lax.slice_in_dim(values, (2 * at + which) * size, (2 * at + which + 1) *...  28 us
  transfers between devices with their start and end apart: 121, of which 36 were waited for; matrix products, arithmetic and copies ran while one was open for 36% of the time, Pallas kernels for 10%

profile of v5, /device:TPU:9, one launch (start us, length us, event | category | flops | bytes accessed | tf_op | source)
XLA Modules:
  0.0 848.8 jit_solution(11253314116642223247)
XLA Ops:
  13.3 5.7 collective-permute-done.2
  60.3 4.7 collective-permute-done.19
  65.1 4.6 collective-permute-start.25
  75.8 4.5 collective-permute-done.26
  82.5 11.4 %collective-permute-done.28 = bf16[16,768]{1,0:T(8,128)(2,1)S(1)} collective-permute-done((bf16[16,768]{1,0:T(8,128)(2,1)S(1)}, bf16[16,768]{1,0:T(8,128)(2,1)S(1)}, u32[]{:S(2)}, u32[]{:S(2)}) %collective-permute-start.28) | collective-permute-done | bytes 24608 | tf_op jit(solution)/shard_map/ppermute | solution.py:341
  97.0 10.2 %collective-permute-done.24 = bf16[512,256]{1,0:T(8,128)(2,1)S(1)} collective-permute-done((bf16[512,256]{1,0:T(8,128)(2,1)S(1)}, bf16[512,256]{1,0:T(8,128)(2,1)S(1)}, u32[]{:S(2)}, u32[]{:S(2)}) %collective-permute-start.24) | collective-permute-done | bytes 262176 | tf_op jit(solution)/shard_map/ppermute | solution.py:341
  132.4 3.8 collective-permute-start.38
  146.0 18.2 %shard_map.169 = bf16[1024,512]{1,0:T(8,128)(2,1)S(1)} custom-call(f32[4,2]{1,0:T(4,128)S(1)} %multiply_power_fusion.slopes, bf16[1024,512]{1,0:T(8,128)(2,1)S(1)} %copy-done.9, bf16[1024,512]{1,0:T(8,128)(2,1)S(1)} %copy-done.11, bf16[1024,512]{1,0:T(8,128)(2,1)S(1)} %add_convert_fusion.14.value_in, s32[1024,1]{1,0:T(8,128)S(1)} %copy.57.seg_col, ...), custom_call_target="tpu_custom_call" | custom-call | flops 10737418240 | bytes 4194304 | tf_op jit(solution)/shard_map/pallas_call | solution.py:170
  177.0 5.0 fusion.155
  184.7 11.3 %collective-permute-done.46 = bf16[256,512]{1,0:T(8,128)(2,1)S(1)} collective-permute-done((bf16[256,512]{1,0:T(8,128)(2,1)S(1)}, bf16[256,512]{1,0:T(8,128)(2,1)S(1)}, u32[]{:S(2)}, u32[]{:S(2)}) %collective-permute-start.46) | collective-permute-done | bytes 262176 | tf_op jit(solution)/shard_map/ppermute | solution.py:341
  214.7 37.9 %collective-permute-done.50 = bf16[256,1024]{1,0:T(8,128)(2,1)S(1)} collective-permute-done((bf16[256,1024]{1,0:T(8,128)(2,1)S(1)}, bf16[256,1024]{1,0:T(8,128)(2,1)S(1)}, u32[]{:S(2)}, u32[]{:S(2)}) %collective-permute-start.50) | collective-permute-done | bytes 524320 | tf_op jit(solution)/shard_map/ppermute | solution.py:341
  269.7 6.1 shard_map.171
  279.1 9.0 %multiply_convert_fusion.1 = (bf16[1024,2048]{1,0:T(8,128)(2,1)S(1)}, f32[1024,2048]{1,0:T(8,128)}) fusion(f32[2048]{0:T(1024)S(1)} %bitcast.265, bf16[1024,1024]{0,1:T(8,128)(2,1)S(1)} %copy-done.57, bf16[1024,2048]{1,0:T(8,128)(2,1)S(1)} %shard_map.170), kind=kOutput, calls=%fused_computation.17 | convolution fusion | flops 4315938816 | bytes 18882560 | tf_op jit(solution)/shard_map/dot_general | solution.py:677
  289.0 5.9 convolution_convert_fusion.12
  294.9 5.2 collective-permute-start.55
  309.1 15.8 %collective-permute-done.56 = bf16[512,1024]{1,0:T(8,128)(2,1)S(1)} collective-permute-done((bf16[512,1024]{1,0:T(8,128)(2,1)S(1)}, bf16[512,1024]{1,0:T(8,128)(2,1)S(1)}, u32[]{:S(2)}, u32[]{:S(2)}) %collective-permute-start.56) | collective-permute-done | bytes 1048608 | tf_op jit(solution)/shard_map/ppermute | solution.py:341
  327.3 3.8 add_convert_fusion.query_in.key_in.value_in
  331.1 18.5 %shard_map.172 = bf16[1024,512]{1,0:T(8,128)(2,1)S(1)} custom-call(f32[4,2]{1,0:T(4,128)S(1)} %multiply_power_fusion.slopes, bf16[1024,1536]{1,0:T(8,128)(2,1)S(1)} %add_convert_fusion.query_in.key_in.value_in, bf16[1024,1536]{1,0:T(8,128)(2,1)S(1)} %add_convert_fusion.query_in.key_in.value_in, ...), custom_call_target="tpu_custom_call" | custom-call | flops 10737418240 | bytes 4194304 | tf_op jit(solution)/shard_map/pallas_call | solution.py:170
  360.2 39.4 %collective-permute-done.59.second = bf16[512,2048]{1,0:T(8,128)(2,1)S(1)} collective-permute-done((bf16[512,2048]{1,0:T(8,128)(2,1)S(1)}, bf16[512,2048]{1,0:T(8,128)(2,1)S(1)}, u32[]{:S(2)}, u32[]{:S(2)}) %collective-permute-start.59) | collective-permute-done | bytes 2097184 | tf_op jit(solution)/shard_map/ppermute | solution.py:341
  402.0 9.8 %multiply_convert_fusion = (bf16[1024,2048]{1,0:T(8,128)(2,1)}, f32[1024,2048]{1,0:T(8,128)}) fusion(f32[2048]{0:T(1024)S(1)} %bitcast.267, bf16[1024,1024]{0,1:T(8,128)(2,1)S(1)} %add_convert_fusion.3, bf16[1024,2048]{1,0:T(8,128)(2,1)S(1)} %shard_map.173), kind=kOutput, calls=%fused_computation.16 | convolution fusion | flops 4315938816 | bytes 18882560 | tf_op jit(solution)/shard_map/dot_general | solution.py:677
  412.9 12.2 %fusion.204 = (f32[2048]{0:T(1024)S(1)}, bf16[1024,2048]{1,0:T(8,128)(2,1)S(1)}) fusion(f32[1024,2048]{1,0:T(8,128)} %get-tuple-element.664, f32[2048]{0:T(1024)S(1)} %bitcast.268, bf16[2048,1024]{1,0:T(8,128)(2,1)S(1)} %shard_map.174, bf16[1024,256]{0,1:T(8,128)(2,1)S(1)} %get-tuple-element.391, bf16[1024,256]{0,1:T(8,128)(2,1)S(1)} %get-tuple-element.392, ...), kind=kOutput, calls=%fused_computation.634 | convolution fusion | flops 4349491200 | bytes 18890752 | tf_op jit(solution)/shard_map/dot_general | solution.py:23
  425.1 5.2 convolution_convert_fusion.9
  431.2 5.8 convolution_convert_fusion.10
  437.0 3.7 convolution_convert_fusion.6
  440.7 3.7 convolution_convert_fusion.4
  444.4 3.8 convolution_convert_fusion.7
  453.4 6.1 convolution_convert_fusion.5
  459.5 4.4 multiply_reduce_fusion
  463.9 7.2 fusion.152
  479.7 27.3 %shard_map.175 = (bf16[3,1024,512]{2,1,0:T(8,128)(2,1)S(1)}, f32[4,2,128]{2,1,0:T(2,128)S(1)}) custom-call(f32[4,2]{1,0:T(4,128)S(1)} %multiply_power_fusion.slopes, bf16[1024,1536]{1,0:T(8,128)(2,1)} %copy-done.13, bf16[1024,1536]{1,0:T(8,128)(2,1)} %copy-done.13, bf16[1024,1536]{1,0:T(8,128)(2,1)} %copy-done.13, ...), custom_call_target="tpu_custom_call" | custom-call | flops 17179869184 | bytes 7340032 | tf_op jit(solution)/shard_map/pallas_call | solution.py:196
  512.6 4.1 fusion.44
  541.2 5.4 multiply_reduce_fusion.1
  555.0 12.0 %fusion.150 = (f32[2048]{0:T(1024)}, bf16[1024,2048]{1,0:T(8,128)(2,1)}) fusion(f32[1024,2048]{1,0:T(8,128)S(1)} %bitcast.276, f32[2048]{0:T(1024)S(1)} %bitcast.266, bf16[1024,1024]{0,1:T(8,128)(2,1)S(1)} %convert_element_type.945, bf16[2048,1024]{1,0:T(8,128)(2,1)S(1)} %copy-done.2), kind=kOutput, calls=%fused_computation.581 | convolution fusion | flops 4341102592 | bytes 18890752 | tf_op jit(solution)/shard_map/dot_general | solution.py:23
  576.2 3.9 convolution_convert_fusion.3
  580.7 6.1 convolution_convert_fusion.2
  587.6 5.0 collective-permute-done.71
  594.2 8.1 convolution_convert_fusion.8
  615.2 3.7 convolution_convert_fusion.1
  630.6 15.6 %collective-permute-done.79 = bf16[512,768]{1,0:T(8,128)(2,1)S(1)} collective-permute-done((bf16[512,768]{1,0:T(8,128)(2,1)S(1)}, bf16[512,768]{1,0:T(8,128)(2,1)S(1)}, u32[]{:S(2)}, u32[]{:S(2)}) %collective-permute-start.79) | collective-permute-done | bytes 786464 | tf_op jit(solution)/shard_map/ppermute | solution.py:341
  647.2 27.5 %shard_map.176 = (bf16[3,1024,512]{2,1,0:T(8,128)(2,1)}, f32[4,2,128]{2,1,0:T(2,128)S(1)}) custom-call(f32[4,2]{1,0:T(4,128)S(1)} %multiply_power_fusion.slopes, bf16[1024,512]{1,0:T(8,128)(2,1)S(1)} %copy-done.10, bf16[1024,512]{1,0:T(8,128)(2,1)S(1)} %copy-done.12, bf16[1024,512]{1,0:T(8,128)(2,1)S(1)} %copy-done.8, ...), custom_call_target="tpu_custom_call" | custom-call | flops 17179869184 | bytes 7340032 | tf_op jit(solution)/shard_map/pallas_call | solution.py:196
  697.7 8.9 %collective-permute-done.82 = bf16[2048,256]{1,0:T(8,128)(2,1)S(1)} collective-permute-done((bf16[2048,256]{1,0:T(8,128)(2,1)S(1)}, bf16[2048,256]{1,0:T(8,128)(2,1)S(1)}, u32[]{:S(2)}, u32[]{:S(2)}) %collective-permute-start.82) | collective-permute-done | bytes 1048608 | tf_op jit(solution)/shard_map/ppermute | solution.py:341
  738.9 4.8 fusion.24
  743.8 5.4 fusion.23
  764.4 8.3 collective-permute-done.97
  793.4 3.9 collective-permute-done.105
  802.8 3.8 collective-permute-start.120
  808.1 5.3 collective-permute-done.108
  829.5 8.5 collective-permute-start.119
  (1135 shorter events, 392.9 us)
Async XLA Ops:
  51.7 30.1 %collective-permute-start.23 = (bf16[256,512]{1,0:T(8,128)(2,1)S(1)}, bf16[256,512]{1,0:T(8,128)(2,1)S(1)}, u32[]{:S(2)}, u32[]{:S(2)}) collective-permute-start(bf16[256,512]{1,0:T(8,128)(2,1)S(1)} %pad_maximum_fusion.32), channel_id=1, source_target_pairs={{0,2},{1,3},{2,0},{3,1},{4,6},{5,7},{6,4},{7,5},{8,10},{9,11},{10,... | collective-permute-start | bytes 786440 | tf_op jit(solution)/shard_map/ppermute | solution.py:341
  70.8 36.4 %collective-permute-start.31 = (bf16[1024,256]{1,0:T(8,128)(2,1)S(1)}, bf16[1024,256]{1,0:T(8,128)(2,1)S(1)}, u32[]{:S(2)}, u32[]{:S(2)}) collective-permute-start(bf16[1024,256]{1,0:T(8,128)(2,1)S(1)} %pad_maximum_fusion.24), channel_id=1, source_target_pairs={{0,1},{1,0},{2,3},{3,2},{4,5},{5,4},{6,7},{7,6},{8,9},{9,8},{10,11... | collective-permute-start | bytes 1572872 | tf_op jit(solution)/shard_map/ppermute | solution.py:341
  75.0 32.2 %collective-permute-start.32 = (bf16[256,1024]{1,0:T(8,128)(2,1)S(1)}, bf16[256,1024]{1,0:T(8,128)(2,1)S(1)}, u32[]{:S(2)}, u32[]{:S(2)}) collective-permute-start(bf16[256,1024]{1,0:T(8,128)(2,1)S(1)} %pad_maximum_fusion.25), channel_id=1, source_target_pairs={{0,1},{1,0},{2,3},{3,2},{4,5},{5,4},{6,7},{7,6},{8,9},{9,8},{10,11... | collective-permute-start | bytes 1572872 | tf_op jit(solution)/shard_map/ppermute | solution.py:341
  80.4 26.8 %collective-permute-start.29 = (bf16[512,512]{1,0:T(8,128)(2,1)S(1)}, bf16[512,512]{1,0:T(8,128)(2,1)S(1)}, u32[]{:S(2)}, u32[]{:S(2)}) collective-permute-start(bf16[512,512]{1,0:T(8,128)(2,1)S(1)} %pad_maximum_fusion.22), channel_id=1, source_target_pairs={{0,16},{1,17},{2,18},{3,19},{4,20},{5,21},{6,22},{7,23},{8,24},{9,... | collective-permute-start | bytes 1572872 | tf_op jit(solution)/shard_map/ppermute | solution.py:341
  81.6 25.5 %collective-permute-start.30 = (bf16[512,512]{1,0:T(8,128)(2,1)S(1)}, bf16[512,512]{1,0:T(8,128)(2,1)S(1)}, u32[]{:S(2)}, u32[]{:S(2)}) collective-permute-start(bf16[512,512]{1,0:T(8,128)(2,1)S(1)} %pad_maximum_fusion.23), channel_id=1, source_target_pairs={{0,8},{1,9},{2,10},{3,11},{4,12},{5,13},{6,14},{7,15},{8,0},{9,1},... | collective-permute-start | bytes 1572872 | tf_op jit(solution)/shard_map/ppermute | solution.py:341
  129.5 34.8 %collective-permute-start.36 = (bf16[512,1024]{0,1:T(8,128)(2,1)}, bf16[512,1024]{0,1:T(8,128)(2,1)S(1)}, u32[]{:S(2)}, u32[]{:S(2)}) collective-permute-start(bf16[512,1024]{0,1:T(8,128)(2,1)} %copy.59), channel_id=1, source_target_pairs={{1,4},{3,6},{4,1},{6,3},{9,12},{11,14},{12,9},{14,11},{17,20},{19,... | collective-permute-start | bytes 3145736 | tf_op jit(solution)/shard_map/ppermute | solution.py:350
  132.1 33.8 %collective-permute-start.37 = (bf16[256,1024]{1,0:T(8,128)(2,1)}, bf16[256,1024]{1,0:T(8,128)(2,1)S(1)}, u32[]{:S(2)}, u32[]{:S(2)}) collective-permute-start(bf16[256,1024]{1,0:T(8,128)(2,1)} %constant_dynamic-update-slice_fusion), channel_id=1, source_target_pairs={{0,8},{1,9},{2,10},{3,11},{4,12},{5,13},{6,14},{7,15},{8,0},{9,1},... | collective-permute-start | bytes 1572872 | tf_op jit(solution)/shard_map/ppermute | solution.py:341
  132.4 33.5 %collective-permute-start.38 = (bf16[1024,256]{1,0:T(8,128)(2,1)S(1)}, bf16[1024,256]{1,0:T(8,128)(2,1)S(1)}, u32[]{:S(2)}, u32[]{:S(2)}) collective-permute-start(bf16[1024,256]{1,0:T(8,128)(2,1)S(1)} %pad_maximum_fusion.26), channel_id=1, source_target_pairs={{0,1},{1,0},{2,3},{3,2},{4,5},{5,4},{6,7},{7,6},{8,9},{9,8},{10,11... | collective-permute-start | bytes 1572872 | tf_op jit(solution)/shard_map/ppermute | solution.py:341
  142.0 23.9 %collective-permute-start.39 = (bf16[256,768]{1,0:T(8,128)(2,1)}, bf16[256,768]{1,0:T(8,128)(2,1)S(1)}, u32[]{:S(2)}, u32[]{:S(2)}) collective-permute-start(bf16[256,768]{1,0:T(8,128)(2,1)} %constant_dynamic-update-slice_fusion.2), channel_id=1, source_target_pairs={{0,16},{1,17},{2,18},{3,19},{4,20},{5,21},{6,22},{7,23},{8,24},{9,... | collective-permute-start | bytes 1179656 | tf_op jit(solution)/shard_map/ppermute | solution.py:341
  143.2 22.7 %collective-permute-start.40 = (bf16[256,256]{1,0:T(8,128)(2,1)S(1)}, bf16[256,256]{1,0:T(8,128)(2,1)S(1)}, u32[]{:S(2)}, u32[]{:S(2)}) collective-permute-start(bf16[256,256]{1,0:T(8,128)(2,1)S(1)} %constant_dynamic-update-slice_fusion.8), channel_id=1, source_target_pairs={{0,16},{1,17},{2,18},{3,19},{4,20},{5,21},{6,22},{7,23},{8,24},{9,... | collective-permute-start | bytes 393224 | tf_op jit(solution)/shard_map/ppermute | solution.py:341
  169.0 27.1 %collective-permute-start.43 = (bf16[512,1024]{1,0:T(8,128)(2,1)S(1)}, bf16[512,1024]{1,0:T(8,128)(2,1)S(1)}, u32[]{:S(2)}, u32[]{:S(2)}) collective-permute-start(bf16[512,1024]{1,0:T(8,128)(2,1)S(1)} %pad_maximum_fusion.9), channel_id=1, source_target_pairs={{0,1},{1,0},{2,3},{3,2},{4,5},{5,4},{6,7},{7,6},{8,9},{9,8},{10,11... | collective-permute-start | bytes 3145736 | tf_op jit(solution)/shard_map/ppermute | solution.py:341
  170.0 26.1 %collective-permute-start.44 = (bf16[2048,256]{1,0:T(8,128)(2,1)S(1)}, bf16[2048,256]{1,0:T(8,128)(2,1)S(1)}, u32[]{:S(2)}, u32[]{:S(2)}) collective-permute-start(bf16[2048,256]{1,0:T(8,128)(2,1)S(1)} %pad_maximum_fusion.15), channel_id=1, source_target_pairs={{0,16},{1,17},{2,18},{3,19},{4,20},{5,21},{6,22},{7,23},{8,24},{9,... | collective-permute-start | bytes 3145736 | tf_op jit(solution)/shard_map/ppermute | solution.py:341
  172.4 23.7 %collective-permute-start.45 = (bf16[512,768]{1,0:T(8,128)(2,1)S(1)}, bf16[512,768]{1,0:T(8,128)(2,1)S(1)}, u32[]{:S(2)}, u32[]{:S(2)}) collective-permute-start(bf16[512,768]{1,0:T(8,128)(2,1)S(1)} %pad_maximum_fusion.20), channel_id=1, source_target_pairs={{0,8},{1,9},{2,10},{3,11},{4,12},{5,13},{6,14},{7,15},{8,0},{9,1},... | collective-permute-start | bytes 2359304 | tf_op jit(solution)/shard_map/ppermute | solution.py:341
  196.8 58.9 %collective-permute-start.47 = (bf16[512,2048]{1,0:T(8,128)(2,1)S(1)}, bf16[512,2048]{1,0:T(8,128)(2,1)}, u32[]{:S(2)}, u32[]{:S(2)}) collective-permute-start(bf16[512,2048]{1,0:T(8,128)(2,1)S(1)} %pad_maximum_fusion.3.first), channel_id=1, source_target_pairs={{0,16},{1,17},{2,18},{3,19},{4,20},{5,21},{6,22},{7,23},{8,24},{9,... | collective-permute-start | bytes 6291464 | tf_op jit(solution)/shard_map/ppermute | solution.py:341
  198.6 57.1 %collective-permute-start.48 = (bf16[2048,512]{1,0:T(8,128)(2,1)}, bf16[2048,512]{1,0:T(8,128)(2,1)}, u32[]{:S(2)}, u32[]{:S(2)}) collective-permute-start(bf16[2048,512]{1,0:T(8,128)(2,1)} %pad_maximum_fusion.4.first), channel_id=1, source_target_pairs={{0,8},{1,9},{2,10},{3,11},{4,12},{5,13},{6,14},{7,15},{8,0},{9,1},... | collective-permute-start | bytes 6291464 | tf_op jit(solution)/shard_map/ppermute | solution.py:341
  202.1 53.6 %collective-permute-start.49 = (bf16[1024,768]{1,0:T(8,128)(2,1)}, bf16[1024,768]{1,0:T(8,128)(2,1)}, u32[]{:S(2)}, u32[]{:S(2)}) collective-permute-start(bf16[1024,768]{1,0:T(8,128)(2,1)} %pad_maximum_fusion.8), channel_id=1, source_target_pairs={{0,1},{1,0},{2,3},{3,2},{4,5},{5,4},{6,7},{7,6},{8,9},{9,8},{10,11... | collective-permute-start | bytes 4718600 | tf_op jit(solution)/shard_map/ppermute | solution.py:341
  205.8 71.2 %collective-permute-start.51 = (bf16[256,512]{1,0:T(8,128)(2,1)}, bf16[256,512]{1,0:T(8,128)(2,1)S(1)}, u32[]{:S(2)}, u32[]{:S(2)}) collective-permute-start(bf16[256,512]{1,0:T(8,128)(2,1)} %pad_maximum_fusion.38), channel_id=1, source_target_pairs={{0,2},{1,3},{2,0},{3,1},{4,6},{5,7},{6,4},{7,5},{8,10},{9,11},{10,... | collective-permute-start | bytes 786440 | tf_op jit(solution)/shard_map/ppermute | solution.py:341
  212.2 40.3 %collective-permute-start.50 = (bf16[256,1024]{1,0:T(8,128)(2,1)S(1)}, bf16[256,1024]{1,0:T(8,128)(2,1)S(1)}, u32[]{:S(2)}, u32[]{:S(2)}) collective-permute-start(bf16[256,1024]{1,0:T(8,128)(2,1)S(1)} %pad_maximum_fusion.27), channel_id=1, source_target_pairs={{0,1},{1,0},{2,3},{3,2},{4,5},{5,4},{6,7},{7,6},{8,9},{9,8},{10,11... | collective-permute-start | bytes 1572872 | tf_op jit(solution)/shard_map/ppermute | solution.py:341
  252.6 24.5 %collective-permute-start.52 = (bf16[512,256]{1,0:T(8,128)(2,1)S(1)}, bf16[512,256]{1,0:T(8,128)(2,1)S(1)}, u32[]{:S(2)}, u32[]{:S(2)}) collective-permute-start(bf16[512,256]{1,0:T(8,128)(2,1)S(1)} %pad_maximum_fusion.39), channel_id=1, source_target_pairs={{0,2},{1,3},{2,0},{3,1},{4,6},{5,7},{6,4},{7,5},{8,10},{9,11},{10,... | collective-permute-start | bytes 786440 | tf_op jit(solution)/shard_map/ppermute | solution.py:341
  300.2 24.8 %collective-permute-start.56 = (bf16[512,1024]{1,0:T(8,128)(2,1)S(1)}, bf16[512,1024]{1,0:T(8,128)(2,1)S(1)}, u32[]{:S(2)}, u32[]{:S(2)}) collective-permute-start(bf16[512,1024]{1,0:T(8,128)(2,1)S(1)} %pad_maximum_fusion.10), channel_id=1, source_target_pairs={{0,1},{1,0},{2,3},{3,2},{4,5},{5,4},{6,7},{7,6},{8,9},{9,8},{10,11... | collective-permute-start | bytes 3145736 | tf_op jit(solution)/shard_map/ppermute | solution.py:341
  302.5 24.8 %collective-permute-start.57 = (bf16[2048,256]{1,0:T(8,128)(2,1)S(1)}, bf16[2048,256]{1,0:T(8,128)(2,1)S(1)}, u32[]{:S(2)}, u32[]{:S(2)}) collective-permute-start(bf16[2048,256]{1,0:T(8,128)(2,1)S(1)} %pad_maximum_fusion.17), channel_id=1, source_target_pairs={{0,16},{1,17},{2,18},{3,19},{4,20},{5,21},{6,22},{7,23},{8,24},{9,... | collective-permute-start | bytes 3145736 | tf_op jit(solution)/shard_map/ppermute | solution.py:341
  352.3 47.3 %collective-permute-start.59 = (bf16[512,2048]{1,0:T(8,128)(2,1)S(1)}, bf16[512,2048]{1,0:T(8,128)(2,1)S(1)}, u32[]{:S(2)}, u32[]{:S(2)}) collective-permute-start(bf16[512,2048]{1,0:T(8,128)(2,1)S(1)} %pad_maximum_fusion.5.first), channel_id=1, source_target_pairs={{0,16},{1,17},{2,18},{3,19},{4,20},{5,21},{6,22},{7,23},{8,24},{9,... | collective-permute-start | bytes 6291464 | tf_op jit(solution)/shard_map/ppermute | solution.py:341
  357.3 54.5 %collective-permute-start.60 = (bf16[2048,512]{1,0:T(8,128)(2,1)S(1)}, bf16[2048,512]{1,0:T(8,128)(2,1)S(1)}, u32[]{:S(2)}, u32[]{:S(2)}) collective-permute-start(bf16[2048,512]{1,0:T(8,128)(2,1)S(1)} %pad_maximum_fusion.6.first), channel_id=1, source_target_pairs={{0,8},{1,9},{2,10},{3,11},{4,12},{5,13},{6,14},{7,15},{8,0},{9,1},... | collective-permute-start | bytes 6291464 | tf_op jit(solution)/shard_map/ppermute | solution.py:341
  430.3 29.2 %collective-permute-start.63 = (bf16[1024,1024]{0,1:T(8,128)(2,1)S(1)}, bf16[1024,1024]{0,1:T(8,128)(2,1)}, u32[]{:S(2)}, u32[]{:S(2)}) collective-permute-start(bf16[1024,1024]{0,1:T(8,128)(2,1)S(1)} %convolution_convert_fusion.9), channel_id=1, source_target_pairs={{0,4},{1,5},{2,6},{3,7},{4,0},{5,1},{6,2},{7,3},{8,12},{9,13},{10,... | collective-permute-start | bytes 6291464 | tf_op jit(solution)/shard_map/ppermute | solution.py:341
  440.6 23.3 %collective-permute-start.61 = (bf16[1024,1024]{0,1:T(8,128)(2,1)}, bf16[1024,1024]{0,1:T(8,128)(2,1)}, u32[]{:S(2)}, u32[]{:S(2)}) collective-permute-start(bf16[1024,1024]{0,1:T(8,128)(2,1)} %convolution_convert_fusion.10), channel_id=1, source_target_pairs={{0,4},{1,5},{2,6},{3,7},{4,0},{5,1},{6,2},{7,3},{8,12},{9,13},{10,... | collective-permute-start | bytes 6291464 | tf_op jit(solution)/shard_map/ppermute | solution.py:341
  448.2 62.5 %collective-permute-start.64 = (bf16[2048,512]{1,0:T(8,128)(2,1)}, bf16[2048,512]{1,0:T(8,128)(2,1)}, u32[]{:S(2)}, u32[]{:S(2)}) collective-permute-start(bf16[2048,512]{1,0:T(8,128)(2,1)} %convolution_convert_fusion.7), channel_id=1, source_target_pairs={{0,8},{1,9},{2,10},{3,11},{4,12},{5,13},{6,14},{7,15},{8,0},{9,1},... | collective-permute-start | bytes 6291464 | tf_op jit(solution)/shard_map/ppermute | solution.py:341
  449.1 61.6 %collective-permute-start.65 = (bf16[512,2048]{1,0:T(8,128)(2,1)}, bf16[512,2048]{1,0:T(8,128)(2,1)}, u32[]{:S(2)}, u32[]{:S(2)}) collective-permute-start(bf16[512,2048]{1,0:T(8,128)(2,1)} %convolution_convert_fusion.6), channel_id=1, source_target_pairs={{0,16},{1,17},{2,18},{3,19},{4,20},{5,21},{6,22},{7,23},{8,24},{9,... | collective-permute-start | bytes 6291464 | tf_op jit(solution)/shard_map/ppermute | solution.py:341
  472.4 63.1 %collective-permute-start.62 = (bf16[512,1024]{0,1:T(8,128)(2,1)}, bf16[512,1024]{0,1:T(8,128)(2,1)}, u32[]{:S(2)}, u32[]{:S(2)}) collective-permute-start(bf16[512,1024]{0,1:T(8,128)(2,1)} %fusion.52), channel_id=1, source_target_pairs={{1,4},{3,6},{4,1},{6,3},{9,12},{11,14},{12,9},{14,11},{17,20},{19,... | collective-permute-start | bytes 3145736 | tf_op jit(solution)/shard_map/ppermute | solution.py:350
  477.0 33.8 %collective-permute-start.66 = (bf16[256,1024]{1,0:T(8,128)(2,1)}, bf16[256,1024]{1,0:T(8,128)(2,1)}, u32[]{:S(2)}, u32[]{:S(2)}) collective-permute-start(bf16[256,1024]{1,0:T(8,128)(2,1)} %convolution_convert_fusion.24), channel_id=1, source_target_pairs={{0,1},{1,0},{2,3},{3,2},{4,5},{5,4},{6,7},{7,6},{8,9},{9,8},{10,11... | collective-permute-start | bytes 1572872 | tf_op jit(solution)/shard_map/ppermute | solution.py:341
  516.7 24.5 %collective-permute-start.67 = (bf16[1024,1024]{0,1:T(8,128)(2,1)S(1)}, bf16[1024,1024]{0,1:T(8,128)(2,1)}, u32[]{:S(2)}, u32[]{:S(2)}) collective-permute-start(bf16[1024,1024]{0,1:T(8,128)(2,1)S(1)} %fusion.44), channel_id=1, source_target_pairs={{0,4},{1,5},{2,6},{3,7},{4,0},{5,1},{6,2},{7,3},{8,12},{9,13},{10,... | collective-permute-start | bytes 6291464 | tf_op jit(solution)/shard_map/ppermute | solution.py:341
  520.0 30.4 %collective-permute-start.68 = (bf16[2048,256]{1,0:T(8,128)(2,1)}, bf16[2048,256]{1,0:T(8,128)(2,1)}, u32[]{:S(2)}, u32[]{:S(2)}) collective-permute-start(bf16[2048,256]{1,0:T(8,128)(2,1)} %get-tuple-element.353), channel_id=1, source_target_pairs={{0,16},{1,17},{2,18},{3,19},{4,20},{5,21},{6,22},{7,23},{8,24},{9,... | collective-permute-start | bytes 3145736 | tf_op jit(solution)/shard_map/ppermute | solution.py:341
  523.3 27.0 %collective-permute-start.69 = (bf16[512,1024]{1,0:T(8,128)(2,1)}, bf16[512,1024]{1,0:T(8,128)(2,1)}, u32[]{:S(2)}, u32[]{:S(2)}) collective-permute-start(bf16[512,1024]{1,0:T(8,128)(2,1)} %add_convert_fusion.12), channel_id=1, source_target_pairs={{0,1},{1,0},{2,3},{3,2},{4,5},{5,4},{6,7},{7,6},{8,9},{9,8},{10,11... | collective-permute-start | bytes 3145736 | tf_op jit(solution)/shard_map/ppermute | solution.py:341
  525.7 24.6 %collective-permute-start.70 = (bf16[256,512]{1,0:T(8,128)(2,1)}, bf16[256,512]{1,0:T(8,128)(2,1)}, u32[]{:S(2)}, u32[]{:S(2)}) collective-permute-start(bf16[256,512]{1,0:T(8,128)(2,1)} %add_convert_fusion.45), channel_id=1, source_target_pairs={{0,8},{1,9},{2,10},{3,11},{4,12},{5,13},{6,14},{7,15},{8,0},{9,1},... | collective-permute-start | bytes 786440 | tf_op jit(solution)/shard_map/ppermute | solution.py:341
  535.6 52.0 %collective-permute-start.74 = (bf16[1024,768]{1,0:T(8,128)(2,1)}, bf16[1024,768]{1,0:T(8,128)(2,1)}, u32[]{:S(2)}, u32[]{:S(2)}) collective-permute-start(bf16[1024,768]{1,0:T(8,128)(2,1)} %convolution_convert_fusion.15), channel_id=1, source_target_pairs={{0,1},{1,0},{2,3},{3,2},{4,5},{5,4},{6,7},{7,6},{8,9},{9,8},{10,11... | collective-permute-start | bytes 4718600 | tf_op jit(solution)/shard_map/ppermute | solution.py:341
  569.3 23.3 %collective-permute-start.71 = (bf16[1024,256]{1,0:T(8,128)(2,1)}, bf16[1024,256]{1,0:T(8,128)(2,1)S(1)}, u32[]{:S(2)}, u32[]{:S(2)}) collective-permute-start(bf16[1024,256]{1,0:T(8,128)(2,1)} %add_convert_fusion.25), channel_id=1, source_target_pairs={{0,1},{1,0},{2,3},{3,2},{4,5},{5,4},{6,7},{7,6},{8,9},{9,8},{10,11... | collective-permute-start | bytes 1572872 | tf_op jit(solution)/shard_map/ppermute | solution.py:341
  580.1 67.1 %collective-permute-start.80 = (bf16[2048,512]{1,0:T(8,128)(2,1)}, bf16[2048,512]{1,0:T(8,128)(2,1)}, u32[]{:S(2)}, u32[]{:S(2)}) collective-permute-start(bf16[2048,512]{1,0:T(8,128)(2,1)} %convolution_convert_fusion.3), channel_id=1, source_target_pairs={{0,8},{1,9},{2,10},{3,11},{4,12},{5,13},{6,14},{7,15},{8,0},{9,1},... | collective-permute-start | bytes 6291464 | tf_op jit(solution)/shard_map/ppermute | solution.py:341
  603.9 26.7 %collective-permute-start.76 = (bf16[512,256]{1,0:T(8,128)(2,1)S(1)}, bf16[512,256]{1,0:T(8,128)(2,1)S(1)}, u32[]{:S(2)}, u32[]{:S(2)}) collective-permute-start(bf16[512,256]{1,0:T(8,128)(2,1)S(1)} %add_convert_fusion.43), channel_id=1, source_target_pairs={{0,2},{1,3},{2,0},{3,1},{4,6},{5,7},{6,4},{7,5},{8,10},{9,11},{10,... | collective-permute-start | bytes 786440 | tf_op jit(solution)/shard_map/ppermute | solution.py:341
  604.1 26.5 %collective-permute-start.77 = (bf16[256,512]{1,0:T(8,128)(2,1)S(1)}, bf16[256,512]{1,0:T(8,128)(2,1)S(1)}, u32[]{:S(2)}, u32[]{:S(2)}) collective-permute-start(bf16[256,512]{1,0:T(8,128)(2,1)S(1)} %add_convert_fusion.42), channel_id=1, source_target_pairs={{0,2},{1,3},{2,0},{3,1},{4,6},{5,7},{6,4},{7,5},{8,10},{9,11},{10,... | collective-permute-start | bytes 786440 | tf_op jit(solution)/shard_map/ppermute | solution.py:341
  618.8 27.4 %collective-permute-start.79 = (bf16[512,768]{1,0:T(8,128)(2,1)S(1)}, bf16[512,768]{1,0:T(8,128)(2,1)S(1)}, u32[]{:S(2)}, u32[]{:S(2)}) collective-permute-start(bf16[512,768]{1,0:T(8,128)(2,1)S(1)} %add_convert_fusion.17), channel_id=1, source_target_pairs={{0,8},{1,9},{2,10},{3,11},{4,12},{5,13},{6,14},{7,15},{8,0},{9,1},... | collective-permute-start | bytes 2359304 | tf_op jit(solution)/shard_map/ppermute | solution.py:341
  629.5 68.3 %collective-permute-start.83 = (bf16[512,2048]{1,0:T(8,128)(2,1)}, bf16[512,2048]{1,0:T(8,128)(2,1)}, u32[]{:S(2)}, u32[]{:S(2)}) collective-permute-start(bf16[512,2048]{1,0:T(8,128)(2,1)} %convolution_convert_fusion.1), channel_id=1, source_target_pairs={{0,16},{1,17},{2,18},{3,19},{4,20},{5,21},{6,22},{7,23},{8,24},{9,... | collective-permute-start | bytes 6291464 | tf_op jit(solution)/shard_map/ppermute | solution.py:341
  679.0 27.6 %collective-permute-start.82 = (bf16[2048,256]{1,0:T(8,128)(2,1)S(1)}, bf16[2048,256]{1,0:T(8,128)(2,1)S(1)}, u32[]{:S(2)}, u32[]{:S(2)}) collective-permute-start(bf16[2048,256]{1,0:T(8,128)(2,1)S(1)} %get-tuple-element.350), channel_id=1, source_target_pairs={{0,16},{1,17},{2,18},{3,19},{4,20},{5,21},{6,22},{7,23},{8,24},{9,... | collective-permute-start | bytes 3145736 | tf_op jit(solution)/shard_map/ppermute | solution.py:341
  712.0 25.7 %collective-permute-start.85 = (bf16[1024,1024]{0,1:T(8,128)(2,1)S(1)}, bf16[1024,1024]{0,1:T(8,128)(2,1)S(1)}, u32[]{:S(2)}, u32[]{:S(2)}) collective-permute-start(bf16[1024,1024]{0,1:T(8,128)(2,1)S(1)} %add_convert_fusion.1), channel_id=1, source_target_pairs={{0,4},{1,5},{2,6},{3,7},{4,0},{5,1},{6,2},{7,3},{8,12},{9,13},{10,... | collective-permute-start | bytes 6291464 | tf_op jit(solution)/shard_map/ppermute | solution.py:341
  717.1 32.1 %collective-permute-start.86 = (bf16[256,384]{1,0:T(8,128)(2,1)S(1)}, bf16[256,384]{1,0:T(8,128)(2,1)S(1)}, u32[]{:S(2)}, u32[]{:S(2)}) collective-permute-start(bf16[256,384]{1,0:T(8,128)(2,1)S(1)} %add_convert_fusion.47), channel_id=1, source_target_pairs={{0,2},{1,3},{2,0},{3,1},{4,6},{5,7},{6,4},{7,5},{8,10},{9,11},{10,... | collective-permute-start | bytes 589832 | tf_op jit(solution)/shard_map/ppermute | solution.py:341
  720.0 42.7 %collective-permute-start.93 = (bf16[1024,256]{1,0:T(8,128)(2,1)}, bf16[1024,256]{1,0:T(8,128)(2,1)}, u32[]{:S(2)}, u32[]{:S(2)}) collective-permute-start(bf16[1024,256]{1,0:T(8,128)(2,1)} %add_convert_fusion.21), channel_id=1, source_target_pairs={{0,1},{1,0},{2,3},{3,2},{4,5},{5,4},{6,7},{7,6},{8,9},{9,8},{10,11... | collective-permute-start | bytes 1572872 | tf_op jit(solution)/shard_map/ppermute | solution.py:341
  723.3 49.9 %collective-permute-start.94 = (bf16[512,1024]{1,0:T(8,128)(2,1)}, bf16[512,1024]{1,0:T(8,128)(2,1)}, u32[]{:S(2)}, u32[]{:S(2)}) collective-permute-start(bf16[512,1024]{1,0:T(8,128)(2,1)} %add_convert_fusion.7), channel_id=1, source_target_pairs={{0,1},{1,0},{2,3},{3,2},{4,5},{5,4},{6,7},{7,6},{8,9},{9,8},{10,11... | collective-permute-start | bytes 3145736 | tf_op jit(solution)/shard_map/ppermute | solution.py:341
  726.4 32.4 %collective-permute-start.95 = (bf16[256,512]{1,0:T(8,128)(2,1)}, bf16[256,512]{1,0:T(8,128)(2,1)}, u32[]{:S(2)}, u32[]{:S(2)}) collective-permute-start(bf16[256,512]{1,0:T(8,128)(2,1)} %add_convert_fusion.39), channel_id=1, source_target_pairs={{0,8},{1,9},{2,10},{3,11},{4,12},{5,13},{6,14},{7,15},{8,0},{9,1},... | collective-permute-start | bytes 786440 | tf_op jit(solution)/shard_map/ppermute | solution.py:341
  737.7 26.6 %collective-permute-start.96 = (bf16[512,512]{1,0:T(8,128)(2,1)}, bf16[512,512]{1,0:T(8,128)(2,1)}, u32[]{:S(2)}, u32[]{:S(2)}) collective-permute-start(bf16[512,512]{1,0:T(8,128)(2,1)} %convolution_convert_fusion.27), channel_id=1, source_target_pairs={{0,16},{1,17},{2,18},{3,19},{4,20},{5,21},{6,22},{7,23},{8,24},{9,... | collective-permute-start | bytes 1572872 | tf_op jit(solution)/shard_map/ppermute | solution.py:341
  816.3 30.1 %collective-permute-start.91 = (bf16[512,1024]{0,1:T(8,128)(2,1)S(1)}, bf16[512,1024]{0,1:T(8,128)(2,1)}, u32[]{:S(2)}, u32[]{:S(2)}) collective-permute-start(bf16[512,1024]{0,1:T(8,128)(2,1)S(1)} %fusion.49), channel_id=1, source_target_pairs={{1,4},{3,6},{4,1},{6,3},{9,12},{11,14},{12,9},{14,11},{17,20},{19,... | collective-permute-start | bytes 3145736 | tf_op jit(solution)/shard_map/ppermute | solution.py:350
  (342 other events, 3798.4 us)
